TPU v7x, 256 devices: a whole 4x4x8 slice. The times are simulated.
256 devices in a mesh: chan: 32 (over z, y), win: 8 (over x, core).
Axes of the slice: x: 4, y: 4, z: 8, core: 2. Of those that a mesh axis runs over, the one named last changes fastest.
Arguments:
- records: bfloat16 [512, 64, 3072], P('chan', 'win'), may hold values from -6 to 6
- pair_source: int32 [32, 32], P('chan'), may hold values from 0 to 15, as said below
- pair_partner: int32 [32, 32], P('chan'), may hold values from 0 to 511, as said below
- pair_count: int32 [32], P('chan'), may hold values from 24 to 32, as said below
Outputs:
- correlations: float32 [1024, 1024], P(('chan', 'win'))
Inputs may be any that keep to these rules, and one draw needn't show every extreme that they name: `pair_source`: index of a pair's source channel within its block of 16 channels. For every block, at most 2 of its 32 pairs have partners in one block (pair_partner // 16), and exactly 2 in some block. Slots 0 to pair_count - 1 of a block are live; some block has all 32 live.
All inputs are finite; a program needn't handle non-finite values.
Results may differ from a plain program's by a relative error of at most 0.0047.
Values may be sent and summed in bfloat16 or wider, within the bound.
No kernel may reach another device: no remote copies, remote signals or barrier semaphores. Data moves between devices by JAX's collectives and lax.ppermute only.
A program may use at most 192 MiB of HBM per device.

v0:
```python
import math

import jax
import jax.numpy as jnp
from jax import lax
from jax.sharding import PartitionSpec as P

BAND = 128
LAGS = 1024


def forward_table(length, freqs):
    samples = jnp.arange(length, dtype=jnp.int32)
    bins = jnp.arange(1, freqs + 1, dtype=jnp.int32)
    phase = samples[:, None] * bins[None, :] % length
    angle = phase.astype(jnp.float32) * (2.0 * math.pi / length)
    return jnp.concatenate(
        [jnp.cos(angle).astype(jnp.bfloat16), (-jnp.sin(angle)).astype(jnp.bfloat16)], axis=1
    )


def inverse_table(length, freqs, lags, windows):
    bins = jnp.arange(1, freqs + 1, dtype=jnp.int32)
    shifts = jnp.arange(lags, dtype=jnp.int32) - lags // 2
    phase = bins[:, None] * shifts[None, :] % length
    angle = phase.astype(jnp.float32) * (2.0 * math.pi / length)
    factor = 1.0 / math.sqrt(freqs * windows)
    return jnp.concatenate([jnp.cos(angle) * factor, -jnp.sin(angle) * factor], axis=0)


def whiten(spectra, freqs, band):
    count = spectra.shape[0]
    real_part = spectra[:, :freqs].reshape(count, freqs // band, band)
    imag_part = spectra[:, freqs:].reshape(count, freqs // band, band)
    power = jnp.mean(real_part * real_part + imag_part * imag_part, axis=2)
    factor = lax.rsqrt(power + 1e-06)[:, :, None]
    real_part = (real_part * factor).reshape(count, freqs)
    imag_part = (imag_part * factor).reshape(count, freqs)
    return jnp.concatenate([real_part, imag_part], axis=1).astype(jnp.bfloat16)


def cross_spectrum(first, second, freqs):
    first = first.astype(jnp.float32)
    second = second.astype(jnp.float32)
    first_re, first_im = (first[..., :freqs], first[..., freqs:])
    second_re, second_im = (second[..., :freqs], second[..., freqs:])
    real_part = jnp.sum(first_re * second_re + first_im * second_im, axis=1)
    imag_part = jnp.sum(first_im * second_re - first_re * second_im, axis=1)
    return jnp.concatenate([real_part, imag_part], axis=1)


def shards(records, pair_source, pair_partner, pair_count):
    chans, wins, length = records.shape
    freqs = length // 2
    pairs = pair_source.shape[1]
    lag_count = LAGS
    win_count = lax.axis_size("win")
    table = forward_table(length, freqs)
    spectra = jnp.dot(
        records.reshape(chans * wins, length), table, preferred_element_type=jnp.float32
    )
    whitened = whiten(spectra, freqs, BAND).reshape(chans, wins, 2 * freqs)
    source = pair_source[0]
    partner = pair_partner[0]
    near_rows = jnp.take(whitened, source, axis=0)
    piece = lax.all_gather(whitened, "chan", axis=0, tiled=True)
    count = piece.shape[0]
    columns = jnp.arange(count, dtype=jnp.int32)
    onehot = (partner[:, None] == columns[None, :]).astype(jnp.bfloat16)
    picked = jnp.dot(
        onehot, piece.reshape(count, wins * 2 * freqs), preferred_element_type=jnp.float32
    )
    collected = picked.astype(jnp.bfloat16)
    far_rows = collected.reshape(pairs, wins, 2 * freqs)
    live = (jnp.arange(pairs, dtype=jnp.int32) < pair_count[0]).astype(jnp.float32)
    inverse = inverse_table(length, freqs, lag_count, wins * win_count)
    stacked = lax.psum_scatter(
        cross_spectrum(near_rows, far_rows, freqs) * live[:, None],
        "win",
        scatter_dimension=0,
        tiled=True,
    )
    return jnp.dot(
        stacked, inverse, precision=lax.Precision.HIGHEST, preferred_element_type=jnp.float32
    )


def solution(mesh):
    placed = (P("chan", "win", None), P("chan", None), P("chan", None), P("chan"))
    return jax.shard_map(
        shards, mesh=mesh, in_specs=placed, out_specs=P(("chan", "win"), None), check_vma=False
    )
```

profile of v0, /device:TPU:8, one launch (start us, length us, event | category | flops | bytes accessed | tf_op | source)
XLA Modules:
  0.0 404.5 jit_solution(515754130304400110)
XLA Ops:
  6.5 79.5 %cosine_convert_fusion = (bf16[3072,1536]{1,0:T(8,128)(2,1)S(1)}, bf16[3072,1536]{1,0:T(8,128)(2,1)}) fusion(s32[1536]{0:T(1024)S(1)} %iota_add_fusion), kind=kLoop, calls=%fused_computation.11 | loop fusion | flops 56623104 | bytes 18880512 | tf_op jit(solution)/shard_map/convert_element_type | solution.py:18
  86.1 8.8 %fusion.19 = f32[128,3072]{1,0:T(8,128)S(1)} fusion(bf16[3072,1536]{1,0:T(8,128)(2,1)} %get-tuple-element.12, bf16[3072,1536]{1,0:T(8,128)(2,1)S(1)} %get-tuple-element.11, bf16[16,8,3072]{2,1,0:T(8,128)(2,1)S(1)} %copy-done), kind=kOutput, calls=%fused_computation.29 | convolution fusion | flops 2453667840 | bytes 21233664 | tf_op jit(solution)/shard_map/dot_general | solution.py:59
  94.9 0.1 multiply_add_fusion
  95.0 0.3 copy.8
  95.3 0.1 reduce_sum.27
  95.4 0.1 mul.113
  95.4 0.3 copy.9
  95.7 0.1 fusion.23
  95.9 1.0 pad_maximum_fusion
  96.9 0.0 all-gather.2.cloned.1.call-update
  96.9 0.2 all-reduce.3.cloned.1.call-start
  97.2 1.8 gather_fusion
  99.6 1.9 select_convert_fusion
  101.5 180.9 %all-gather.2.cloned.1.call-done = bf16[512,8,3072]{2,1,0:T(8,128)(2,1)} async-done(((bf16[16,8,3072]{2,1,0:T(8,128)(2,1)}), bf16[512,8,3072]{2,1,0:T(8,128)(2,1)}) %all-gather.2.cloned.1.call-update) | async-done | bytes 25165840 | tf_op jit(solution)/shard_map/all_gather | solution.py:66
  282.4 27.0 %copy.11 = bf16[64,8,8,3072]{3,1,2,0:T(8,128)(2,1)} copy(bf16[64,8,8,3072]{3,2,1,0:T(8,128)(2,1)} %bitcast.27) | data formatting | bytes 50331648
  309.4 10.4 %fusion = f32[32,24576]{1,0:T(8,128)S(1)} fusion(bf16[512,24576]{1,0:T(8,128)(2,1)} %bitcast.26, s32[32]{0:T(128)S(1)} %bitcast.32), kind=kOutput, calls=%fused_computation.3 | convolution fusion | flops 806895616 | bytes 28311680 | tf_op jit(solution)/shard_map/dot_general | solution.py:70
  319.8 1.8 copy.12
  321.6 0.1 copy-done.2
  321.7 1.4 add_reduce_fusion
  323.1 0.9 maximum_multiply_fusion
  324.0 28.2 %cosine_multiply_fusion = (f32[1536,1024]{1,0:T(8,128)}, f32[1536,1024]{1,0:T(8,128)}) fusion(s32[1024]{0:T(1024)S(1)} %iota_add_fusion.1, s32[1536]{0:T(1024)S(1)} %iota_add_fusion), kind=kLoop, calls=%fused_computation.24 | loop fusion | flops 18874368 | bytes 12593152 | tf_op jit(solution)/shard_map/mul | solution.py:28
  352.2 0.6 dynamic-slice
  353.5 34.5 %all-reduce.3.cloned.1.call-done = f32[32,3072]{1,0:T(8,128)} async-done(((f32[32,3072]{1,0:T(8,128)}), f32[32,3072]{1,0:T(8,128)}) %all-reduce.3.cloned.1.call-update) | async-done | bytes 393232
  388.0 9.6 %fusion.10 = f32[4,1024]{1,0:T(4,128)} fusion(f32[1536,1024]{1,0:T(8,128)} %get-tuple-element.10, f32[1536,1024]{1,0:T(8,128)} %get-tuple-element.9, f32[32,3072]{1,0:T(8,128)} %all-reduce.3.cloned.1.call-done, u32[]{:T(128)S(6)} %multiply.6), kind=kOutput, calls=%fused_computation.16 | convolution fusion | flops 154140672 | bytes 12648452 | tf_op jit(solution)/shard_map/dot_general | solution.py:83
  (20 shorter events, 0.1 us)
Async XLA Ops:
  6.5 79.5 %copy-start = (bf16[16,8,3072]{2,1,0:T(8,128)(2,1)S(1)}, bf16[16,8,3072]{2,1,0:T(8,128)(2,1)}, u32[]{:S(2)}) copy-start(bf16[16,8,3072]{2,1,0:T(8,128)(2,1)} %param.4) | copy-start | bytes 2359300
  6.5 275.9 %all-gather.2.cloned.1.call-start = ((), (), s32[]{:S(2)}) async-start(), calls=%async_computation | async-start | bytes 25952256 | tf_op jit(solution)/shard_map/all_gather | solution.py:66
  94.9 2.2 copy-start.4
  96.9 291.1 %all-reduce.3.cloned.1.call-start = ((), (), s32[]{:S(2)}) async-start(), calls=%async_computation.1 | async-start | bytes 786432
  282.4 27.0 %copy-start.3 = (s32[1,32]{1,0:T(1,128)S(1)}, s32[1,32]{1,0:T(1,128)}, u32[]{:S(2)}) copy-start(s32[1,32]{1,0:T(1,128)} %param.6) | copy-start | bytes 388
  319.8 1.9 copy-start.2
  324.0 28.2 %copy-start.5 = (u32[256]{0:T(256)S(1)}, u32[256]{0:T(256)}, u32[]{:S(2)}) copy-start(u32[256]{0:T(256)} %constant.56) | copy-start | bytes 3076
  388.0 9.7 %copy-start.1 = (bf16[16,8,3072]{2,1,0:T(8,128)(2,1)S(1)}, bf16[16,8,3072]{2,1,0:T(8,128)(2,1)}, u32[]{:S(2)}) copy-start(bf16[16,8,3072]{2,1,0:T(8,128)(2,1)} %param.4) | copy-start | bytes 2359300
Sparse Core Ops, SparseCore 0:
  97.0 185.3 all-gather.1
  324.1 63.7 all-reduce.2
where the time goes:
time: 405 us; the launch traced here: 404 us
  waiting for transfers between devices  215 us (53%)
  other arithmetic  113 us (28%)
  local copies, waits for them, and re-layouts  31.8 us (8%)
  matrix products  28.9 us (7%)
  between operations  14.9 us (4%)
    all_gather x1, waiting for transfers between devices, shards(): piece = lax.all_gather(whitened, 'chan', axis=0, tiled=True)  181 us
    convert_element_type x1, other arithmetic, forward_table(): jnp.cos(angle).astype(jnp.bfloat16)  79.5 us
    unnamed x3, waiting for transfers between devices  34.5 us
    unnamed x15, local copies, waits for them, and re-layouts  29.4 us
    mul x1, other arithmetic, inverse_table(): jnp.cos(angle) * factor  28.2 us
    dot_general x1, matrix products, shards(): jnp.dot(onehot, piece.reshape(count, wins * 2 * freqs), preferred_element...  10.4 us
    dot_general x1, matrix products, shards(): jnp.dot(stacked, inverse, precision=lax.Precision.HIGHEST, preferred_elem...  9.65 us
    dot_general x1, matrix products, shards(): jnp.dot(records.reshape(chans * wins, length), table, preferred_element_t...  8.83 us
  transfers between devices with their start and end apart: 2, of which 2 were waited for; matrix products, arithmetic and copies ran while one was open for 8% of the time, Pallas kernels for 0%

commit v1 on v0

v1 whole, which is shorter than its diff:
```python
import math

import jax
import jax.numpy as jnp
from jax import lax
from jax.experimental import pallas as pl
from jax.experimental.pallas import tpu as pltpu
from jax.sharding import PartitionSpec as P

N = 3072
HALF = N // 2
BAND = 128
LAGS = 1024
QUARTER = N // 4
CHANS, WINS = 16, 8
ROWS = CHANS * WINS
BLOCKS = 32
PAIRS = 32
DATA = 6 * CHANS
PIECE = DATA + 8
VMEM = 56 * 1024 * 1024


def cos_sin(phase):
    turn = jnp.floor(phase * (1.0 / QUARTER) + 0.5)
    t = (phase - QUARTER * turn) * (2.0 * math.pi / N)
    quadrant = turn - 4.0 * jnp.floor(turn * 0.25)
    u = t * t
    s = t * (1.0 + u * (-1 / 6 + u * (1 / 120 + u * (-1 / 5040 + u * (1 / 362880)))))
    c = 1.0 + u * (-1 / 2 + u * (1 / 24 + u * (-1 / 720 + u * (1 / 40320))))
    odd = (quadrant == 1.0) | (quadrant == 3.0)
    cos = jnp.where(odd, s, c)
    sin = jnp.where(odd, c, s)
    cos = jnp.where((quadrant == 1.0) | (quadrant == 2.0), -cos, cos)
    sin = jnp.where(quadrant >= 2.0, -sin, sin)
    return cos, sin


def iota(shape, axis):
    return lax.broadcasted_iota(jnp.int32, shape, axis)


def transform_kernel(x_ref, source_ref, partner_ref, count_ref, out_ref,
                     even_ref, odd_ref, base_ref, step_ref, table_ref, spec_ref, power_ref, white_ref, list_ref):
    partner = partner_ref[...]
    slot = iota((1, PAIRS), 1)
    source = jnp.where(slot < count_ref[0], source_ref[...], -1)
    list_ref[...] = jnp.zeros((8, 128), jnp.float32)
    list_ref[0:1, 0:PAIRS] = (partner // CHANS).astype(jnp.float32)
    list_ref[1:2, 0:PAIRS] = (partner % CHANS).astype(jnp.float32)
    list_ref[2:3, 0:PAIRS] = source.astype(jnp.float32)
    lists = list_ref[...].astype(jnp.bfloat16)
    for c in range(BLOCKS):
        out_ref[c, DATA:PIECE, :] = lists

    lane = iota((ROWS, 128), 1)
    i = iota((256, 256), 0)
    k = iota((256, 256), 1)
    low = k < 128
    k = jnp.where(low, k, k - 128)
    ahead = jnp.where(low, 2 * ((k + 1) % 128), 2 * k + 1)
    back = jnp.where(low, 2 * (127 - k), 2 * (127 - k) + 1)
    ahead = jnp.where(i == ahead, 1.0, 0.0).astype(jnp.bfloat16)
    back = jnp.where(i == back, 1.0, 0.0).astype(jnp.bfloat16)
    rotated = []
    for t in range(6):
        part = jnp.dot(x_ref[:, 256 * t:256 * t + 256], ahead, preferred_element_type=jnp.float32)
        rotated.append(part[:, :128])
        odd_ref[0:ROWS, 128 * t:128 * t + 128] = part[:, 128:].astype(jnp.bfloat16)
        at = 256 * (11 - t)
        part = jnp.dot(x_ref[:, at:at + 256], back, preferred_element_type=jnp.float32)
        even_ref[ROWS:2 * ROWS, 128 * t:128 * t + 128] = part[:, :128].astype(jnp.bfloat16)
        odd_ref[ROWS:2 * ROWS, 128 * t:128 * t + 128] = part[:, 128:].astype(jnp.bfloat16)
    for t in range(6):
        following = rotated[t + 1] if t < 5 else 0.0
        even_ref[0:ROWS, 128 * t:128 * t + 128] = jnp.where(lane < 127, rotated[t], following).astype(jnp.bfloat16)
    first = jnp.sum(jnp.where(lane == 127, rotated[0], 0.0), axis=1, keepdims=True)

    last = jnp.zeros((ROWS, 128), jnp.float32)
    for t in range(24):
        last = last + x_ref[:, 128 * t:128 * t + 128].astype(jnp.float32)
    last = jnp.sum(jnp.where(lane % 2 == 0, last, -last), axis=1, keepdims=True)

    bins = (iota((16, QUARTER), 1) + 1).astype(jnp.float32)
    row = iota((16, QUARTER), 0).astype(jnp.float32)
    base_ref[0], base_ref[1] = cos_sin((2.0 * row + 2.0) * bins)
    base_ref[2], base_ref[3] = cos_sin((2.0 * row + 1.0) * bins)
    for a in range(3):
        cos, sin = cos_sin(32.0 * (row + 16.0 * a) * bins)
        step_ref[0, 16 * a:16 * a + 16, :] = cos
        step_ref[1, 16 * a:16 * a + 16, :] = sin

    @pl.loop(0, 48)
    def _(a):
        cos = step_ref[0, pl.ds(a, 1), :]
        sin = step_ref[1, pl.ds(a, 1), :]
        rows = pl.ds(pl.multiple_of(16 * a, 16), 16)
        for parity in range(2):
            base_cos, base_sin = base_ref[2 * parity], base_ref[2 * parity + 1]
            table_ref[2 * parity, rows, :] = (base_cos * cos - base_sin * sin).astype(jnp.bfloat16)
            table_ref[2 * parity + 1, rows, :] = (base_sin * cos + base_cos * sin).astype(jnp.bfloat16)

    for which in range(4):
        samples = even_ref if which < 2 else odd_ref
        spec_ref[which] = jnp.dot(samples[...], table_ref[which], preferred_element_type=jnp.float32)

    top, bottom = slice(0, ROWS), slice(ROWS, 2 * ROWS)
    for t in range(6):
        at = slice(128 * t, 128 * t + 128)
        even_cos = spec_ref[0, top, at] + spec_ref[0, bottom, at] + first
        even_sin = spec_ref[1, top, at] - spec_ref[1, bottom, at]
        odd_cos = spec_ref[2, top, at] + spec_ref[2, bottom, at]
        odd_sin = spec_ref[3, top, at] - spec_ref[3, bottom, at]
        real, imag = even_cos + odd_cos, -(even_sin + odd_sin)
        real_back, imag_back = even_cos - odd_cos, even_sin - odd_sin
        if t == 5:
            real_back = jnp.where(lane < 127, real_back, last)
            imag_back = jnp.where(lane < 127, imag_back, 0.0)
        white_ref[0, t], white_ref[1, t] = real, imag
        white_ref[0, 6 + t], white_ref[1, 6 + t] = real_back, imag_back
        power_ref[t] = real * real + imag * imag
        power_ref[6 + t] = real_back * real_back + imag_back * imag_back
    factor = []
    for t in range(12):
        power = power_ref[t]
        if t >= 6:
            power = jnp.where(lane < 127, power, power_ref[6 + (t - 7) % 6])
        mean = jnp.sum(power, axis=1, keepdims=True) * (1.0 / BAND)
        factor.append(lax.rsqrt(mean + 1e-06))

    segment = iota((CHANS, 128), 1) // 16
    for t in range(12):
        scale = factor[t]
        if t >= 6:
            scale = jnp.where(lane < 127, scale, factor[6 + (t - 5) % 6])
        for part in range(2):
            white_ref[part, t] = white_ref[part, t] * scale
            slabs = [white_ref[part, t, pl.ds(w, CHANS, stride=WINS), :] for w in range(WINS)]
            for bit in range(3):
                step = 1 << bit
                high = (segment // step) % 2 == 1
                mixed = [None] * WINS
                for w in range(WINS):
                    if w & step:
                        continue
                    one, two = slabs[w], slabs[w + step]
                    mixed[w] = jnp.where(high, pltpu.roll(two, 16 * step, 1), one)
                    mixed[w + step] = jnp.where(high, two, pltpu.roll(one, 128 - 16 * step, 1))
                slabs = mixed
            at = CHANS * (2 * (t % 3) + part)
            for s in range(8):
                out_ref[8 * (t // 3) + s, at:at + CHANS, :] = slabs[s].astype(jnp.bfloat16)


def transform(x, source, partner, count):
    vmem = pl.BlockSpec(memory_space=pltpu.VMEM)
    return pl.pallas_call(
        transform_kernel,
        out_shape=jax.ShapeDtypeStruct((BLOCKS, PIECE, 128), jnp.bfloat16),
        in_specs=[vmem, vmem, vmem, pl.BlockSpec(memory_space=pltpu.SMEM)],
        out_specs=vmem,
        scratch_shapes=[
            pltpu.VMEM((2 * ROWS, QUARTER), jnp.bfloat16),
            pltpu.VMEM((2 * ROWS, QUARTER), jnp.bfloat16),
            pltpu.VMEM((4, 16, QUARTER), jnp.float32),
            pltpu.VMEM((2, 48, QUARTER), jnp.float32),
            pltpu.VMEM((4, QUARTER, QUARTER), jnp.bfloat16),
            pltpu.VMEM((4, 2 * ROWS, QUARTER), jnp.float32),
            pltpu.VMEM((12, ROWS, 128), jnp.float32),
            pltpu.VMEM((2, 12, ROWS, 128), jnp.float32),
            pltpu.VMEM((8, 128), jnp.float32),
        ],
        compiler_params=pltpu.CompilerParams(vmem_limit_bytes=VMEM),
        cost_estimate=pl.CostEstimate(flops=2 * 4 * 2 * ROWS * QUARTER**2, bytes_accessed=2 * 10**6, transcendentals=0),
        name="transform",
    )(x, source, partner, count)


def cross_kernel(got_ref, out_ref, data_ref, near_ref, far_ref, list_ref):
    for q in range(6):
        data_ref[:, 128 * q:128 * q + 128] = got_ref[:, CHANS * q:CHANS * (q + 1), :].reshape(BLOCKS * CHANS, 128)
    lists = got_ref[:, DATA:PIECE, :].astype(jnp.float32)
    block = iota((BLOCKS, 128), 0)
    list_ref[...] = jnp.zeros((2, 128, 128), jnp.float32)
    list_ref[0, 0:BLOCKS, :] = lists[:, 0, :] * CHANS + lists[:, 1, :]
    inside = (block % 16 * CHANS).astype(jnp.float32)
    list_ref[1, 0:BLOCKS, :] = jnp.where(lists[:, 2, :] < 0.0, -1.0, lists[:, 2, :] + inside)
    partner = jnp.transpose(list_ref[0])
    source = jnp.transpose(list_ref[1])
    channel = iota((PAIRS, BLOCKS * CHANS), 1).astype(jnp.float32)
    for o in range(BLOCKS):
        rows = slice(PAIRS * o, PAIRS * (o + 1))
        far_ref[rows, :] = jnp.where(channel == partner[0:PAIRS, o:o + 1], 1.0, 0.0).astype(jnp.bfloat16)
        near = channel[:, :256] == source[0:PAIRS, o:o + 1]
        near_ref[rows, :] = jnp.where(near, 1.0, 0.0).astype(jnp.bfloat16)

    size = 256
    lane = iota((size, 128), 1)
    for m in range(BLOCKS * PAIRS // size):
        rows = slice(size * m, size * (m + 1))
        half = slice(256 * (2 * m // 4), 256 * (2 * m // 4) + 256)
        far = jnp.dot(far_ref[rows, :], data_ref[...], preferred_element_type=jnp.float32)
        near = jnp.dot(near_ref[rows, :], data_ref[half, :], preferred_element_type=jnp.float32)
        tiles = []
        for t in range(3):
            re, im = slice(256 * t, 256 * t + 128), slice(256 * t + 128, 256 * t + 256)
            a_re, a_im, b_re, b_im = near[:, re], near[:, im], far[:, re], far[:, im]
            real = a_re * b_re + a_im * b_im
            imag = a_im * b_re - a_re * b_im
            low = lane < 64
            tiles.append(jnp.where(low, real, imag) + pltpu.roll(jnp.where(low, imag, real), 64, 1))
        low = lane // 32 % 2 == 0
        one = jnp.where(low, tiles[0] + pltpu.roll(tiles[0], 96, 1), tiles[1] + pltpu.roll(tiles[1], 32, 1))
        two = jnp.where(low, tiles[2] + pltpu.roll(tiles[2], 96, 1), 0.0)
        low = lane // 16 % 2 == 0
        out_ref[rows, :] = jnp.where(low, one + pltpu.roll(one, 112, 1), two + pltpu.roll(two, 16, 1))


def cross(got):
    vmem = pl.BlockSpec(memory_space=pltpu.VMEM)
    pairs = BLOCKS * PAIRS
    return pl.pallas_call(
        cross_kernel,
        out_shape=jax.ShapeDtypeStruct((pairs, 128), jnp.float32),
        in_specs=[vmem],
        out_specs=vmem,
        scratch_shapes=[
            pltpu.VMEM((BLOCKS * CHANS, 6 * 128), jnp.bfloat16),
            pltpu.VMEM((pairs, 256), jnp.bfloat16),
            pltpu.VMEM((pairs, BLOCKS * CHANS), jnp.bfloat16),
            pltpu.VMEM((2, 128, 128), jnp.float32),
        ],
        compiler_params=pltpu.CompilerParams(vmem_limit_bytes=VMEM),
        cost_estimate=pl.CostEstimate(flops=2 * pairs * 768 * 768, bytes_accessed=2 * 10**6, transcendentals=0),
        name="cross",
    )(got)


def bin_of(block, lane):
    tile = 3 * (block // 8) + jnp.where(lane // 32 % 2 == 1, 1, jnp.where(lane // 16 % 2 == 1, 2, 0))
    place = 128 * tile + 16 * (block % 8) + lane % 16 + 1
    back = place - 768
    back = jnp.where(back == 768, 0, back)
    return jnp.where(tile < 6, place, HALF - back), lane // 16 % 4 != 3


def inverse_kernel(turn_ref, table_ref):
    scale = 1.0 / math.sqrt(HALF * 64)

    @pl.loop(0, BLOCKS)
    def _(c):
        lane = iota((32, 128), 1)
        a = iota((32, 128), 0) // 4 - 4
        j, used = bin_of(c, lane)
        cos, sin = cos_sin((128 * (a + 24) * j).astype(jnp.float32))
        factor = jnp.where(used, scale, 0.0)
        rows = pl.ds(pl.multiple_of(32 * c, 32), 32)
        turn_ref[0, rows, :] = cos * factor
        turn_ref[1, rows, :] = jnp.where(lane < 64, -sin, sin) * factor
        lane = iota((128, 128), 0)
        b = iota((128, 128), 1)
        j, _ = bin_of(c, lane)
        table, _ = cos_sin((j * b + jnp.where(lane < 64, 0, QUARTER)).astype(jnp.float32))
        coarse = table.astype(jnp.bfloat16)
        rows = pl.ds(pl.multiple_of(128 * c, 128), 128)
        table_ref[rows, 0:128] = coarse
        table_ref[rows, 128:256] = (table - coarse.astype(jnp.float32)).astype(jnp.bfloat16)


def inverse():
    vmem = pl.BlockSpec(memory_space=pltpu.VMEM)
    return pl.pallas_call(
        inverse_kernel,
        out_shape=(
            jax.ShapeDtypeStruct((2, 32 * BLOCKS, 128), jnp.float32),
            jax.ShapeDtypeStruct((128 * BLOCKS, 256), jnp.bfloat16),
        ),
        out_specs=(vmem, vmem),
        compiler_params=pltpu.CompilerParams(vmem_limit_bytes=VMEM),
        cost_estimate=pl.CostEstimate(flops=40 * 10**6, bytes_accessed=3 * 10**6, transcendentals=0),
        name="inverse",
    )()


def lags_kernel(got_ref, turn_ref, table_ref, out_ref, left_ref):
    for c in range(BLOCKS):
        rows = got_ref[32 * c:32 * c + 32, :]
        total = rows[0:8] + rows[8:16] + rows[16:24] + rows[24:32]
        total = total + pltpu.roll(total, 4, 0)
        total = jnp.concatenate([total] * 4, axis=0)
        at = slice(32 * c, 32 * c + 32)
        turned = total * turn_ref[0, at, :] + pltpu.roll(total, 64, 1) * turn_ref[1, at, :]
        coarse = turned.astype(jnp.bfloat16)
        left_ref[0:32, 128 * c:128 * c + 128] = coarse
        left_ref[32:64, 128 * c:128 * c + 128] = (turned - coarse.astype(jnp.float32)).astype(jnp.bfloat16)
    both = jnp.dot(left_ref[...], table_ref[...], preferred_element_type=jnp.float32)
    both = both[:32] + both[32:]
    both = both[:, :128] + both[:, 128:]
    for a in range(8):
        out_ref[:, 128 * a:128 * a + 128] = both[4 * a:4 * a + 4, :]


def lags(got, turn, table):
    vmem = pl.BlockSpec(memory_space=pltpu.VMEM)
    return pl.pallas_call(
        lags_kernel,
        out_shape=jax.ShapeDtypeStruct((4, LAGS), jnp.float32),
        in_specs=[vmem] * 3,
        out_specs=vmem,
        scratch_shapes=[pltpu.VMEM((64, 128 * BLOCKS), jnp.bfloat16)],
        compiler_params=pltpu.CompilerParams(vmem_limit_bytes=VMEM),
        cost_estimate=pl.CostEstimate(flops=2 * 64 * 4096 * 256, bytes_accessed=4 * 10**6, transcendentals=0),
        name="lags",
    )(got, turn, table)


def shards(records, pair_source, pair_partner, pair_count):
    sent = transform(records.reshape(ROWS, N), pair_source, pair_partner, pair_count)
    got = lax.all_to_all(sent, "chan", 0, 0)
    turn, table = inverse()
    spectra = cross(got).reshape(BLOCKS * WINS, 4, 128)
    parts = lax.all_to_all(spectra, ("chan", "win"), 0, 0)
    return lags(parts.reshape(BLOCKS * PAIRS, 128), turn, table)


def solution(mesh):
    placed = (P("chan", "win", None), P("chan", None), P("chan", None), P("chan"))
    return jax.shard_map(
        shards, mesh=mesh, in_specs=placed, out_specs=P(("chan", "win"), None), check_vma=False
    )
```

time: 405 us -> 80.8 us (0.20)
  waiting for transfers between devices: 215 us -> 13.5 us
  other arithmetic: 113 us -> 0 us
  blocking collectives: 0 us -> 35.7 us
  local copies, waits for them, and re-layouts: 31.8 us -> 0.79 us
  matrix products: 28.9 us -> 0 us
  Pallas kernels: 0 us -> 20.6 us
  between operations: 14.9 us -> 0.66 us
  starting transfers between devices: 0.22 us -> 8.48 us
    all_gather x1 -> x0, waiting for transfers between devices: 181 us -> none  [shards(): piece = lax.all_gather(whitened, 'chan', axis=0, tiled=True)]
    convert_element_type x3 -> x0, other arithmetic: 81.4 us -> none  [the longest x1 79.5 us: forward_table(): jnp.cos(angle).astype(jnp.bfloat16)]
    all_to_all x0 -> x1, blocking collectives: none -> 35.7 us  [shards(): got = lax.all_to_all(sent, 'chan', 0, 0)]
    unnamed x3 -> x0, waiting for transfers between devices: 34.5 us -> none
    mul x2 -> x0, other arithmetic: 29.1 us -> none  [the longest x1 28.2 us: inverse_table(): jnp.cos(angle) * factor]
    dot_general x3 -> x0, matrix products: 28.9 us -> none  [the longest x1 10.4 us: shards(): jnp.dot(onehot, piece.reshape(count, wins * 2 * freqs), preferred_element...]
    unnamed x15 -> x2, local copies, waits for them, and re-layouts: 29.4 us -> 0.79 us
    pallas_call x0 -> x4, Pallas kernels: none -> 20.6 us  [the longest x1 6.82 us: transform(): pl.pallas_call(transform_kernel, out_shape=jax.ShapeDtypeStruct((BLOCKS,...]
  transfers between devices with their start and end apart: 2 -> 1, of which waited for: 2 -> 1; matrix products, arithmetic and copies ran while one was open for 8% -> 0% of each run, Pallas kernels for 0% -> 8%
where the time goes in v1:
time: 80.8 us; the launch traced here: 79.6 us
  blocking collectives  35.7 us (44%)
  Pallas kernels  20.6 us (25%)
  waiting for transfers between devices  13.5 us (17%)
  starting transfers between devices  8.48 us (10%)
    all_to_all x1, blocking collectives, shards(): got = lax.all_to_all(sent, 'chan', 0, 0)  35.7 us
    all_to_all x1, waiting for transfers between devices, shards(): parts = lax.all_to_all(spectra, ('chan', 'win'), 0, 0)  13.5 us
    all_to_all x1, starting transfers between devices, shards(): parts = lax.all_to_all(spectra, ('chan', 'win'), 0, 0)  8.48 us
    pallas_call x1, Pallas kernels, transform(): pl.pallas_call(transform_kernel, out_shape=jax.ShapeDtypeStruct((BLOCKS,...  6.82 us
    pallas_call x1, Pallas kernels, inverse(): pl.pallas_call(inverse_kernel, out_shape=(jax.ShapeDtypeStruct((2, 32 * B...  6.64 us
    pallas_call x1, Pallas kernels, cross(): pl.pallas_call(cross_kernel, out_shape=jax.ShapeDtypeStruct((pairs, 128),...  3.87 us
    pallas_call x1, Pallas kernels, lags(): pl.pallas_call(lags_kernel, out_shape=jax.ShapeDtypeStruct((4, LAGS), jnp...  3.25 us
  transfers between devices with their start and end apart: 1, of which 1 were waited for; matrix products, arithmetic and copies ran while one was open for 0% of the time, Pallas kernels for 8%

profile of v1, /device:TPU:8, one launch (start us, length us, event | category | flops | bytes accessed | tf_op | source)
XLA Modules:
  0.0 79.6 jit_solution(2180863889291835792)
XLA Ops:
  0.7 6.8 %transform.1 = bf16[32,104,128]{2,1,0:T(8,128)(2,1)} custom-call(bf16[128,3072]{1,0:T(8,128)(2,1)} %bitcast.5, s32[1,32]{1,0:T(1,128)} %source_ref.1, s32[1,32]{1,0:T(1,128)} %partner_ref.1, s32[1]{0:T(128)S(6)} %copy.5.count_ref), custom_call_target="tpu_custom_call" | custom-call | flops 1207959552 | bytes 2000000 | tf_op jit(solution)/shard_map/transform/pallas_call | solution.py:157
  7.5 35.7 %all_to_all.10.got_ref = bf16[32,104,128]{2,1,0:T(8,128)(2,1)} all-to-all(bf16[32,104,128]{2,1,0:T(8,128)(2,1)} %transform.1), channel_id=1, replica_groups=mesh['chan'=32,'win'=8] {'chan'}, dimensions={0} | all-to-all | bytes 1703936 | tf_op jit(solution)/shard_map/all_to_all | solution.py:319
  43.1 3.9 %cross.1 = f32[1024,128]{1,0:T(8,128)} custom-call(bf16[32,104,128]{2,1,0:T(8,128)(2,1)} %all_to_all.10.got_ref), custom_call_target="tpu_custom_call" | custom-call | flops 1207959552 | bytes 2000000 | tf_op jit(solution)/shard_map/cross/pallas_call | solution.py:222
  47.0 8.5 %all-to-all-start.1 = ((f32[256,4,128]{2,1,0:T(4,128)}), f32[256,4,128]{2,1,0:T(4,128)S(1)}, u32[]{:S(2)}, u32[]{:S(2)}) async-start(f32[256,4,128]{2,1,0:T(4,128)} %bitcast.4), calls=%async_computation.1 | async-start | bytes 1048576 | tf_op jit(solution)/shard_map/all_to_all | solution.py:322
  55.5 6.6 %inverse.1 = (f32[2,1024,128]{2,1,0:T(8,128)}, bf16[4096,256]{1,0:T(8,128)(2,1)}) custom-call(), custom_call_target="tpu_custom_call" | custom-call | flops 40000000 | bytes 3000000 | tf_op jit(solution)/shard_map/inverse/pallas_call | solution.py:272
  62.1 13.5 %all-to-all-done.1 = f32[256,4,128]{2,1,0:T(4,128)S(1)} async-done(((f32[256,4,128]{2,1,0:T(4,128)}), f32[256,4,128]{2,1,0:T(4,128)S(1)}, u32[]{:S(2)}, u32[]{:S(2)}) %all-to-all-start.1) | async-done | bytes 524320 | tf_op jit(solution)/shard_map/all_to_all | solution.py:322
  75.6 0.0 copy-start
  75.6 0.8 copy-done
  76.4 3.2 %lags.1 = f32[4,1024]{1,0:T(4,128)} custom-call(f32[1024,128]{1,0:T(8,128)} %bitcast.3, f32[2,1024,128]{2,1,0:T(8,128)} %get-tuple-element.7.turn_ref, bf16[4096,256]{1,0:T(8,128)(2,1)} %get-tuple-element.8.table_ref), custom_call_target="tpu_custom_call" | custom-call | flops 134217728 | bytes 4000000 | tf_op jit(solution)/shard_map/lags/pallas_call | solution.py:305
Async XLA Ops:
  47.0 28.6 %all-to-all-start.1 = ((f32[256,4,128]{2,1,0:T(4,128)}), f32[256,4,128]{2,1,0:T(4,128)S(1)}, u32[]{:S(2)}, u32[]{:S(2)}) async-start(f32[256,4,128]{2,1,0:T(4,128)} %bitcast.4), calls=%async_computation.1 | async-start | bytes 1048576 | tf_op jit(solution)/shard_map/all_to_all | solution.py:322
  75.6 0.8 copy-start

commit v2 on v1

--- a/solution.py
+++ b/solution.py
@@ -1,3 +1,4 @@
+import functools
 import math
 
 import jax
@@ -5,6 +6,7 @@
 from jax import lax
 from jax.experimental import pallas as pl
 from jax.experimental.pallas import tpu as pltpu
+from jax.sharding import Mesh
 from jax.sharding import PartitionSpec as P
 
 N = 3072
@@ -16,9 +18,10 @@
 ROWS = CHANS * WINS
 BLOCKS = 32
 PAIRS = 32
+HALF_PAIRS = PAIRS // 2
 DATA = 6 * CHANS
 PIECE = DATA + 8
-VMEM = 56 * 1024 * 1024
+MB = 1024 * 1024
 
 
 def cos_sin(phase):
@@ -49,7 +52,14 @@
     list_ref[0:1, 0:PAIRS] = (partner // CHANS).astype(jnp.float32)
     list_ref[1:2, 0:PAIRS] = (partner % CHANS).astype(jnp.float32)
     list_ref[2:3, 0:PAIRS] = source.astype(jnp.float32)
-    lists = list_ref[...].astype(jnp.bfloat16)
+    plain = list_ref[...]
+    lane = iota((8, 128), 1)
+    lists = jnp.zeros((8, 128), jnp.float32)
+    for quad in range(8):
+        at, to = 4 * quad, 16 * (quad % 2) + 4 * (quad // 2)
+        moved = pltpu.roll(plain, (to - at) % 128, 1)
+        lists = jnp.where((lane >= to) & (lane < to + 4), moved, lists)
+    lists = lists.astype(jnp.bfloat16)
     for c in range(BLOCKS):
         out_ref[c, DATA:PIECE, :] = lists
 
@@ -170,13 +180,13 @@
             pltpu.VMEM((2, 12, ROWS, 128), jnp.float32),
             pltpu.VMEM((8, 128), jnp.float32),
         ],
-        compiler_params=pltpu.CompilerParams(vmem_limit_bytes=VMEM),
+        compiler_params=pltpu.CompilerParams(vmem_limit_bytes=32 * MB),
         cost_estimate=pl.CostEstimate(flops=2 * 4 * 2 * ROWS * QUARTER**2, bytes_accessed=2 * 10**6, transcendentals=0),
         name="transform",
     )(x, source, partner, count)
 
 
-def cross_kernel(got_ref, out_ref, data_ref, near_ref, far_ref, list_ref):
+def cross_kernel(away, got_ref, after_ref, out_ref, data_ref, near_ref, far_ref, list_ref):
     for q in range(6):
         data_ref[:, 128 * q:128 * q + 128] = got_ref[:, CHANS * q:CHANS * (q + 1), :].reshape(BLOCKS * CHANS, 128)
     lists = got_ref[:, DATA:PIECE, :].astype(jnp.float32)
@@ -187,20 +197,23 @@
     list_ref[1, 0:BLOCKS, :] = jnp.where(lists[:, 2, :] < 0.0, -1.0, lists[:, 2, :] + inside)
     partner = jnp.transpose(list_ref[0])
     source = jnp.transpose(list_ref[1])
-    channel = iota((PAIRS, BLOCKS * CHANS), 1).astype(jnp.float32)
+    list_ref[0], list_ref[1] = partner, source
+    core = (lax.axis_index("core") + away) % 2
+    pick = pl.ds(pl.multiple_of(HALF_PAIRS * core, HALF_PAIRS), HALF_PAIRS)
+    partner, source = list_ref[0, pick, :], list_ref[1, pick, :]
+    channel = iota((HALF_PAIRS, BLOCKS * CHANS), 1).astype(jnp.float32)
     for o in range(BLOCKS):
-        rows = slice(PAIRS * o, PAIRS * (o + 1))
-        far_ref[rows, :] = jnp.where(channel == partner[0:PAIRS, o:o + 1], 1.0, 0.0).astype(jnp.bfloat16)
-        near = channel[:, :256] == source[0:PAIRS, o:o + 1]
+        rows = slice(HALF_PAIRS * o, HALF_PAIRS * (o + 1))
+        far_ref[rows, :] = jnp.where(channel == partner[:, o:o + 1], 1.0, 0.0).astype(jnp.bfloat16)
+        near = channel[:, :256] == source[:, o:o + 1]
         near_ref[rows, :] = jnp.where(near, 1.0, 0.0).astype(jnp.bfloat16)
 
     size = 256
     lane = iota((size, 128), 1)
-    for m in range(BLOCKS * PAIRS // size):
+    for m in range(2):
         rows = slice(size * m, size * (m + 1))
-        half = slice(256 * (2 * m // 4), 256 * (2 * m // 4) + 256)
         far = jnp.dot(far_ref[rows, :], data_ref[...], preferred_element_type=jnp.float32)
-        near = jnp.dot(near_ref[rows, :], data_ref[half, :], preferred_element_type=jnp.float32)
+        near = jnp.dot(near_ref[rows, :], data_ref[rows, :], preferred_element_type=jnp.float32)
         tiles = []
         for t in range(3):
             re, im = slice(256 * t, 256 * t + 128), slice(256 * t + 128, 256 * t + 256)
@@ -216,13 +229,13 @@
         out_ref[rows, :] = jnp.where(low, one + pltpu.roll(one, 112, 1), two + pltpu.roll(two, 16, 1))
 
 
-def cross(got):
+def cross(got, after, away):
     vmem = pl.BlockSpec(memory_space=pltpu.VMEM)
-    pairs = BLOCKS * PAIRS
+    pairs = BLOCKS * HALF_PAIRS
     return pl.pallas_call(
-        cross_kernel,
+        functools.partial(cross_kernel, away),
         out_shape=jax.ShapeDtypeStruct((pairs, 128), jnp.float32),
-        in_specs=[vmem],
+        in_specs=[vmem, pl.BlockSpec(memory_space=pl.ANY)],
         out_specs=vmem,
         scratch_shapes=[
             pltpu.VMEM((BLOCKS * CHANS, 6 * 128), jnp.bfloat16),
@@ -230,10 +243,10 @@
             pltpu.VMEM((pairs, BLOCKS * CHANS), jnp.bfloat16),
             pltpu.VMEM((2, 128, 128), jnp.float32),
         ],
-        compiler_params=pltpu.CompilerParams(vmem_limit_bytes=VMEM),
+        compiler_params=pltpu.CompilerParams(vmem_limit_bytes=16 * MB),
         cost_estimate=pl.CostEstimate(flops=2 * pairs * 768 * 768, bytes_accessed=2 * 10**6, transcendentals=0),
         name="cross",
-    )(got)
+    )(got, after)
 
 
 def bin_of(block, lane):
@@ -244,7 +257,7 @@
     return jnp.where(tile < 6, place, HALF - back), lane // 16 % 4 != 3
 
 
-def inverse_kernel(turn_ref, table_ref):
+def inverse_kernel(after_ref, turn_ref, table_ref):
     scale = 1.0 / math.sqrt(HALF * 64)
 
     @pl.loop(0, BLOCKS)
@@ -267,7 +280,7 @@
         table_ref[rows, 128:256] = (table - coarse.astype(jnp.float32)).astype(jnp.bfloat16)
 
 
-def inverse():
+def inverse(after):
     vmem = pl.BlockSpec(memory_space=pltpu.VMEM)
     return pl.pallas_call(
         inverse_kernel,
@@ -275,17 +288,17 @@
             jax.ShapeDtypeStruct((2, 32 * BLOCKS, 128), jnp.float32),
             jax.ShapeDtypeStruct((128 * BLOCKS, 256), jnp.bfloat16),
         ),
+        in_specs=[pl.BlockSpec(memory_space=pl.ANY)],
         out_specs=(vmem, vmem),
-        compiler_params=pltpu.CompilerParams(vmem_limit_bytes=VMEM),
+        compiler_params=pltpu.CompilerParams(vmem_limit_bytes=12 * MB),
         cost_estimate=pl.CostEstimate(flops=40 * 10**6, bytes_accessed=3 * 10**6, transcendentals=0),
         name="inverse",
-    )()
+    )(after)
 
 
 def lags_kernel(got_ref, turn_ref, table_ref, out_ref, left_ref):
     for c in range(BLOCKS):
-        rows = got_ref[32 * c:32 * c + 32, :]
-        total = rows[0:8] + rows[8:16] + rows[16:24] + rows[24:32]
+        total = got_ref[16 * c:16 * c + 8, :] + got_ref[16 * c + 8:16 * c + 16, :]
         total = total + pltpu.roll(total, 4, 0)
         total = jnp.concatenate([total] * 4, axis=0)
         at = slice(32 * c, 32 * c + 32)
@@ -308,7 +321,7 @@
         in_specs=[vmem] * 3,
         out_specs=vmem,
         scratch_shapes=[pltpu.VMEM((64, 128 * BLOCKS), jnp.bfloat16)],
-        compiler_params=pltpu.CompilerParams(vmem_limit_bytes=VMEM),
+        compiler_params=pltpu.CompilerParams(vmem_limit_bytes=16 * MB),
         cost_estimate=pl.CostEstimate(flops=2 * 64 * 4096 * 256, bytes_accessed=4 * 10**6, transcendentals=0),
         name="lags",
     )(got, turn, table)
@@ -317,14 +330,17 @@
 def shards(records, pair_source, pair_partner, pair_count):
     sent = transform(records.reshape(ROWS, N), pair_source, pair_partner, pair_count)
     got = lax.all_to_all(sent, "chan", 0, 0)
-    turn, table = inverse()
-    spectra = cross(got).reshape(BLOCKS * WINS, 4, 128)
-    parts = lax.all_to_all(spectra, ("chan", "win"), 0, 0)
-    return lags(parts.reshape(BLOCKS * PAIRS, 128), turn, table)
+    turn, table = inverse(sent)
+    away = cross(got, turn, 1)
+    near = lax.ppermute(away, "core", [(0, 1), (1, 0)])
+    spectra = cross(got, turn, 0) + near
+    parts = lax.all_to_all(spectra.reshape(BLOCKS * 4, 4, 128), ("chan", "x"), 0, 0)
+    return lags(parts.reshape(BLOCKS * HALF_PAIRS, 128), turn, table)
 
 
 def solution(mesh):
-    placed = (P("chan", "win", None), P("chan", None), P("chan", None), P("chan"))
+    chips = Mesh(mesh.devices.reshape(BLOCKS, WINS // 2, 2), ("chan", "x", "core"))
+    placed = (P("chan", ("x", "core"), None), P("chan", None), P("chan", None), P("chan"))
     return jax.shard_map(
-        shards, mesh=mesh, in_specs=placed, out_specs=P(("chan", "win"), None), check_vma=False
+        shards, mesh=chips, in_specs=placed, out_specs=P(("chan", "x", "core"), None), check_vma=False
     )

time: 80.8 us -> 75.9 us (0.939)
  blocking collectives: 35.7 us -> 24.3 us
  waiting for transfers between devices: 13.5 us -> 18.8 us
  Pallas kernels: 20.6 us -> 16.9 us
  starting transfers between devices: 8.48 us -> 11.8 us
  local copies, waits for them, and re-layouts: 0.79 us -> 2.44 us
    all_to_all x1, blocking collectives: 35.7 us -> 24.3 us  [shards(): lax.all_to_all(spectra.reshape(BLOCKS * 4, 4, 128), ('chan', 'x'), 0, 0)]
    all_to_all x1, waiting for transfers between devices: 13.5 us -> 18.8 us  [shards(): got = lax.all_to_all(sent, 'chan', 0, 0)]
    all_to_all x1, starting transfers between devices: 8.48 us -> 11.7 us  [shards(): got = lax.all_to_all(sent, 'chan', 0, 0)]
    pallas_call x1, Pallas kernels: 3.25 us -> 1.16 us  [lags(): pl.pallas_call(lags_kernel, out_shape=jax.ShapeDtypeStruct((4, LAGS), jnp...]
    unnamed x2 -> x6, local copies, waits for them, and re-layouts: 0.79 us -> 2.44 us
    pallas_call x1, Pallas kernels: 6.64 us -> 5.11 us  [inverse(): pl.pallas_call(inverse_kernel, out_shape=(jax.ShapeDtypeStruct((2, 32 * B...]
    pallas_call x1, Pallas kernels: 6.82 us -> 5.7 us  [transform(): pl.pallas_call(transform_kernel, out_shape=jax.ShapeDtypeStruct((BLOCKS,...]
    pallas_call x1 -> x2, Pallas kernels: 3.87 us -> 4.95 us  [cross(): pl.pallas_call(functools.partial(cross_kernel, away), out_shape=jax.Shape...]
  transfers between devices with their start and end apart: 1 -> 2, of which waited for: 1 -> 1; matrix products, arithmetic and copies ran while one was open for 0% -> 0% of each run, Pallas kernels for 8% -> 10%
where the time goes in v2:
time: 75.9 us; the launch traced here: 75 us
  blocking collectives  24.3 us (32%)
  waiting for transfers between devices  18.8 us (25%)
  Pallas kernels  16.9 us (22%)
  starting transfers between devices  11.8 us (16%)
  local copies, waits for them, and re-layouts  2.44 us (3%)
    all_to_all x1, blocking collectives, shards(): lax.all_to_all(spectra.reshape(BLOCKS * 4, 4, 128), ('chan', 'x'), 0, 0)  24.3 us
    all_to_all x1, waiting for transfers between devices, shards(): got = lax.all_to_all(sent, 'chan', 0, 0)  18.8 us
    all_to_all x1, starting transfers between devices, shards(): got = lax.all_to_all(sent, 'chan', 0, 0)  11.7 us
    pallas_call x1, Pallas kernels, transform(): pl.pallas_call(transform_kernel, out_shape=jax.ShapeDtypeStruct((BLOCKS,...  5.7 us
    pallas_call x1, Pallas kernels, inverse(): pl.pallas_call(inverse_kernel, out_shape=(jax.ShapeDtypeStruct((2, 32 * B...  5.11 us
    pallas_call x2, Pallas kernels, cross(): pl.pallas_call(functools.partial(cross_kernel, away), out_shape=jax.Shape...  4.95 us
    unnamed x6, local copies, waits for them, and re-layouts  2.44 us
  transfers between devices with their start and end apart: 2, of which 1 were waited for; matrix products, arithmetic and copies ran while one was open for 0% of the time, Pallas kernels for 10%

profile of v2, /device:TPU:8, one launch (start us, length us, event | category | flops | bytes accessed | tf_op | source)
XLA Modules:
  0.0 75.0 jit_solution(910833572915784610)
XLA Ops:
  0.7 0.0 copy-start
  0.7 1.1 %copy-done = bf16[16,8,3072]{2,1,0:T(8,128)(2,1)S(1)} copy-done((bf16[16,8,3072]{2,1,0:T(8,128)(2,1)S(1)}, bf16[16,8,3072]{2,1,0:T(8,128)(2,1)}, u32[]{:S(2)}) %copy-start) | copy-done | bytes 786456
  1.8 0.0 copy-start.1
  1.8 0.7 copy-done.1
  2.4 0.0 copy-start.2
  2.4 0.7 copy-done.2
  3.1 5.7 %transform.1.after_ref = bf16[32,104,128]{2,1,0:T(8,128)(2,1)} custom-call(bf16[128,3072]{1,0:T(8,128)(2,1)S(1)} %bitcast.4, s32[1,32]{1,0:T(1,128)S(1)} %copy-done.1, s32[1,32]{1,0:T(1,128)S(1)} %copy-done.2, s32[1]{0:T(128)S(6)} %copy.5.count_ref), custom_call_target="tpu_custom_call" | custom-call | flops 1207959552 | bytes 2000000 | tf_op jit(solution)/shard_map/transform/pallas_call | solution.py:167
  8.8 11.7 %all-to-all-start = ((bf16[32,104,128]{2,1,0:T(8,128)(2,1)}), bf16[32,104,128]{2,1,0:T(8,128)(2,1)}, u32[]{:S(2)}, u32[]{:S(2)}) async-start(bf16[32,104,128]{2,1,0:T(8,128)(2,1)} %transform.1.after_ref), calls=%async_computation | async-start | bytes 1703936 | tf_op jit(solution)/shard_map/all_to_all | solution.py:332
  20.6 5.1 %inverse.1 = (f32[2,1024,128]{2,1,0:T(8,128)S(1)}, bf16[4096,256]{1,0:T(8,128)(2,1)S(1)}) custom-call(bf16[32,104,128]{2,1,0:T(8,128)(2,1)} %transform.1.after_ref), custom_call_target="tpu_custom_call" | custom-call | flops 40000000 | bytes 3000000 | tf_op jit(solution)/shard_map/inverse/pallas_call | solution.py:285
  25.7 18.8 %all-to-all-done.got_ref = bf16[32,104,128]{2,1,0:T(8,128)(2,1)} async-done(((bf16[32,104,128]{2,1,0:T(8,128)(2,1)}), bf16[32,104,128]{2,1,0:T(8,128)(2,1)}, u32[]{:S(2)}, u32[]{:S(2)}) %all-to-all-start) | async-done | bytes 852000 | tf_op jit(solution)/shard_map/all_to_all | solution.py:332
  44.5 2.5 %cross.3 = f32[512,128]{1,0:T(8,128)S(1)} custom-call(bf16[32,104,128]{2,1,0:T(8,128)(2,1)} %all-to-all-done.got_ref, f32[2,1024,128]{2,1,0:T(8,128)S(1)} %get-tuple-element.7.after_ref.turn_ref), custom_call_target="tpu_custom_call" | custom-call | flops 603979776 | bytes 2000000 | tf_op jit(solution)/shard_map/cross/pallas_call | solution.py:235
  47.0 0.1 collective-permute-start
  47.1 2.5 %cross.2 = f32[512,128]{1,0:T(8,128)S(1)} custom-call(bf16[32,104,128]{2,1,0:T(8,128)(2,1)} %all-to-all-done.got_ref, f32[2,1024,128]{2,1,0:T(8,128)S(1)} %get-tuple-element.7.after_ref.turn_ref), custom_call_target="tpu_custom_call" | custom-call | flops 603979776 | bytes 2000000 | tf_op jit(solution)/shard_map/cross/pallas_call | solution.py:235
  49.5 0.0 collective-permute-done
  49.6 24.3 %all_to_all.10 = f32[128,4,128]{2,1,0:T(4,128)S(1)} all-to-all(f32[128,4,128]{2,1,0:T(4,128)S(1)} %bitcast.5), channel_id=1, replica_groups=mesh['chan'=32,'x'=4,'core'=2] {'chan','x'}, dimensions={0} | all-to-all | bytes 524288 | tf_op jit(solution)/shard_map/all_to_all | solution.py:337
  73.9 1.2 %lags.1 = f32[4,1024]{1,0:T(4,128)} custom-call(f32[512,128]{1,0:T(8,128)S(1)} %bitcast.3, f32[2,1024,128]{2,1,0:T(8,128)S(1)} %get-tuple-element.7.after_ref.turn_ref, bf16[4096,256]{1,0:T(8,128)(2,1)S(1)} %get-tuple-element.8.table_ref), custom_call_target="tpu_custom_call" | custom-call | flops 134217728 | bytes 4000000 | tf_op jit(solution)/shard_map/lags/pallas_call | solution.py:318
  (1 shorter events, 0.0 us)
Async XLA Ops:
  0.7 1.1 %copy-start = (bf16[16,8,3072]{2,1,0:T(8,128)(2,1)S(1)}, bf16[16,8,3072]{2,1,0:T(8,128)(2,1)}, u32[]{:S(2)}) copy-start(bf16[16,8,3072]{2,1,0:T(8,128)(2,1)} %param.4) | copy-start | bytes 2359300
  1.8 0.7 copy-start.1
  2.4 0.7 copy-start.2
  8.8 35.7 %all-to-all-start = ((bf16[32,104,128]{2,1,0:T(8,128)(2,1)}), bf16[32,104,128]{2,1,0:T(8,128)(2,1)}, u32[]{:S(2)}, u32[]{:S(2)}) async-start(bf16[32,104,128]{2,1,0:T(8,128)(2,1)} %transform.1.after_ref), calls=%async_computation | async-start | bytes 1703936 | tf_op jit(solution)/shard_map/all_to_all | solution.py:332
  47.0 2.6 %collective-permute-start = (f32[512,128]{1,0:T(8,128)S(1)}, f32[512,128]{1,0:T(8,128)S(1)}, u32[]{:S(2)}, u32[]{:S(2)}) collective-permute-start(f32[512,128]{1,0:T(8,128)S(1)} %cross.3), channel_id=1, source_target_pairs={{0,1},{1,0},{2,3},{3,2},{4,5},{5,4},{6,7},{7,6},{8,9},{9,8},{10,11... | collective-permute-start | bytes 786440 | tf_op jit(solution)/shard_map/ppermute | solution.py:335

commit v3 on v2

--- a/solution.py
+++ b/solution.py
@@ -43,8 +43,45 @@
     return lax.broadcasted_iota(jnp.int32, shape, axis)
 
 
-def transform_kernel(x_ref, source_ref, partner_ref, count_ref, out_ref,
-                     even_ref, odd_ref, base_ref, step_ref, table_ref, spec_ref, power_ref, white_ref, list_ref):
+def tables_kernel(table_ref, base_ref, step_ref):
+    bins = (iota((16, QUARTER), 1) + 1).astype(jnp.float32)
+    row = iota((16, QUARTER), 0).astype(jnp.float32)
+    base_ref[0], base_ref[1] = cos_sin((2.0 * row + 2.0) * bins)
+    base_ref[2], base_ref[3] = cos_sin((2.0 * row + 1.0) * bins)
+    for a in range(3):
+        cos, sin = cos_sin(32.0 * (row + 16.0 * a) * bins)
+        step_ref[0, 16 * a:16 * a + 16, :] = cos
+        step_ref[1, 16 * a:16 * a + 16, :] = sin
+
+    @pl.loop(0, 48)
+    def _(a):
+        cos = step_ref[0, pl.ds(a, 1), :]
+        sin = step_ref[1, pl.ds(a, 1), :]
+        rows = pl.ds(pl.multiple_of(16 * a, 16), 16)
+        for parity in range(2):
+            base_cos, base_sin = base_ref[2 * parity], base_ref[2 * parity + 1]
+            table_ref[2 * parity, rows, :] = (base_cos * cos - base_sin * sin).astype(jnp.bfloat16)
+            table_ref[2 * parity + 1, rows, :] = (base_sin * cos + base_cos * sin).astype(jnp.bfloat16)
+
+
+def tables():
+    vmem = pl.BlockSpec(memory_space=pltpu.VMEM)
+    return pl.pallas_call(
+        tables_kernel,
+        out_shape=jax.ShapeDtypeStruct((4, QUARTER, QUARTER), jnp.bfloat16),
+        out_specs=vmem,
+        scratch_shapes=[
+            pltpu.VMEM((4, 16, QUARTER), jnp.float32),
+            pltpu.VMEM((2, 48, QUARTER), jnp.float32),
+        ],
+        compiler_params=pltpu.CompilerParams(vmem_limit_bytes=12 * MB),
+        cost_estimate=pl.CostEstimate(flops=20 * 10**6, bytes_accessed=5 * 10**6, transcendentals=0),
+        name="tables",
+    )()
+
+
+def transform_kernel(x_ref, source_ref, partner_ref, count_ref, table_ref, out_ref,
+                     even_ref, odd_ref, spec_ref, power_ref, white_ref, list_ref):
     partner = partner_ref[...]
     slot = iota((1, PAIRS), 1)
     source = jnp.where(slot < count_ref[0], source_ref[...], -1)
@@ -90,25 +127,6 @@
     for t in range(24):
         last = last + x_ref[:, 128 * t:128 * t + 128].astype(jnp.float32)
     last = jnp.sum(jnp.where(lane % 2 == 0, last, -last), axis=1, keepdims=True)
-
-    bins = (iota((16, QUARTER), 1) + 1).astype(jnp.float32)
-    row = iota((16, QUARTER), 0).astype(jnp.float32)
-    base_ref[0], base_ref[1] = cos_sin((2.0 * row + 2.0) * bins)
-    base_ref[2], base_ref[3] = cos_sin((2.0 * row + 1.0) * bins)
-    for a in range(3):
-        cos, sin = cos_sin(32.0 * (row + 16.0 * a) * bins)
-        step_ref[0, 16 * a:16 * a + 16, :] = cos
-        step_ref[1, 16 * a:16 * a + 16, :] = sin
-
-    @pl.loop(0, 48)
-    def _(a):
-        cos = step_ref[0, pl.ds(a, 1), :]
-        sin = step_ref[1, pl.ds(a, 1), :]
-        rows = pl.ds(pl.multiple_of(16 * a, 16), 16)
-        for parity in range(2):
-            base_cos, base_sin = base_ref[2 * parity], base_ref[2 * parity + 1]
-            table_ref[2 * parity, rows, :] = (base_cos * cos - base_sin * sin).astype(jnp.bfloat16)
-            table_ref[2 * parity + 1, rows, :] = (base_sin * cos + base_cos * sin).astype(jnp.bfloat16)
 
     for which in range(4):
         samples = even_ref if which < 2 else odd_ref
@@ -162,31 +180,28 @@
                 out_ref[8 * (t // 3) + s, at:at + CHANS, :] = slabs[s].astype(jnp.bfloat16)
 
 
-def transform(x, source, partner, count):
+def transform(x, source, partner, count, table):
     vmem = pl.BlockSpec(memory_space=pltpu.VMEM)
     return pl.pallas_call(
         transform_kernel,
         out_shape=jax.ShapeDtypeStruct((BLOCKS, PIECE, 128), jnp.bfloat16),
-        in_specs=[vmem, vmem, vmem, pl.BlockSpec(memory_space=pltpu.SMEM)],
+        in_specs=[vmem, vmem, vmem, pl.BlockSpec(memory_space=pltpu.SMEM), vmem],
         out_specs=vmem,
         scratch_shapes=[
             pltpu.VMEM((2 * ROWS, QUARTER), jnp.bfloat16),
             pltpu.VMEM((2 * ROWS, QUARTER), jnp.bfloat16),
-            pltpu.VMEM((4, 16, QUARTER), jnp.float32),
-            pltpu.VMEM((2, 48, QUARTER), jnp.float32),
-            pltpu.VMEM((4, QUARTER, QUARTER), jnp.bfloat16),
             pltpu.VMEM((4, 2 * ROWS, QUARTER), jnp.float32),
             pltpu.VMEM((12, ROWS, 128), jnp.float32),
             pltpu.VMEM((2, 12, ROWS, 128), jnp.float32),
             pltpu.VMEM((8, 128), jnp.float32),
         ],
-        compiler_params=pltpu.CompilerParams(vmem_limit_bytes=32 * MB),
+        compiler_params=pltpu.CompilerParams(vmem_limit_bytes=20 * MB),
         cost_estimate=pl.CostEstimate(flops=2 * 4 * 2 * ROWS * QUARTER**2, bytes_accessed=2 * 10**6, transcendentals=0),
         name="transform",
-    )(x, source, partner, count)
-
-
-def cross_kernel(away, got_ref, after_ref, out_ref, data_ref, near_ref, far_ref, list_ref):
+    )(x, source, partner, count, table)
+
+
+def cross_kernel(away, got_ref, out_ref, data_ref, near_ref, far_ref, list_ref):
     for q in range(6):
         data_ref[:, 128 * q:128 * q + 128] = got_ref[:, CHANS * q:CHANS * (q + 1), :].reshape(BLOCKS * CHANS, 128)
     lists = got_ref[:, DATA:PIECE, :].astype(jnp.float32)
@@ -226,16 +241,27 @@
         one = jnp.where(low, tiles[0] + pltpu.roll(tiles[0], 96, 1), tiles[1] + pltpu.roll(tiles[1], 32, 1))
         two = jnp.where(low, tiles[2] + pltpu.roll(tiles[2], 96, 1), 0.0)
         low = lane // 16 % 2 == 0
-        out_ref[rows, :] = jnp.where(low, one + pltpu.roll(one, 112, 1), two + pltpu.roll(two, 16, 1))
-
-
-def cross(got, after, away):
+        packed = jnp.where(low, one + pltpu.roll(one, 112, 1), two + pltpu.roll(two, 16, 1))
+        low = iota((8, 128), 0) < 4
+        for o in range(0, 16, 2):
+            for pair in range(2):
+                one = packed[16 * o + 8 * pair:16 * o + 8 * pair + 8]
+                two = packed[16 * o + 16 + 8 * pair:16 * o + 24 + 8 * pair]
+                for x, tile in (
+                    (2 * pair, jnp.where(low, one, pltpu.roll(two, 4, 0))),
+                    (2 * pair + 1, jnp.where(low, pltpu.roll(one, 4, 0), two)),
+                ):
+                    to = 4 * BLOCKS * ((x + 4 - lax.axis_index("x")) % 4) + 4 * (16 * m + o)
+                    out_ref[pl.ds(pl.multiple_of(to, 8), 8), :] = tile
+
+
+def cross(got, away):
     vmem = pl.BlockSpec(memory_space=pltpu.VMEM)
     pairs = BLOCKS * HALF_PAIRS
     return pl.pallas_call(
         functools.partial(cross_kernel, away),
         out_shape=jax.ShapeDtypeStruct((pairs, 128), jnp.float32),
-        in_specs=[vmem, pl.BlockSpec(memory_space=pl.ANY)],
+        in_specs=[vmem],
         out_specs=vmem,
         scratch_shapes=[
             pltpu.VMEM((BLOCKS * CHANS, 6 * 128), jnp.bfloat16),
@@ -246,7 +272,7 @@
         compiler_params=pltpu.CompilerParams(vmem_limit_bytes=16 * MB),
         cost_estimate=pl.CostEstimate(flops=2 * pairs * 768 * 768, bytes_accessed=2 * 10**6, transcendentals=0),
         name="cross",
-    )(got, after)
+    )(got)
 
 
 def bin_of(block, lane):
@@ -298,8 +324,9 @@
 
 def lags_kernel(got_ref, turn_ref, table_ref, out_ref, left_ref):
     for c in range(BLOCKS):
-        total = got_ref[16 * c:16 * c + 8, :] + got_ref[16 * c + 8:16 * c + 16, :]
-        total = total + pltpu.roll(total, 4, 0)
+        two = got_ref[8 * (c // 2):8 * (c // 2) + 8, :]
+        low = iota((8, 128), 0) < 4
+        total = jnp.where(low, two, pltpu.roll(two, 4, 0)) if c % 2 == 0 else jnp.where(low, pltpu.roll(two, 4, 0), two)
         total = jnp.concatenate([total] * 4, axis=0)
         at = slice(32 * c, 32 * c + 32)
         turned = total * turn_ref[0, at, :] + pltpu.roll(total, 64, 1) * turn_ref[1, at, :]
@@ -328,14 +355,16 @@
 
 
 def shards(records, pair_source, pair_partner, pair_count):
-    sent = transform(records.reshape(ROWS, N), pair_source, pair_partner, pair_count)
+    sent = transform(records.reshape(ROWS, N), pair_source, pair_partner, pair_count, tables())
     got = lax.all_to_all(sent, "chan", 0, 0)
-    turn, table = inverse(sent)
-    away = cross(got, turn, 1)
+    away = cross(got, 1)
     near = lax.ppermute(away, "core", [(0, 1), (1, 0)])
-    spectra = cross(got, turn, 0) + near
-    parts = lax.all_to_all(spectra.reshape(BLOCKS * 4, 4, 128), ("chan", "x"), 0, 0)
-    return lags(parts.reshape(BLOCKS * HALF_PAIRS, 128), turn, table)
+    spectra = (cross(got, 0) + near).reshape(4, 4 * BLOCKS, 128)
+    parts = [lax.ppermute(spectra[k], "x", [(x, (x + k) % 4) for x in range(4)]) for k in (1, 2, 3)]
+    turn, table = inverse(spectra)
+    total = spectra[0] + parts[0] + parts[1] + parts[2]
+    last = lax.all_to_all(total.reshape(BLOCKS, 4, 128), "chan", 0, 0)
+    return lags(last.reshape(4 * BLOCKS, 128), turn, table)
 
 
 def solution(mesh):

time: 75.9 us -> 69 us (0.909)
  blocking collectives: 24.3 us -> 35.4 us
  waiting for transfers between devices: 18.8 us -> 7.73 us
  Pallas kernels: 16.9 us -> 13.5 us
  local copies, waits for them, and re-layouts: 2.44 us -> 0.03 us
  starting transfers between devices: 11.8 us -> 10.8 us
    all_to_all x1, waiting for transfers between devices: 18.8 us -> 3.59 us  [shards(): last = lax.all_to_all(total.reshape(BLOCKS, 4, 128), 'chan', 0, 0)]
    all_to_all x1, blocking collectives: 24.3 us -> 35.4 us  [shards(): got = lax.all_to_all(sent, 'chan', 0, 0)]
    all_to_all x1, starting transfers between devices: 11.7 us -> 5.57 us  [shards(): last = lax.all_to_all(total.reshape(BLOCKS, 4, 128), 'chan', 0, 0)]
    ppermute x0 -> x3, starting transfers between devices: none -> 5.13 us  [shards(): lax.ppermute(spectra[k], 'x', [(x, (x + k) % 4) for x in range(4)])]
    ppermute x0 -> x3, waiting for transfers between devices: none -> 3.95 us  [shards(): lax.ppermute(spectra[k], 'x', [(x, (x + k) % 4) for x in range(4)])]
    pallas_call x1, Pallas kernels: 5.7 us -> 2.69 us  [transform(): pl.pallas_call(transform_kernel, out_shape=jax.ShapeDtypeStruct((BLOCKS,...]
    unnamed x6, local copies, waits for them, and re-layouts: 2.44 us -> 0.01 us
    pallas_call x2, Pallas kernels: 4.95 us -> 2.66 us  [cross(): pl.pallas_call(functools.partial(cross_kernel, away), out_shape=jax.Shape...]
  transfers between devices with their start and end apart: 2 -> 5, of which waited for: 1 -> 5; matrix products, arithmetic and copies ran while one was open for 0% -> 0% of each run, Pallas kernels for 10% -> 9%
where the time goes in v3:
time: 69 us; the launch traced here: 68.8 us
  blocking collectives  35.4 us (51%)
  Pallas kernels  13.5 us (20%)
  starting transfers between devices  10.8 us (16%)
  waiting for transfers between devices  7.73 us (11%)
  between operations  0.74 us (1%)
    all_to_all x1, blocking collectives, shards(): got = lax.all_to_all(sent, 'chan', 0, 0)  35.4 us
    all_to_all x1, starting transfers between devices, shards(): last = lax.all_to_all(total.reshape(BLOCKS, 4, 128), 'chan', 0, 0)  5.57 us
    ppermute x3, starting transfers between devices, shards(): lax.ppermute(spectra[k], 'x', [(x, (x + k) % 4) for x in range(4)])  5.13 us
    pallas_call x1, Pallas kernels, inverse(): pl.pallas_call(inverse_kernel, out_shape=(jax.ShapeDtypeStruct((2, 32 * B...  5.11 us
    ppermute x3, waiting for transfers between devices, shards(): lax.ppermute(spectra[k], 'x', [(x, (x + k) % 4) for x in range(4)])  3.95 us
    all_to_all x1, waiting for transfers between devices, shards(): last = lax.all_to_all(total.reshape(BLOCKS, 4, 128), 'chan', 0, 0)  3.59 us
    pallas_call x1, Pallas kernels, transform(): pl.pallas_call(transform_kernel, out_shape=jax.ShapeDtypeStruct((BLOCKS,...  2.69 us
    pallas_call x2, Pallas kernels, cross(): pl.pallas_call(functools.partial(cross_kernel, away), out_shape=jax.Shape...  2.66 us
  transfers between devices with their start and end apart: 5, of which 5 were waited for; matrix products, arithmetic and copies ran while one was open for 0% of the time, Pallas kernels for 9%

profile of v3, /device:TPU:8, one launch (start us, length us, event | category | flops | bytes accessed | tf_op | source)
XLA Modules:
  0.0 68.8 jit_solution(7941504386262711410)
XLA Ops:
  0.0 0.0 copy-start.2
  0.0 0.0 copy-start.1
  0.0 0.0 copy-start
  0.0 1.9 %tables.1.table_ref = bf16[4,768,768]{2,1,0:T(8,128)(2,1)S(1)} custom-call(), custom_call_target="tpu_custom_call" | custom-call | flops 20000000 | bytes 5000000 | tf_op jit(solution)/shard_map/tables/pallas_call | solution.py:69
  2.5 0.0 copy-done.2
  2.5 0.0 copy-done.1
  2.6 0.0 copy-done
  2.6 2.7 %transform.1 = bf16[32,104,128]{2,1,0:T(8,128)(2,1)S(1)} custom-call(bf16[128,3072]{1,0:T(8,128)(2,1)S(1)} %bitcast.5, s32[1,32]{1,0:T(1,128)S(1)} %copy-done.1, s32[1,32]{1,0:T(1,128)S(1)} %copy-done.2, s32[1]{0:T(128)S(6)} %copy.5.count_ref, bf16[4,768,768]{2,1,0:T(8,128)(2,1)S(1)} %tables.1.table_ref), custom_call_target="tpu_custom_call" | custom-call | flops 1207959552 | bytes 2000000 | tf_op jit(solution)/shard_map/transform/pallas_call | solution.py:185
  5.3 35.4 %all_to_all.10.got_ref = bf16[32,104,128]{2,1,0:T(8,128)(2,1)S(1)} all-to-all(bf16[32,104,128]{2,1,0:T(8,128)(2,1)S(1)} %transform.1), channel_id=1, replica_groups=mesh['chan'=32,'x'=4,'core'=2] {'chan'}, dimensions={0} | all-to-all | bytes 1703936 | tf_op jit(solution)/shard_map/all_to_all | solution.py:359
  40.6 1.3 %cross.3 = f32[512,128]{1,0:T(8,128)S(1)} custom-call(bf16[32,104,128]{2,1,0:T(8,128)(2,1)S(1)} %all_to_all.10.got_ref), custom_call_target="tpu_custom_call" | custom-call | flops 603979776 | bytes 2000000 | tf_op jit(solution)/shard_map/cross/pallas_call | solution.py:261
  42.0 0.1 collective-permute-start
  42.1 1.3 %cross.2 = f32[512,128]{1,0:T(8,128)S(1)} custom-call(bf16[32,104,128]{2,1,0:T(8,128)(2,1)S(1)} %all_to_all.10.got_ref), custom_call_target="tpu_custom_call" | custom-call | flops 603979776 | bytes 2000000 | tf_op jit(solution)/shard_map/cross/pallas_call | solution.py:261
  43.4 0.2 collective-permute-done
  43.6 1.6 %collective-permute-start.1 = (f32[128,128]{1,0:T(8,128)S(1)}, f32[128,128]{1,0:T(8,128)S(1)}, u32[]{:S(2)}, u32[]{:S(2)}) collective-permute-start(f32[128,128]{1,0:T(8,128)S(1)} %get-tuple-element.9), channel_id=1, source_target_pairs={{0,2},{2,4},{4,6},{6,0},{1,3},{3,5},{5,7},{7,1},{8,10},{10,12},{12... | collective-permute-start | bytes 196616 | tf_op jit(solution)/shard_map/ppermute | solution.py:363
  45.2 1.7 %collective-permute-start.3 = (f32[128,128]{1,0:T(8,128)S(1)}, f32[128,128]{1,0:T(8,128)S(1)}, u32[]{:S(2)}, u32[]{:S(2)}) collective-permute-start(f32[128,128]{1,0:T(8,128)S(1)} %get-tuple-element.10), channel_id=1, source_target_pairs={{0,6},{2,0},{4,2},{6,4},{1,7},{3,1},{5,3},{7,5},{8,14},{10,8},{12,... | collective-permute-start | bytes 196616 | tf_op jit(solution)/shard_map/ppermute | solution.py:363
  46.9 1.8 %collective-permute-start.2 = (f32[128,128]{1,0:T(8,128)S(1)}, f32[128,128]{1,0:T(8,128)S(1)}, u32[]{:S(2)}, u32[]{:S(2)}) collective-permute-start(f32[128,128]{1,0:T(8,128)S(1)} %get-tuple-element.11), channel_id=1, source_target_pairs={{0,4},{2,6},{4,0},{6,2},{1,5},{3,7},{5,1},{7,3},{8,12},{10,14},{12... | collective-permute-start | bytes 196616 | tf_op jit(solution)/shard_map/ppermute | solution.py:363
  48.8 0.5 collective-permute-done.1
  49.2 0.2 collective-permute-done.3
  49.5 3.2 %collective-permute-done.2 = f32[128,128]{1,0:T(8,128)S(1)} collective-permute-done((f32[128,128]{1,0:T(8,128)S(1)}, f32[128,128]{1,0:T(8,128)S(1)}, u32[]{:S(2)}, u32[]{:S(2)}) %collective-permute-start.2) | collective-permute-done | bytes 65568 | tf_op jit(solution)/shard_map/ppermute | solution.py:363
  52.7 0.6 fusion.1
  53.4 5.6 %all-to-all-start.1 = ((f32[32,4,128]{2,1,0:T(4,128)}), f32[32,4,128]{2,1,0:T(4,128)S(1)}, u32[]{:S(2)}, u32[]{:S(2)}) async-start(f32[32,4,128]{2,1,0:T(4,128)} %bitcast.1), calls=%async_computation.1 | async-start | bytes 131072 | tf_op jit(solution)/shard_map/all_to_all | solution.py:366
  58.9 5.1 %inverse.1 = (f32[2,1024,128]{2,1,0:T(8,128)S(1)}, bf16[4096,256]{1,0:T(8,128)(2,1)S(1)}) custom-call(f32[4,128,128]{2,1,0:T(8,128)S(1)} %bitcast.4), custom_call_target="tpu_custom_call" | custom-call | flops 40000000 | bytes 3000000 | tf_op jit(solution)/shard_map/inverse/pallas_call | solution.py:311
  64.0 3.6 %all-to-all-done.1 = f32[32,4,128]{2,1,0:T(4,128)S(1)} async-done(((f32[32,4,128]{2,1,0:T(4,128)}), f32[32,4,128]{2,1,0:T(4,128)S(1)}, u32[]{:S(2)}, u32[]{:S(2)}) %all-to-all-start.1) | async-done | bytes 65568 | tf_op jit(solution)/shard_map/all_to_all | solution.py:366
  67.6 1.2 %lags.1 = f32[4,1024]{1,0:T(4,128)} custom-call(f32[128,128]{1,0:T(8,128)S(1)} %bitcast.6, f32[2,1024,128]{2,1,0:T(8,128)S(1)} %get-tuple-element.7.turn_ref, bf16[4096,256]{1,0:T(8,128)(2,1)S(1)} %get-tuple-element.8.table_ref), custom_call_target="tpu_custom_call" | custom-call | flops 134217728 | bytes 4000000 | tf_op jit(solution)/shard_map/lags/pallas_call | solution.py:345
  (2 shorter events, 0.0 us)
Async XLA Ops:
  0.0 2.5 %copy-start.2 = (s32[1,32]{1,0:T(1,128)S(1)}, s32[1,32]{1,0:T(1,128)}, u32[]{:S(2)}) copy-start(s32[1,32]{1,0:T(1,128)} %partner_ref.1) | copy-start | bytes 388
  0.0 2.5 %copy-start.1 = (s32[1,32]{1,0:T(1,128)S(1)}, s32[1,32]{1,0:T(1,128)}, u32[]{:S(2)}) copy-start(s32[1,32]{1,0:T(1,128)} %source_ref.1) | copy-start | bytes 388
  0.0 2.5 %copy-start = (bf16[16,8,3072]{2,1,0:T(8,128)(2,1)S(1)}, bf16[16,8,3072]{2,1,0:T(8,128)(2,1)}, u32[]{:S(2)}) copy-start(bf16[16,8,3072]{2,1,0:T(8,128)(2,1)} %param.4) | copy-start | bytes 2359300
  42.0 1.6 %collective-permute-start = (f32[512,128]{1,0:T(8,128)S(1)}, f32[512,128]{1,0:T(8,128)S(1)}, u32[]{:S(2)}, u32[]{:S(2)}) collective-permute-start(f32[512,128]{1,0:T(8,128)S(1)} %cross.3), channel_id=1, source_target_pairs={{0,1},{1,0},{2,3},{3,2},{4,5},{5,4},{6,7},{7,6},{8,9},{9,8},{10,11... | collective-permute-start | bytes 786440 | tf_op jit(solution)/shard_map/ppermute | solution.py:361
  43.6 5.6 %collective-permute-start.1 = (f32[128,128]{1,0:T(8,128)S(1)}, f32[128,128]{1,0:T(8,128)S(1)}, u32[]{:S(2)}, u32[]{:S(2)}) collective-permute-start(f32[128,128]{1,0:T(8,128)S(1)} %get-tuple-element.9), channel_id=1, source_target_pairs={{0,2},{2,4},{4,6},{6,0},{1,3},{3,5},{5,7},{7,1},{8,10},{10,12},{12... | collective-permute-start | bytes 196616 | tf_op jit(solution)/shard_map/ppermute | solution.py:363
  45.2 4.3 %collective-permute-start.3 = (f32[128,128]{1,0:T(8,128)S(1)}, f32[128,128]{1,0:T(8,128)S(1)}, u32[]{:S(2)}, u32[]{:S(2)}) collective-permute-start(f32[128,128]{1,0:T(8,128)S(1)} %get-tuple-element.10), channel_id=1, source_target_pairs={{0,6},{2,0},{4,2},{6,4},{1,7},{3,1},{5,3},{7,5},{8,14},{10,8},{12,... | collective-permute-start | bytes 196616 | tf_op jit(solution)/shard_map/ppermute | solution.py:363
  46.9 5.8 %collective-permute-start.2 = (f32[128,128]{1,0:T(8,128)S(1)}, f32[128,128]{1,0:T(8,128)S(1)}, u32[]{:S(2)}, u32[]{:S(2)}) collective-permute-start(f32[128,128]{1,0:T(8,128)S(1)} %get-tuple-element.11), channel_id=1, source_target_pairs={{0,4},{2,6},{4,0},{6,2},{1,5},{3,7},{5,1},{7,3},{8,12},{10,14},{12... | collective-permute-start | bytes 196616 | tf_op jit(solution)/shard_map/ppermute | solution.py:363
  53.4 14.3 %all-to-all-start.1 = ((f32[32,4,128]{2,1,0:T(4,128)}), f32[32,4,128]{2,1,0:T(4,128)S(1)}, u32[]{:S(2)}, u32[]{:S(2)}) async-start(f32[32,4,128]{2,1,0:T(4,128)} %bitcast.1), calls=%async_computation.1 | async-start | bytes 131072 | tf_op jit(solution)/shard_map/all_to_all | solution.py:366

commit v4 on v3

--- a/solution.py
+++ b/solution.py
@@ -80,26 +80,8 @@
     )()
 
 
-def transform_kernel(x_ref, source_ref, partner_ref, count_ref, table_ref, out_ref,
-                     even_ref, odd_ref, spec_ref, power_ref, white_ref, list_ref):
-    partner = partner_ref[...]
-    slot = iota((1, PAIRS), 1)
-    source = jnp.where(slot < count_ref[0], source_ref[...], -1)
-    list_ref[...] = jnp.zeros((8, 128), jnp.float32)
-    list_ref[0:1, 0:PAIRS] = (partner // CHANS).astype(jnp.float32)
-    list_ref[1:2, 0:PAIRS] = (partner % CHANS).astype(jnp.float32)
-    list_ref[2:3, 0:PAIRS] = source.astype(jnp.float32)
-    plain = list_ref[...]
-    lane = iota((8, 128), 1)
-    lists = jnp.zeros((8, 128), jnp.float32)
-    for quad in range(8):
-        at, to = 4 * quad, 16 * (quad % 2) + 4 * (quad // 2)
-        moved = pltpu.roll(plain, (to - at) % 128, 1)
-        lists = jnp.where((lane >= to) & (lane < to + 4), moved, lists)
-    lists = lists.astype(jnp.bfloat16)
-    for c in range(BLOCKS):
-        out_ref[c, DATA:PIECE, :] = lists
-
+def transform_kernel(x_ref, source_ref, partner_ref, table_ref, out_ref,
+                     even_ref, odd_ref, power_ref, white_ref, list_ref):
     lane = iota((ROWS, 128), 1)
     i = iota((256, 256), 0)
     k = iota((256, 256), 1)
@@ -128,26 +110,27 @@
         last = last + x_ref[:, 128 * t:128 * t + 128].astype(jnp.float32)
     last = jnp.sum(jnp.where(lane % 2 == 0, last, -last), axis=1, keepdims=True)
 
-    for which in range(4):
-        samples = even_ref if which < 2 else odd_ref
-        spec_ref[which] = jnp.dot(samples[...], table_ref[which], preferred_element_type=jnp.float32)
-
-    top, bottom = slice(0, ROWS), slice(ROWS, 2 * ROWS)
-    for t in range(6):
-        at = slice(128 * t, 128 * t + 128)
-        even_cos = spec_ref[0, top, at] + spec_ref[0, bottom, at] + first
-        even_sin = spec_ref[1, top, at] - spec_ref[1, bottom, at]
-        odd_cos = spec_ref[2, top, at] + spec_ref[2, bottom, at]
-        odd_sin = spec_ref[3, top, at] - spec_ref[3, bottom, at]
-        real, imag = even_cos + odd_cos, -(even_sin + odd_sin)
-        real_back, imag_back = even_cos - odd_cos, even_sin - odd_sin
-        if t == 5:
-            real_back = jnp.where(lane < 127, real_back, last)
-            imag_back = jnp.where(lane < 127, imag_back, 0.0)
-        white_ref[0, t], white_ref[1, t] = real, imag
-        white_ref[0, 6 + t], white_ref[1, 6 + t] = real_back, imag_back
-        power_ref[t] = real * real + imag * imag
-        power_ref[6 + t] = real_back * real_back + imag_back * imag_back
+    for u in range(3):
+        wide = slice(256 * u, 256 * u + 256)
+        even_cos, even_sin, odd_cos, odd_sin = (
+            jnp.dot(samples[...], table_ref[which, :, wide], preferred_element_type=jnp.float32)
+            for which, samples in enumerate((even_ref, even_ref, odd_ref, odd_ref))
+        )
+        even_cos = even_cos[:ROWS] + even_cos[ROWS:] + first
+        even_sin = even_sin[:ROWS] - even_sin[ROWS:]
+        odd_cos = odd_cos[:ROWS] + odd_cos[ROWS:]
+        odd_sin = odd_sin[:ROWS] - odd_sin[ROWS:]
+        for t in (2 * u, 2 * u + 1):
+            at = slice(128 * (t % 2), 128 * (t % 2) + 128)
+            real, imag = even_cos[:, at] + odd_cos[:, at], -(even_sin[:, at] + odd_sin[:, at])
+            real_back, imag_back = even_cos[:, at] - odd_cos[:, at], even_sin[:, at] - odd_sin[:, at]
+            if t == 5:
+                real_back = jnp.where(lane < 127, real_back, last)
+                imag_back = jnp.where(lane < 127, imag_back, 0.0)
+            white_ref[0, t], white_ref[1, t] = real, imag
+            white_ref[0, 6 + t], white_ref[1, 6 + t] = real_back, imag_back
+            power_ref[t] = real * real + imag * imag
+            power_ref[6 + t] = real_back * real_back + imag_back * imag_back
     factor = []
     for t in range(12):
         power = power_ref[t]
@@ -179,18 +162,33 @@
             for s in range(8):
                 out_ref[8 * (t // 3) + s, at:at + CHANS, :] = slabs[s].astype(jnp.bfloat16)
 
-
-def transform(x, source, partner, count, table):
+    partner = partner_ref[...]
+    list_ref[...] = jnp.zeros((8, 128), jnp.float32)
+    list_ref[0:1, 0:PAIRS] = (partner // CHANS).astype(jnp.float32)
+    list_ref[1:2, 0:PAIRS] = (partner % CHANS).astype(jnp.float32)
+    list_ref[2:3, 0:PAIRS] = source_ref[...].astype(jnp.float32)
+    plain = list_ref[...]
+    lane = iota((8, 128), 1)
+    lists = jnp.zeros((8, 128), jnp.float32)
+    for quad in range(8):
+        at, to = 4 * quad, 16 * (quad % 2) + 4 * (quad // 2)
+        moved = pltpu.roll(plain, (to - at) % 128, 1)
+        lists = jnp.where((lane >= to) & (lane < to + 4), moved, lists)
+    lists = lists.astype(jnp.bfloat16)
+    for c in range(BLOCKS):
+        out_ref[c, DATA:PIECE, :] = lists
+
+
+def transform(x, source, partner, table):
     vmem = pl.BlockSpec(memory_space=pltpu.VMEM)
     return pl.pallas_call(
         transform_kernel,
         out_shape=jax.ShapeDtypeStruct((BLOCKS, PIECE, 128), jnp.bfloat16),
-        in_specs=[vmem, vmem, vmem, pl.BlockSpec(memory_space=pltpu.SMEM), vmem],
+        in_specs=[vmem] * 4,
         out_specs=vmem,
         scratch_shapes=[
             pltpu.VMEM((2 * ROWS, QUARTER), jnp.bfloat16),
             pltpu.VMEM((2 * ROWS, QUARTER), jnp.bfloat16),
-            pltpu.VMEM((4, 2 * ROWS, QUARTER), jnp.float32),
             pltpu.VMEM((12, ROWS, 128), jnp.float32),
             pltpu.VMEM((2, 12, ROWS, 128), jnp.float32),
             pltpu.VMEM((8, 128), jnp.float32),
@@ -198,7 +196,7 @@
         compiler_params=pltpu.CompilerParams(vmem_limit_bytes=20 * MB),
         cost_estimate=pl.CostEstimate(flops=2 * 4 * 2 * ROWS * QUARTER**2, bytes_accessed=2 * 10**6, transcendentals=0),
         name="transform",
-    )(x, source, partner, count, table)
+    )(x, source, partner, table)
 
 
 def cross_kernel(away, got_ref, out_ref, data_ref, near_ref, far_ref, list_ref):
@@ -209,7 +207,7 @@
     list_ref[...] = jnp.zeros((2, 128, 128), jnp.float32)
     list_ref[0, 0:BLOCKS, :] = lists[:, 0, :] * CHANS + lists[:, 1, :]
     inside = (block % 16 * CHANS).astype(jnp.float32)
-    list_ref[1, 0:BLOCKS, :] = jnp.where(lists[:, 2, :] < 0.0, -1.0, lists[:, 2, :] + inside)
+    list_ref[1, 0:BLOCKS, :] = lists[:, 2, :] + inside
     partner = jnp.transpose(list_ref[0])
     source = jnp.transpose(list_ref[1])
     list_ref[0], list_ref[1] = partner, source
@@ -283,30 +281,69 @@
     return jnp.where(tile < 6, place, HALF - back), lane // 16 % 4 != 3
 
 
-def inverse_kernel(after_ref, turn_ref, table_ref):
+def inverse_kernel(count_ref, after_ref, turn_ref, table_ref, first_ref, powers_ref):
     scale = 1.0 / math.sqrt(HALF * 64)
-
-    @pl.loop(0, BLOCKS)
+    b = iota((96, 128), 1)
+    block, tile = iota((96, 128), 0) // 3, iota((96, 128), 0) % 3
+    place = 128 * (3 * (block // 8) + tile) + 16 * (block % 8) + 1
+    j0 = jnp.where(block < 16, place, HALF + 768 - place)
+    first_ref[0], first_ref[1] = cos_sin((j0 * b).astype(jnp.float32))
+    k = iota((16, 128), 0)
+    cos_k, sin_k = cos_sin((k * iota((16, 128), 1)).astype(jnp.float32))
+    nothing = jnp.zeros((16, 128), jnp.bfloat16)
+
+    def put(at, value):
+        coarse = value.astype(jnp.bfloat16)
+        rows = pl.ds(pl.multiple_of(at, 16), 16)
+        table_ref[rows, 0:128] = coarse
+        table_ref[rows, 128:256] = (value - coarse.astype(jnp.float32)).astype(jnp.bfloat16)
+
+    for back in range(2):
+        way = -sin_k if back else sin_k
+
+        @pl.loop(16 * back, 16 * back + 16, unroll=4)
+        def _(c):
+            for i, at in enumerate((0, 32, 16)):
+                cos, sin = first_ref[0, pl.ds(3 * c + i, 1), :], first_ref[1, pl.ds(3 * c + i, 1), :]
+                put(128 * c + at, cos * cos_k - sin * way)
+                put(128 * c + 64 + at, -(sin * cos_k + cos * way))
+            for at in (48, 112):
+                rows = pl.ds(pl.multiple_of(128 * c + at, 16), 16)
+                table_ref[rows, 0:128] = nothing
+                table_ref[rows, 128:256] = nothing
+
+    cos, sin = first_ref[0, 95:96, :], first_ref[1, 95:96, :]
+    end = jnp.where(iota((16, 128), 1) % 2 == 0, 1.0, -1.0)
+    put(128 * 31 + 16, jnp.where(k < 15, cos * cos_k + sin * sin_k, end))
+    put(128 * 31 + 80, jnp.where(k < 15, -(sin * cos_k - cos * sin_k), 0.0))
+
+    lane = iota((BLOCKS, 128), 1)
+    j, used = bin_of(iota((BLOCKS, 128), 0), lane)
+    factor = jnp.where(used, scale, 0.0)
+    signed = jnp.where(lane < 64, -factor, factor)
+    for a in range(5):
+        cos, sin = cos_sin((128 * a * j).astype(jnp.float32))
+        if a < 4:
+            powers_ref[0, 4 + a] = cos * factor
+            powers_ref[1, 4 + a] = sin * signed
+        if a > 0:
+            powers_ref[0, 4 - a] = cos * factor
+            powers_ref[1, 4 - a] = -sin * signed
+    row = iota((8, 128), 0)
+    low = row < 4
+    slot = 4 * (2 * lax.axis_index("x") + lax.axis_index("core")) + row % 4
+    live = jnp.where(slot < count_ref[0], 1.0, 0.0)
+
+    @pl.loop(0, BLOCKS, unroll=4)
     def _(c):
-        lane = iota((32, 128), 1)
-        a = iota((32, 128), 0) // 4 - 4
-        j, used = bin_of(c, lane)
-        cos, sin = cos_sin((128 * (a + 24) * j).astype(jnp.float32))
-        factor = jnp.where(used, scale, 0.0)
-        rows = pl.ds(pl.multiple_of(32 * c, 32), 32)
-        turn_ref[0, rows, :] = cos * factor
-        turn_ref[1, rows, :] = jnp.where(lane < 64, -sin, sin) * factor
-        lane = iota((128, 128), 0)
-        b = iota((128, 128), 1)
-        j, _ = bin_of(c, lane)
-        table, _ = cos_sin((j * b + jnp.where(lane < 64, 0, QUARTER)).astype(jnp.float32))
-        coarse = table.astype(jnp.bfloat16)
-        rows = pl.ds(pl.multiple_of(128 * c, 128), 128)
-        table_ref[rows, 0:128] = coarse
-        table_ref[rows, 128:256] = (table - coarse.astype(jnp.float32)).astype(jnp.bfloat16)
-
-
-def inverse(after):
+        row = pl.ds(c, 1)
+        for part in range(2):
+            for q in range(4):
+                two = jnp.where(low, powers_ref[part, 2 * q, row, :], powers_ref[part, 2 * q + 1, row, :])
+                turn_ref[part, pl.ds(pl.multiple_of(32 * c + 8 * q, 8), 8), :] = two * live
+
+
+def inverse(count, after):
     vmem = pl.BlockSpec(memory_space=pltpu.VMEM)
     return pl.pallas_call(
         inverse_kernel,
@@ -314,12 +351,30 @@
             jax.ShapeDtypeStruct((2, 32 * BLOCKS, 128), jnp.float32),
             jax.ShapeDtypeStruct((128 * BLOCKS, 256), jnp.bfloat16),
         ),
-        in_specs=[pl.BlockSpec(memory_space=pl.ANY)],
+        in_specs=[pl.BlockSpec(memory_space=pltpu.SMEM), pl.BlockSpec(memory_space=pl.ANY)],
         out_specs=(vmem, vmem),
+        scratch_shapes=[pltpu.VMEM((2, 96, 128), jnp.float32), pltpu.VMEM((2, 8, BLOCKS, 128), jnp.float32)],
         compiler_params=pltpu.CompilerParams(vmem_limit_bytes=12 * MB),
-        cost_estimate=pl.CostEstimate(flops=40 * 10**6, bytes_accessed=3 * 10**6, transcendentals=0),
+        cost_estimate=pl.CostEstimate(flops=10 * 10**6, bytes_accessed=3 * 10**6, transcendentals=0),
         name="inverse",
-    )(after)
+    )(count, after)
+
+
+def total_kernel(own_ref, one_ref, two_ref, three_ref, after_ref, out_ref):
+    out_ref[...] = own_ref[...] + one_ref[...] + two_ref[...] + three_ref[...]
+
+
+def add_parts(own, parts, after):
+    vmem = pl.BlockSpec(memory_space=pltpu.VMEM)
+    return pl.pallas_call(
+        total_kernel,
+        out_shape=jax.ShapeDtypeStruct(own.shape, jnp.float32),
+        in_specs=[vmem] * 4 + [pl.BlockSpec(memory_space=pl.ANY)],
+        out_specs=vmem,
+        compiler_params=pltpu.CompilerParams(vmem_limit_bytes=4 * MB),
+        cost_estimate=pl.CostEstimate(flops=10**5, bytes_accessed=3 * 10**5, transcendentals=0),
+        name="total",
+    )(own, *parts, after)
 
 
 def lags_kernel(got_ref, turn_ref, table_ref, out_ref, left_ref):
@@ -355,14 +410,14 @@
 
 
 def shards(records, pair_source, pair_partner, pair_count):
-    sent = transform(records.reshape(ROWS, N), pair_source, pair_partner, pair_count, tables())
+    sent = transform(records.reshape(ROWS, N), pair_source, pair_partner, tables())
     got = lax.all_to_all(sent, "chan", 0, 0)
     away = cross(got, 1)
     near = lax.ppermute(away, "core", [(0, 1), (1, 0)])
     spectra = (cross(got, 0) + near).reshape(4, 4 * BLOCKS, 128)
     parts = [lax.ppermute(spectra[k], "x", [(x, (x + k) % 4) for x in range(4)]) for k in (1, 2, 3)]
-    turn, table = inverse(spectra)
-    total = spectra[0] + parts[0] + parts[1] + parts[2]
+    turn, table = inverse(pair_count, spectra)
+    total = add_parts(spectra[0], parts, turn)
     last = lax.all_to_all(total.reshape(BLOCKS, 4, 128), "chan", 0, 0)
     return lags(last.reshape(4 * BLOCKS, 128), turn, table)
 

time: 69 us -> 67.5 us (0.978); the launches traced: 68.8 us -> 66.4 us
  blocking collectives: 35.4 us -> 49.3 us
  waiting for transfers between devices: 7.73 us -> 1.39 us
  starting transfers between devices: 10.8 us -> 5.83 us
  Pallas kernels: 13.5 us -> 8.99 us
    all_to_all x0 -> x1, blocking collectives: none -> 14 us  [shards(): last = lax.all_to_all(total.reshape(BLOCKS, 4, 128), 'chan', 0, 0)]
    all_to_all x1 -> x0, starting transfers between devices: 5.57 us -> none  [shards(): last = lax.all_to_all(total.reshape(BLOCKS, 4, 128), 'chan', 0, 0)]
    pallas_call x1, Pallas kernels: 5.11 us -> 0.98 us  [inverse(): pl.pallas_call(inverse_kernel, out_shape=(jax.ShapeDtypeStruct((2, 32 * B...]
    all_to_all x1 -> x0, waiting for transfers between devices: 3.59 us -> none  [shards(): last = lax.all_to_all(total.reshape(BLOCKS, 4, 128), 'chan', 0, 0)]
    ppermute x3, waiting for transfers between devices: 3.95 us -> 1.18 us  [shards(): lax.ppermute(spectra[k], 'x', [(x, (x + k) % 4) for x in range(4)])]
  transfers between devices with their start and end apart: 5 -> 4, of which waited for: 5 -> 3; matrix products, arithmetic and copies ran while one was open for 0% -> 0% of each run, Pallas kernels for 9% -> 3%
where the time goes in v4:
time: 67.5 us; the launch traced here: 66.4 us
  blocking collectives  49.3 us (73%)
  Pallas kernels  8.99 us (13%)
  starting transfers between devices  5.83 us (9%)
  waiting for transfers between devices  1.39 us (2%)
  between operations  0.75 us (1%)
    all_to_all x1, blocking collectives, shards(): got = lax.all_to_all(sent, 'chan', 0, 0)  35.4 us
    all_to_all x1, blocking collectives, shards(): last = lax.all_to_all(total.reshape(BLOCKS, 4, 128), 'chan', 0, 0)  14 us
    ppermute x3, starting transfers between devices, shards(): lax.ppermute(spectra[k], 'x', [(x, (x + k) % 4) for x in range(4)])  5.74 us
    pallas_call x2, Pallas kernels, cross(): pl.pallas_call(functools.partial(cross_kernel, away), out_shape=jax.Shape...  2.61 us
    pallas_call x1, Pallas kernels, transform(): pl.pallas_call(transform_kernel, out_shape=jax.ShapeDtypeStruct((BLOCKS,...  2.36 us
    pallas_call x1, Pallas kernels, tables(): pl.pallas_call(tables_kernel, out_shape=jax.ShapeDtypeStruct((4, QUARTER,...  1.87 us
  transfers between devices with their start and end apart: 4, of which 3 were waited for; matrix products, arithmetic and copies ran while one was open for 0% of the time, Pallas kernels for 3%

profile of v4, /device:TPU:8, one launch (start us, length us, event | category | flops | bytes accessed | tf_op | source)
XLA Modules:
  0.0 66.4 jit_solution(8037993896700686404)
XLA Ops:
  0.0 0.0 copy-start
  0.0 0.0 copy-start.1
  0.0 0.0 copy-start.2
  0.0 1.9 %tables.1.table_ref = bf16[4,768,768]{2,1,0:T(8,128)(2,1)S(1)} custom-call(), custom_call_target="tpu_custom_call" | custom-call | flops 20000000 | bytes 5000000 | tf_op jit(solution)/shard_map/tables/pallas_call | solution.py:69
  1.9 0.0 copy-done
  1.9 0.0 copy-done.1
  1.9 0.0 copy-done.2
  1.9 2.4 %transform.1 = bf16[32,104,128]{2,1,0:T(8,128)(2,1)S(1)} custom-call(bf16[128,3072]{1,0:T(8,128)(2,1)S(1)} %bitcast.5, s32[1,32]{1,0:T(1,128)S(1)} %copy-done.1, s32[1,32]{1,0:T(1,128)S(1)} %copy-done.2, bf16[4,768,768]{2,1,0:T(8,128)(2,1)S(1)} %tables.1.table_ref), custom_call_target="tpu_custom_call" | custom-call | flops 1207959552 | bytes 2000000 | tf_op jit(solution)/shard_map/transform/pallas_call | solution.py:184
  4.3 35.4 %all_to_all.10.got_ref = bf16[32,104,128]{2,1,0:T(8,128)(2,1)S(1)} all-to-all(bf16[32,104,128]{2,1,0:T(8,128)(2,1)S(1)} %transform.1), channel_id=1, replica_groups=mesh['chan'=32,'x'=4,'core'=2] {'chan'}, dimensions={0} | all-to-all | bytes 1703936 | tf_op jit(solution)/shard_map/all_to_all | solution.py:414
  39.6 1.3 %cross.3 = f32[512,128]{1,0:T(8,128)S(1)} custom-call(bf16[32,104,128]{2,1,0:T(8,128)(2,1)S(1)} %all_to_all.10.got_ref), custom_call_target="tpu_custom_call" | custom-call | flops 603979776 | bytes 2000000 | tf_op jit(solution)/shard_map/cross/pallas_call | solution.py:259
  40.9 0.1 collective-permute-start
  41.0 1.3 %cross.2 = f32[512,128]{1,0:T(8,128)S(1)} custom-call(bf16[32,104,128]{2,1,0:T(8,128)(2,1)S(1)} %all_to_all.10.got_ref), custom_call_target="tpu_custom_call" | custom-call | flops 603979776 | bytes 2000000 | tf_op jit(solution)/shard_map/cross/pallas_call | solution.py:259
  42.4 0.2 collective-permute-done
  42.6 1.6 %collective-permute-start.1 = (f32[128,128]{1,0:T(8,128)S(1)}, f32[128,128]{1,0:T(8,128)S(1)}, u32[]{:S(2)}, u32[]{:S(2)}) collective-permute-start(f32[128,128]{1,0:T(8,128)S(1)} %get-tuple-element.11), channel_id=1, source_target_pairs={{0,2},{2,4},{4,6},{6,0},{1,3},{3,5},{5,7},{7,1},{8,10},{10,12},{12... | collective-permute-start | bytes 196616 | tf_op jit(solution)/shard_map/ppermute | solution.py:418
  44.2 2.7 %collective-permute-start.2 = (f32[128,128]{1,0:T(8,128)S(1)}, f32[128,128]{1,0:T(8,128)S(1)}, u32[]{:S(2)}, u32[]{:S(2)}) collective-permute-start(f32[128,128]{1,0:T(8,128)S(1)} %get-tuple-element.10), channel_id=1, source_target_pairs={{0,4},{2,6},{4,0},{6,2},{1,5},{3,7},{5,1},{7,3},{8,12},{10,14},{12... | collective-permute-start | bytes 196616 | tf_op jit(solution)/shard_map/ppermute | solution.py:418
  46.9 1.4 %collective-permute-start.3 = (f32[128,128]{1,0:T(8,128)S(1)}, f32[128,128]{1,0:T(8,128)S(1)}, u32[]{:S(2)}, u32[]{:S(2)}) collective-permute-start(f32[128,128]{1,0:T(8,128)S(1)} %get-tuple-element.9), channel_id=1, source_target_pairs={{0,6},{2,0},{4,2},{6,4},{1,7},{3,1},{5,3},{7,5},{8,14},{10,8},{12,... | collective-permute-start | bytes 196616 | tf_op jit(solution)/shard_map/ppermute | solution.py:418
  49.0 1.0 %inverse.1 = (f32[2,1024,128]{2,1,0:T(8,128)S(1)}, bf16[4096,256]{1,0:T(8,128)(2,1)S(1)}) custom-call(s32[1]{0:T(128)S(6)} %copy.5.count_ref, f32[4,128,128]{2,1,0:T(8,128)S(1)} %bitcast.4), custom_call_target="tpu_custom_call" | custom-call | flops 10000000 | bytes 3000000 | tf_op jit(solution)/shard_map/inverse/pallas_call | solution.py:348
  50.0 0.0 collective-permute-done.1.one_ref
  50.0 0.6 collective-permute-done.2.two_ref
  50.6 0.6 collective-permute-done.3.three_ref
  51.2 14.0 %all_to_all.11 = f32[32,4,128]{2,1,0:T(4,128)S(1)} all-to-all(f32[32,4,128]{2,1,0:T(4,128)S(1)} %bitcast.7), channel_id=1, replica_groups=mesh['chan'=32,'x'=4,'core'=2] {'chan'}, dimensions={0} | all-to-all | bytes 131072 | tf_op jit(solution)/shard_map/all_to_all | solution.py:421
  65.2 1.2 %lags.1 = f32[4,1024]{1,0:T(4,128)} custom-call(f32[128,128]{1,0:T(8,128)S(1)} %bitcast.6, f32[2,1024,128]{2,1,0:T(8,128)S(1)} %get-tuple-element.7.after_ref.turn_ref, bf16[4096,256]{1,0:T(8,128)(2,1)S(1)} %get-tuple-element.8.table_ref), custom_call_target="tpu_custom_call" | custom-call | flops 134217728 | bytes 4000000 | tf_op jit(solution)/shard_map/lags/pallas_call | solution.py:400
  (3 shorter events, 0.1 us)
Async XLA Ops:
  0.0 1.9 %copy-start = (bf16[16,8,3072]{2,1,0:T(8,128)(2,1)S(1)}, bf16[16,8,3072]{2,1,0:T(8,128)(2,1)}, u32[]{:S(2)}) copy-start(bf16[16,8,3072]{2,1,0:T(8,128)(2,1)} %param.4) | copy-start | bytes 2359300
  0.0 1.9 %copy-start.1 = (s32[1,32]{1,0:T(1,128)S(1)}, s32[1,32]{1,0:T(1,128)}, u32[]{:S(2)}) copy-start(s32[1,32]{1,0:T(1,128)} %source_ref.1) | copy-start | bytes 388
  0.0 1.9 %copy-start.2 = (s32[1,32]{1,0:T(1,128)S(1)}, s32[1,32]{1,0:T(1,128)}, u32[]{:S(2)}) copy-start(s32[1,32]{1,0:T(1,128)} %partner_ref.1) | copy-start | bytes 388
  40.9 1.6 %collective-permute-start = (f32[512,128]{1,0:T(8,128)S(1)}, f32[512,128]{1,0:T(8,128)S(1)}, u32[]{:S(2)}, u32[]{:S(2)}) collective-permute-start(f32[512,128]{1,0:T(8,128)S(1)} %cross.3), channel_id=1, source_target_pairs={{0,1},{1,0},{2,3},{3,2},{4,5},{5,4},{6,7},{7,6},{8,9},{9,8},{10,11... | collective-permute-start | bytes 786440 | tf_op jit(solution)/shard_map/ppermute | solution.py:416
  42.6 7.4 %collective-permute-start.1 = (f32[128,128]{1,0:T(8,128)S(1)}, f32[128,128]{1,0:T(8,128)S(1)}, u32[]{:S(2)}, u32[]{:S(2)}) collective-permute-start(f32[128,128]{1,0:T(8,128)S(1)} %get-tuple-element.11), channel_id=1, source_target_pairs={{0,2},{2,4},{4,6},{6,0},{1,3},{3,5},{5,7},{7,1},{8,10},{10,12},{12... | collective-permute-start | bytes 196616 | tf_op jit(solution)/shard_map/ppermute | solution.py:418
  44.2 6.4 %collective-permute-start.2 = (f32[128,128]{1,0:T(8,128)S(1)}, f32[128,128]{1,0:T(8,128)S(1)}, u32[]{:S(2)}, u32[]{:S(2)}) collective-permute-start(f32[128,128]{1,0:T(8,128)S(1)} %get-tuple-element.10), channel_id=1, source_target_pairs={{0,4},{2,6},{4,0},{6,2},{1,5},{3,7},{5,1},{7,3},{8,12},{10,14},{12... | collective-permute-start | bytes 196616 | tf_op jit(solution)/shard_map/ppermute | solution.py:418
  46.9 4.3 %collective-permute-start.3 = (f32[128,128]{1,0:T(8,128)S(1)}, f32[128,128]{1,0:T(8,128)S(1)}, u32[]{:S(2)}, u32[]{:S(2)}) collective-permute-start(f32[128,128]{1,0:T(8,128)S(1)} %get-tuple-element.9), channel_id=1, source_target_pairs={{0,6},{2,0},{4,2},{6,4},{1,7},{3,1},{5,3},{7,5},{8,14},{10,8},{12,... | collective-permute-start | bytes 196616 | tf_op jit(solution)/shard_map/ppermute | solution.py:418

commit v5 on v4

--- a/solution.py
+++ b/solution.py
@@ -41,6 +41,10 @@
 
 def iota(shape, axis):
     return lax.broadcasted_iota(jnp.int32, shape, axis)
+
+
+ORDER = list(range(BLOCKS))[::-1]
+SLOT = [ORDER.index(block) for block in range(BLOCKS)]
 
 
 def tables_kernel(table_ref, base_ref, step_ref):
@@ -160,7 +164,7 @@
                 slabs = mixed
             at = CHANS * (2 * (t % 3) + part)
             for s in range(8):
-                out_ref[8 * (t // 3) + s, at:at + CHANS, :] = slabs[s].astype(jnp.bfloat16)
+                out_ref[SLOT[8 * (t // 3) + s], at:at + CHANS, :] = slabs[s].astype(jnp.bfloat16)
 
     partner = partner_ref[...]
     list_ref[...] = jnp.zeros((8, 128), jnp.float32)
@@ -200,14 +204,14 @@
 
 
 def cross_kernel(away, got_ref, out_ref, data_ref, near_ref, far_ref, list_ref):
-    for q in range(6):
-        data_ref[:, 128 * q:128 * q + 128] = got_ref[:, CHANS * q:CHANS * (q + 1), :].reshape(BLOCKS * CHANS, 128)
+    for o in range(BLOCKS):
+        for q in range(6):
+            rows = slice(CHANS * o, CHANS * (o + 1))
+            data_ref[rows, 128 * q:128 * q + 128] = got_ref[SLOT[o], CHANS * q:CHANS * (q + 1), :]
     lists = got_ref[:, DATA:PIECE, :].astype(jnp.float32)
-    block = iota((BLOCKS, 128), 0)
     list_ref[...] = jnp.zeros((2, 128, 128), jnp.float32)
     list_ref[0, 0:BLOCKS, :] = lists[:, 0, :] * CHANS + lists[:, 1, :]
-    inside = (block % 16 * CHANS).astype(jnp.float32)
-    list_ref[1, 0:BLOCKS, :] = lists[:, 2, :] + inside
+    list_ref[1, 0:BLOCKS, :] = lists[:, 2, :]
     partner = jnp.transpose(list_ref[0])
     source = jnp.transpose(list_ref[1])
     list_ref[0], list_ref[1] = partner, source
@@ -216,9 +220,10 @@
     partner, source = list_ref[0, pick, :], list_ref[1, pick, :]
     channel = iota((HALF_PAIRS, BLOCKS * CHANS), 1).astype(jnp.float32)
     for o in range(BLOCKS):
+        at = SLOT[o]
         rows = slice(HALF_PAIRS * o, HALF_PAIRS * (o + 1))
-        far_ref[rows, :] = jnp.where(channel == partner[:, o:o + 1], 1.0, 0.0).astype(jnp.bfloat16)
-        near = channel[:, :256] == source[:, o:o + 1]
+        far_ref[rows, :] = jnp.where(channel == partner[:, at:at + 1], 1.0, 0.0).astype(jnp.bfloat16)
+        near = channel[:, :256] == source[:, at:at + 1] + float(CHANS * (o % 16))
         near_ref[rows, :] = jnp.where(near, 1.0, 0.0).astype(jnp.bfloat16)
 
     size = 256
@@ -242,14 +247,17 @@
         packed = jnp.where(low, one + pltpu.roll(one, 112, 1), two + pltpu.roll(two, 16, 1))
         low = iota((8, 128), 0) < 4
         for o in range(0, 16, 2):
+            slots = SLOT[16 * m + o], SLOT[16 * m + o + 1]
             for pair in range(2):
                 one = packed[16 * o + 8 * pair:16 * o + 8 * pair + 8]
                 two = packed[16 * o + 16 + 8 * pair:16 * o + 24 + 8 * pair]
+                if slots[0] > slots[1]:
+                    one, two = two, one
                 for x, tile in (
                     (2 * pair, jnp.where(low, one, pltpu.roll(two, 4, 0))),
                     (2 * pair + 1, jnp.where(low, pltpu.roll(one, 4, 0), two)),
                 ):
-                    to = 4 * BLOCKS * ((x + 4 - lax.axis_index("x")) % 4) + 4 * (16 * m + o)
+                    to = 4 * BLOCKS * ((x + 4 - lax.axis_index("x")) % 4) + 4 * min(slots)
                     out_ref[pl.ds(pl.multiple_of(to, 8), 8), :] = tile
 
 
@@ -379,9 +387,11 @@
 
 def lags_kernel(got_ref, turn_ref, table_ref, out_ref, left_ref):
     for c in range(BLOCKS):
-        two = got_ref[8 * (c // 2):8 * (c // 2) + 8, :]
+        slot = SLOT[c]
+        two = got_ref[8 * (slot // 2):8 * (slot // 2) + 8, :]
         low = iota((8, 128), 0) < 4
-        total = jnp.where(low, two, pltpu.roll(two, 4, 0)) if c % 2 == 0 else jnp.where(low, pltpu.roll(two, 4, 0), two)
+        turned = pltpu.roll(two, 4, 0)
+        total = jnp.where(low, two, turned) if slot % 2 == 0 else jnp.where(low, turned, two)
         total = jnp.concatenate([total] * 4, axis=0)
         at = slice(32 * c, 32 * c + 32)
         turned = total * turn_ref[0, at, :] + pltpu.roll(total, 64, 1) * turn_ref[1, at, :]
@@ -411,14 +421,14 @@
 
 def shards(records, pair_source, pair_partner, pair_count):
     sent = transform(records.reshape(ROWS, N), pair_source, pair_partner, tables())
-    got = lax.all_to_all(sent, "chan", 0, 0)
+    got = lax.all_to_all(sent, "chan", 0, 0, axis_index_groups=[ORDER])
     away = cross(got, 1)
     near = lax.ppermute(away, "core", [(0, 1), (1, 0)])
     spectra = (cross(got, 0) + near).reshape(4, 4 * BLOCKS, 128)
     parts = [lax.ppermute(spectra[k], "x", [(x, (x + k) % 4) for x in range(4)]) for k in (1, 2, 3)]
     turn, table = inverse(pair_count, spectra)
     total = add_parts(spectra[0], parts, turn)
-    last = lax.all_to_all(total.reshape(BLOCKS, 4, 128), "chan", 0, 0)
+    last = lax.all_to_all(total.reshape(BLOCKS, 4, 128), "chan", 0, 0, axis_index_groups=[ORDER])
     return lags(last.reshape(4 * BLOCKS, 128), turn, table)
 
 

time: 67.5 us -> 64.6 us (0.957)
  blocking collectives: 49.3 us -> 46.4 us
    all_to_all x2, blocking collectives: 49.3 us -> 46.4 us  [the longest x1 30.9 us: shards(): got = lax.all_to_all(sent, 'chan', 0, 0, axis_index_groups=[ORDER])]
  transfers between devices with their start and end apart: 4 -> 4, of which waited for: 3 -> 3; matrix products, arithmetic and copies ran while one was open for 0% -> 0% of each run, Pallas kernels for 3% -> 4%
where the time goes in v5:
time: 64.6 us; the launch traced here: 63.4 us
  blocking collectives  46.4 us (72%)
  Pallas kernels  8.97 us (14%)
  starting transfers between devices  5.82 us (9%)
  waiting for transfers between devices  1.39 us (2%)
  between operations  0.75 us (1%)
    all_to_all x1, blocking collectives, shards(): got = lax.all_to_all(sent, 'chan', 0, 0, axis_index_groups=[ORDER])  30.9 us
    all_to_all x1, blocking collectives, shards(): lax.all_to_all(total.reshape(BLOCKS, 4, 128), 'chan', 0, 0, axis_index_gr...  15.5 us
    ppermute x3, starting transfers between devices, shards(): lax.ppermute(spectra[k], 'x', [(x, (x + k) % 4) for x in range(4)])  5.73 us
    pallas_call x2, Pallas kernels, cross(): pl.pallas_call(functools.partial(cross_kernel, away), out_shape=jax.Shape...  2.6 us
    pallas_call x1, Pallas kernels, transform(): pl.pallas_call(transform_kernel, out_shape=jax.ShapeDtypeStruct((BLOCKS,...  2.36 us
    pallas_call x1, Pallas kernels, tables(): pl.pallas_call(tables_kernel, out_shape=jax.ShapeDtypeStruct((4, QUARTER,...  1.87 us
  transfers between devices with their start and end apart: 4, of which 3 were waited for; matrix products, arithmetic and copies ran while one was open for 0% of the time, Pallas kernels for 4%

profile of v5, /device:TPU:8, one launch (start us, length us, event | category | flops | bytes accessed | tf_op | source)
XLA Modules:
  0.0 63.4 jit_solution(11645940504971442852)
XLA Ops:
  0.0 0.0 copy-start
  0.0 0.0 copy-start.1
  0.0 0.0 copy-start.2
  0.0 1.9 %tables.1.table_ref = bf16[4,768,768]{2,1,0:T(8,128)(2,1)S(1)} custom-call(), custom_call_target="tpu_custom_call" | custom-call | flops 20000000 | bytes 5000000 | tf_op jit(solution)/shard_map/tables/pallas_call | solution.py:73
  1.9 0.0 copy-done
  1.9 0.0 copy-done.1
  1.9 0.0 copy-done.2
  1.9 2.4 %transform.1 = bf16[32,104,128]{2,1,0:T(8,128)(2,1)S(1)} custom-call(bf16[128,3072]{1,0:T(8,128)(2,1)S(1)} %bitcast.5, s32[1,32]{1,0:T(1,128)S(1)} %copy-done.1, s32[1,32]{1,0:T(1,128)S(1)} %copy-done.2, bf16[4,768,768]{2,1,0:T(8,128)(2,1)S(1)} %tables.1.table_ref), custom_call_target="tpu_custom_call" | custom-call | flops 1207959552 | bytes 2000000 | tf_op jit(solution)/shard_map/transform/pallas_call | solution.py:188
  4.3 30.9 %all_to_all.10.got_ref = bf16[32,104,128]{2,1,0:T(8,128)(2,1)S(1)} all-to-all(bf16[32,104,128]{2,1,0:T(8,128)(2,1)S(1)} %transform.1), channel_id=1, replica_groups={{248,240,232,224,216,208,200,192,184,176,168,160,152,144,136,128,120,11..., dimensions={0} | all-to-all | bytes 1703936 | tf_op jit(solution)/shard_map/all_to_all | solution.py:424
  35.2 1.3 %cross.3 = f32[512,128]{1,0:T(8,128)S(1)} custom-call(bf16[32,104,128]{2,1,0:T(8,128)(2,1)S(1)} %all_to_all.10.got_ref), custom_call_target="tpu_custom_call" | custom-call | flops 603979776 | bytes 2000000 | tf_op jit(solution)/shard_map/cross/pallas_call | solution.py:267
  36.5 0.1 collective-permute-start
  36.6 1.3 %cross.2 = f32[512,128]{1,0:T(8,128)S(1)} custom-call(bf16[32,104,128]{2,1,0:T(8,128)(2,1)S(1)} %all_to_all.10.got_ref), custom_call_target="tpu_custom_call" | custom-call | flops 603979776 | bytes 2000000 | tf_op jit(solution)/shard_map/cross/pallas_call | solution.py:267
  37.9 0.2 collective-permute-done
  38.2 1.6 %collective-permute-start.1 = (f32[128,128]{1,0:T(8,128)S(1)}, f32[128,128]{1,0:T(8,128)S(1)}, u32[]{:S(2)}, u32[]{:S(2)}) collective-permute-start(f32[128,128]{1,0:T(8,128)S(1)} %get-tuple-element.11), channel_id=1, source_target_pairs={{0,2},{2,4},{4,6},{6,0},{1,3},{3,5},{5,7},{7,1},{8,10},{10,12},{12... | collective-permute-start | bytes 196616 | tf_op jit(solution)/shard_map/ppermute | solution.py:428
  39.8 2.7 %collective-permute-start.2 = (f32[128,128]{1,0:T(8,128)S(1)}, f32[128,128]{1,0:T(8,128)S(1)}, u32[]{:S(2)}, u32[]{:S(2)}) collective-permute-start(f32[128,128]{1,0:T(8,128)S(1)} %get-tuple-element.10), channel_id=1, source_target_pairs={{0,4},{2,6},{4,0},{6,2},{1,5},{3,7},{5,1},{7,3},{8,12},{10,14},{12... | collective-permute-start | bytes 196616 | tf_op jit(solution)/shard_map/ppermute | solution.py:428
  42.5 1.4 %collective-permute-start.3 = (f32[128,128]{1,0:T(8,128)S(1)}, f32[128,128]{1,0:T(8,128)S(1)}, u32[]{:S(2)}, u32[]{:S(2)}) collective-permute-start(f32[128,128]{1,0:T(8,128)S(1)} %get-tuple-element.9), channel_id=1, source_target_pairs={{0,6},{2,0},{4,2},{6,4},{1,7},{3,1},{5,3},{7,5},{8,14},{10,8},{12,... | collective-permute-start | bytes 196616 | tf_op jit(solution)/shard_map/ppermute | solution.py:428
  44.6 1.0 %inverse.1 = (f32[2,1024,128]{2,1,0:T(8,128)S(1)}, bf16[4096,256]{1,0:T(8,128)(2,1)S(1)}) custom-call(s32[1]{0:T(128)S(6)} %copy.5.count_ref, f32[4,128,128]{2,1,0:T(8,128)S(1)} %bitcast.4), custom_call_target="tpu_custom_call" | custom-call | flops 10000000 | bytes 3000000 | tf_op jit(solution)/shard_map/inverse/pallas_call | solution.py:356
  45.6 0.0 collective-permute-done.1.one_ref
  45.6 0.6 collective-permute-done.2.two_ref
  46.2 0.6 collective-permute-done.3.three_ref
  46.8 15.5 %all_to_all.11 = f32[32,4,128]{2,1,0:T(4,128)S(1)} all-to-all(f32[32,4,128]{2,1,0:T(4,128)S(1)} %bitcast.7), channel_id=1, replica_groups={{248,240,232,224,216,208,200,192,184,176,168,160,152,144,136,128,120,11..., dimensions={0} | all-to-all | bytes 131072 | tf_op jit(solution)/shard_map/all_to_all | solution.py:431
  62.3 1.2 %lags.1 = f32[4,1024]{1,0:T(4,128)} custom-call(f32[128,128]{1,0:T(8,128)S(1)} %bitcast.6, f32[2,1024,128]{2,1,0:T(8,128)S(1)} %get-tuple-element.7.after_ref.turn_ref, bf16[4096,256]{1,0:T(8,128)(2,1)S(1)} %get-tuple-element.8.table_ref), custom_call_target="tpu_custom_call" | custom-call | flops 134217728 | bytes 4000000 | tf_op jit(solution)/shard_map/lags/pallas_call | solution.py:410
  (3 shorter events, 0.1 us)
Async XLA Ops:
  0.0 1.9 %copy-start = (bf16[16,8,3072]{2,1,0:T(8,128)(2,1)S(1)}, bf16[16,8,3072]{2,1,0:T(8,128)(2,1)}, u32[]{:S(2)}) copy-start(bf16[16,8,3072]{2,1,0:T(8,128)(2,1)} %param.4) | copy-start | bytes 2359300
  0.0 1.9 %copy-start.1 = (s32[1,32]{1,0:T(1,128)S(1)}, s32[1,32]{1,0:T(1,128)}, u32[]{:S(2)}) copy-start(s32[1,32]{1,0:T(1,128)} %source_ref.1) | copy-start | bytes 388
  0.0 1.9 %copy-start.2 = (s32[1,32]{1,0:T(1,128)S(1)}, s32[1,32]{1,0:T(1,128)}, u32[]{:S(2)}) copy-start(s32[1,32]{1,0:T(1,128)} %partner_ref.1) | copy-start | bytes 388
  36.5 1.6 %collective-permute-start = (f32[512,128]{1,0:T(8,128)S(1)}, f32[512,128]{1,0:T(8,128)S(1)}, u32[]{:S(2)}, u32[]{:S(2)}) collective-permute-start(f32[512,128]{1,0:T(8,128)S(1)} %cross.3), channel_id=1, source_target_pairs={{0,1},{1,0},{2,3},{3,2},{4,5},{5,4},{6,7},{7,6},{8,9},{9,8},{10,11... | collective-permute-start | bytes 786440 | tf_op jit(solution)/shard_map/ppermute | solution.py:426
  38.2 7.4 %collective-permute-start.1 = (f32[128,128]{1,0:T(8,128)S(1)}, f32[128,128]{1,0:T(8,128)S(1)}, u32[]{:S(2)}, u32[]{:S(2)}) collective-permute-start(f32[128,128]{1,0:T(8,128)S(1)} %get-tuple-element.11), channel_id=1, source_target_pairs={{0,2},{2,4},{4,6},{6,0},{1,3},{3,5},{5,7},{7,1},{8,10},{10,12},{12... | collective-permute-start | bytes 196616 | tf_op jit(solution)/shard_map/ppermute | solution.py:428
  39.8 6.4 %collective-permute-start.2 = (f32[128,128]{1,0:T(8,128)S(1)}, f32[128,128]{1,0:T(8,128)S(1)}, u32[]{:S(2)}, u32[]{:S(2)}) collective-permute-start(f32[128,128]{1,0:T(8,128)S(1)} %get-tuple-element.10), channel_id=1, source_target_pairs={{0,4},{2,6},{4,0},{6,2},{1,5},{3,7},{5,1},{7,3},{8,12},{10,14},{12... | collective-permute-start | bytes 196616 | tf_op jit(solution)/shard_map/ppermute | solution.py:428
  42.5 4.3 %collective-permute-start.3 = (f32[128,128]{1,0:T(8,128)S(1)}, f32[128,128]{1,0:T(8,128)S(1)}, u32[]{:S(2)}, u32[]{:S(2)}) collective-permute-start(f32[128,128]{1,0:T(8,128)S(1)} %get-tuple-element.9), channel_id=1, source_target_pairs={{0,6},{2,0},{4,2},{6,4},{1,7},{3,1},{5,3},{7,5},{8,14},{10,8},{12,... | collective-permute-start | bytes 196616 | tf_op jit(solution)/shard_map/ppermute | solution.py:428

commit v6 on v5

--- a/solution.py
+++ b/solution.py
@@ -62,30 +62,29 @@
         cos = step_ref[0, pl.ds(a, 1), :]
         sin = step_ref[1, pl.ds(a, 1), :]
         rows = pl.ds(pl.multiple_of(16 * a, 16), 16)
-        for parity in range(2):
-            base_cos, base_sin = base_ref[2 * parity], base_ref[2 * parity + 1]
-            table_ref[2 * parity, rows, :] = (base_cos * cos - base_sin * sin).astype(jnp.bfloat16)
-            table_ref[2 * parity + 1, rows, :] = (base_sin * cos + base_cos * sin).astype(jnp.bfloat16)
+        base_cos, base_sin = base_ref[0], base_ref[1]
+        table_ref[0, rows, :] = (base_cos * cos - base_sin * sin).astype(jnp.bfloat16)
+        table_ref[1, rows, :] = (base_sin * cos + base_cos * sin).astype(jnp.bfloat16)
 
 
 def tables():
     vmem = pl.BlockSpec(memory_space=pltpu.VMEM)
     return pl.pallas_call(
         tables_kernel,
-        out_shape=jax.ShapeDtypeStruct((4, QUARTER, QUARTER), jnp.bfloat16),
-        out_specs=vmem,
-        scratch_shapes=[
-            pltpu.VMEM((4, 16, QUARTER), jnp.float32),
-            pltpu.VMEM((2, 48, QUARTER), jnp.float32),
-        ],
+        out_shape=(
+            jax.ShapeDtypeStruct((2, QUARTER, QUARTER), jnp.bfloat16),
+            jax.ShapeDtypeStruct((4, 16, QUARTER), jnp.float32),
+            jax.ShapeDtypeStruct((2, 48, QUARTER), jnp.float32),
+        ),
+        out_specs=(vmem,) * 3,
         compiler_params=pltpu.CompilerParams(vmem_limit_bytes=12 * MB),
-        cost_estimate=pl.CostEstimate(flops=20 * 10**6, bytes_accessed=5 * 10**6, transcendentals=0),
+        cost_estimate=pl.CostEstimate(flops=10**9, bytes_accessed=10**7, transcendentals=0),
         name="tables",
     )()
 
 
-def transform_kernel(x_ref, source_ref, partner_ref, table_ref, out_ref,
-                     even_ref, odd_ref, power_ref, white_ref, list_ref):
+def transform_kernel(x_ref, source_ref, partner_ref, even_table_ref, base_ref, step_ref, out_ref,
+                     odd_table_ref, even_ref, odd_ref, power_ref, white_ref, list_ref):
     lane = iota((ROWS, 128), 1)
     i = iota((256, 256), 0)
     k = iota((256, 256), 1)
@@ -114,11 +113,18 @@
         last = last + x_ref[:, 128 * t:128 * t + 128].astype(jnp.float32)
     last = jnp.sum(jnp.where(lane % 2 == 0, last, -last), axis=1, keepdims=True)
 
+    for a in range(48):
+        cos, sin = step_ref[0, a:a + 1, :], step_ref[1, a:a + 1, :]
+        base_cos, base_sin = base_ref[2], base_ref[3]
+        odd_table_ref[0, 16 * a:16 * a + 16, :] = (base_cos * cos - base_sin * sin).astype(jnp.bfloat16)
+        odd_table_ref[1, 16 * a:16 * a + 16, :] = (base_sin * cos + base_cos * sin).astype(jnp.bfloat16)
+
     for u in range(3):
         wide = slice(256 * u, 256 * u + 256)
         even_cos, even_sin, odd_cos, odd_sin = (
-            jnp.dot(samples[...], table_ref[which, :, wide], preferred_element_type=jnp.float32)
-            for which, samples in enumerate((even_ref, even_ref, odd_ref, odd_ref))
+            jnp.dot(samples[...], table[which, :, wide], preferred_element_type=jnp.float32)
+            for samples, table in ((even_ref, even_table_ref), (odd_ref, odd_table_ref))
+            for which in range(2)
         )
         even_cos = even_cos[:ROWS] + even_cos[ROWS:] + first
         even_sin = even_sin[:ROWS] - even_sin[ROWS:]
@@ -150,7 +156,9 @@
             scale = jnp.where(lane < 127, scale, factor[6 + (t - 5) % 6])
         for part in range(2):
             white_ref[part, t] = white_ref[part, t] * scale
-            slabs = [white_ref[part, t, pl.ds(w, CHANS, stride=WINS), :] for w in range(WINS)]
+            slabs = [
+                white_ref[part, t, pl.ds(w, CHANS, stride=WINS), :].astype(jnp.bfloat16) for w in range(WINS)
+            ]
             for bit in range(3):
                 step = 1 << bit
                 high = (segment // step) % 2 == 1
@@ -164,7 +172,7 @@
                 slabs = mixed
             at = CHANS * (2 * (t % 3) + part)
             for s in range(8):
-                out_ref[SLOT[8 * (t // 3) + s], at:at + CHANS, :] = slabs[s].astype(jnp.bfloat16)
+                out_ref[SLOT[8 * (t // 3) + s], at:at + CHANS, :] = slabs[s]
 
     partner = partner_ref[...]
     list_ref[...] = jnp.zeros((8, 128), jnp.float32)
@@ -188,9 +196,10 @@
     return pl.pallas_call(
         transform_kernel,
         out_shape=jax.ShapeDtypeStruct((BLOCKS, PIECE, 128), jnp.bfloat16),
-        in_specs=[vmem] * 4,
+        in_specs=[vmem] * 6,
         out_specs=vmem,
         scratch_shapes=[
+            pltpu.VMEM((2, QUARTER, QUARTER), jnp.bfloat16),
             pltpu.VMEM((2 * ROWS, QUARTER), jnp.bfloat16),
             pltpu.VMEM((2 * ROWS, QUARTER), jnp.bfloat16),
             pltpu.VMEM((12, ROWS, 128), jnp.float32),
@@ -200,7 +209,7 @@
         compiler_params=pltpu.CompilerParams(vmem_limit_bytes=20 * MB),
         cost_estimate=pl.CostEstimate(flops=2 * 4 * 2 * ROWS * QUARTER**2, bytes_accessed=2 * 10**6, transcendentals=0),
         name="transform",
-    )(x, source, partner, table)
+    )(x, source, partner, *table)
 
 
 def cross_kernel(away, got_ref, out_ref, data_ref, near_ref, far_ref, list_ref):
@@ -219,26 +228,25 @@
     pick = pl.ds(pl.multiple_of(HALF_PAIRS * core, HALF_PAIRS), HALF_PAIRS)
     partner, source = list_ref[0, pick, :], list_ref[1, pick, :]
     channel = iota((HALF_PAIRS, BLOCKS * CHANS), 1).astype(jnp.float32)
-    for o in range(BLOCKS):
-        at = SLOT[o]
-        rows = slice(HALF_PAIRS * o, HALF_PAIRS * (o + 1))
-        far_ref[rows, :] = jnp.where(channel == partner[:, at:at + 1], 1.0, 0.0).astype(jnp.bfloat16)
-        near = channel[:, :256] == source[:, at:at + 1] + float(CHANS * (o % 16))
-        near_ref[rows, :] = jnp.where(near, 1.0, 0.0).astype(jnp.bfloat16)
-
     size = 256
     lane = iota((size, 128), 1)
     for m in range(2):
+        for o in range(16 * m, 16 * m + 16):
+            at = SLOT[o]
+            rows = slice(HALF_PAIRS * o, HALF_PAIRS * (o + 1))
+            far_ref[rows, :] = jnp.where(channel == partner[:, at:at + 1], 1.0, 0.0).astype(jnp.bfloat16)
+            near = channel[:, :256] == source[:, at:at + 1] + float(CHANS * (o % 16))
+            near_ref[rows, :] = jnp.where(near, 1.0, 0.0).astype(jnp.bfloat16)
         rows = slice(size * m, size * (m + 1))
-        far = jnp.dot(far_ref[rows, :], data_ref[...], preferred_element_type=jnp.float32)
-        near = jnp.dot(near_ref[rows, :], data_ref[rows, :], preferred_element_type=jnp.float32)
         tiles = []
+        low = lane < 64
         for t in range(3):
-            re, im = slice(256 * t, 256 * t + 128), slice(256 * t + 128, 256 * t + 256)
-            a_re, a_im, b_re, b_im = near[:, re], near[:, im], far[:, re], far[:, im]
+            at = slice(256 * t, 256 * t + 256)
+            far = jnp.dot(far_ref[rows, :], data_ref[:, at], preferred_element_type=jnp.float32)
+            near = jnp.dot(near_ref[rows, :], data_ref[rows, at], preferred_element_type=jnp.float32)
+            a_re, a_im, b_re, b_im = near[:, :128], near[:, 128:], far[:, :128], far[:, 128:]
             real = a_re * b_re + a_im * b_im
             imag = a_im * b_re - a_re * b_im
-            low = lane < 64
             tiles.append(jnp.where(low, real, imag) + pltpu.roll(jnp.where(low, imag, real), 64, 1))
         low = lane // 32 % 2 == 0
         one = jnp.where(low, tiles[0] + pltpu.roll(tiles[0], 96, 1), tiles[1] + pltpu.roll(tiles[1], 32, 1))
@@ -425,7 +433,7 @@
     away = cross(got, 1)
     near = lax.ppermute(away, "core", [(0, 1), (1, 0)])
     spectra = (cross(got, 0) + near).reshape(4, 4 * BLOCKS, 128)
-    parts = [lax.ppermute(spectra[k], "x", [(x, (x + k) % 4) for x in range(4)]) for k in (1, 2, 3)]
+    parts = [lax.ppermute(spectra[k], "x", [(x, (x + k) % 4) for x in range(4)]) for k in (1, 3, 2)]
     turn, table = inverse(pair_count, spectra)
     total = add_parts(spectra[0], parts, turn)
     last = lax.all_to_all(total.reshape(BLOCKS, 4, 128), "chan", 0, 0, axis_index_groups=[ORDER])

time: 64.6 us -> 63.9 us (0.989); the launches traced: 63.4 us -> 63.5 us
  waiting for transfers between devices: 1.39 us -> 2.58 us
    ppermute x3, waiting for transfers between devices: 1.18 us -> 2.3 us  [shards(): lax.ppermute(spectra[k], 'x', [(x, (x + k) % 4) for x in range(4)])]
  transfers between devices with their start and end apart: 4 -> 4, of which waited for: 3 -> 2; matrix products, arithmetic and copies ran while one was open for 0% -> 0% of each run, Pallas kernels for 4% -> 3%
where the time goes in v6:
time: 63.9 us; the launch traced here: 63.5 us
  blocking collectives  46.4 us (73%)
  Pallas kernels  8.49 us (13%)
  starting transfers between devices  5.22 us (8%)
  waiting for transfers between devices  2.58 us (4%)
  between operations  0.75 us (1%)
    all_to_all x1, blocking collectives, shards(): got = lax.all_to_all(sent, 'chan', 0, 0, axis_index_groups=[ORDER])  30.9 us
    all_to_all x1, blocking collectives, shards(): lax.all_to_all(total.reshape(BLOCKS, 4, 128), 'chan', 0, 0, axis_index_gr...  15.4 us
    ppermute x3, starting transfers between devices, shards(): lax.ppermute(spectra[k], 'x', [(x, (x + k) % 4) for x in range(4)])  5.13 us
    pallas_call x1, Pallas kernels, transform(): pl.pallas_call(transform_kernel, out_shape=jax.ShapeDtypeStruct((BLOCKS,...  2.55 us
    pallas_call x2, Pallas kernels, cross(): pl.pallas_call(functools.partial(cross_kernel, away), out_shape=jax.Shape...  2.45 us
    ppermute x3, waiting for transfers between devices, shards(): lax.ppermute(spectra[k], 'x', [(x, (x + k) % 4) for x in range(4)])  2.3 us
    pallas_call x1, Pallas kernels, tables(): pl.pallas_call(tables_kernel, out_shape=(jax.ShapeDtypeStruct((2, QUARTER...  1.34 us
  transfers between devices with their start and end apart: 4, of which 2 were waited for; matrix products, arithmetic and copies ran while one was open for 0% of the time, Pallas kernels for 3%

profile of v6, /device:TPU:8, one launch (start us, length us, event | category | flops | bytes accessed | tf_op | source)
XLA Modules:
  0.0 63.5 jit_solution(13656413819169694341)
XLA Ops:
  0.0 0.0 copy-start
  0.0 0.0 copy-start.1
  0.0 0.0 copy-start.2
  0.0 1.3 %tables.1 = (bf16[2,768,768]{2,1,0:T(8,128)(2,1)S(1)}, f32[4,16,768]{2,1,0:T(8,128)S(1)}, f32[2,48,768]{2,1,0:T(8,128)S(1)}) custom-call(), custom_call_target="tpu_custom_call" | custom-call | flops 1000000000 | bytes 10000000 | tf_op jit(solution)/shard_map/tables/pallas_call | solution.py:72
  1.4 0.0 copy-done
  1.4 0.0 copy-done.1
  1.4 0.0 copy-done.2
  1.4 2.6 %transform.1 = bf16[32,104,128]{2,1,0:T(8,128)(2,1)S(1)} custom-call(bf16[128,3072]{1,0:T(8,128)(2,1)S(1)} %bitcast.5, s32[1,32]{1,0:T(1,128)S(1)} %copy-done.1, s32[1,32]{1,0:T(1,128)S(1)} %copy-done.2, bf16[2,768,768]{2,1,0:T(8,128)(2,1)S(1)} %get-tuple-element.10.even_table_ref, f32[4,16,768]{2,1,0:T(8,128)S(1)} %get-tuple-element.11.base_ref, ...), custom_call_target="tpu_custom_call" | custom-call | flops 1207959552 | bytes 2000000 | tf_op jit(solution)/shard_map/transform/pallas_call | solution.py:196
  3.9 30.9 %all_to_all.10.got_ref = bf16[32,104,128]{2,1,0:T(8,128)(2,1)S(1)} all-to-all(bf16[32,104,128]{2,1,0:T(8,128)(2,1)S(1)} %transform.1), channel_id=1, replica_groups={{248,240,232,224,216,208,200,192,184,176,168,160,152,144,136,128,120,11..., dimensions={0} | all-to-all | bytes 1703936 | tf_op jit(solution)/shard_map/all_to_all | solution.py:432
  34.9 1.2 %cross.3 = f32[512,128]{1,0:T(8,128)S(1)} custom-call(bf16[32,104,128]{2,1,0:T(8,128)(2,1)S(1)} %all_to_all.10.got_ref), custom_call_target="tpu_custom_call" | custom-call | flops 603979776 | bytes 2000000 | tf_op jit(solution)/shard_map/cross/pallas_call | solution.py:275
  36.1 0.1 collective-permute-start
  36.2 1.2 %cross.2 = f32[512,128]{1,0:T(8,128)S(1)} custom-call(bf16[32,104,128]{2,1,0:T(8,128)(2,1)S(1)} %all_to_all.10.got_ref), custom_call_target="tpu_custom_call" | custom-call | flops 603979776 | bytes 2000000 | tf_op jit(solution)/shard_map/cross/pallas_call | solution.py:275
  37.5 0.3 collective-permute-done
  37.8 1.6 %collective-permute-start.1 = (f32[128,128]{1,0:T(8,128)S(1)}, f32[128,128]{1,0:T(8,128)S(1)}, u32[]{:S(2)}, u32[]{:S(2)}) collective-permute-start(f32[128,128]{1,0:T(8,128)S(1)} %get-tuple-element.17), channel_id=1, source_target_pairs={{0,2},{2,4},{4,6},{6,0},{1,3},{3,5},{5,7},{7,1},{8,10},{10,12},{12... | collective-permute-start | bytes 196616 | tf_op jit(solution)/shard_map/ppermute | solution.py:436
  39.4 1.7 %collective-permute-start.2 = (f32[128,128]{1,0:T(8,128)S(1)}, f32[128,128]{1,0:T(8,128)S(1)}, u32[]{:S(2)}, u32[]{:S(2)}) collective-permute-start(f32[128,128]{1,0:T(8,128)S(1)} %get-tuple-element.16), channel_id=1, source_target_pairs={{0,6},{2,0},{4,2},{6,4},{1,7},{3,1},{5,3},{7,5},{8,14},{10,8},{12,... | collective-permute-start | bytes 196616 | tf_op jit(solution)/shard_map/ppermute | solution.py:436
  41.1 1.8 %collective-permute-start.3 = (f32[128,128]{1,0:T(8,128)S(1)}, f32[128,128]{1,0:T(8,128)S(1)}, u32[]{:S(2)}, u32[]{:S(2)}) collective-permute-start(f32[128,128]{1,0:T(8,128)S(1)} %get-tuple-element.15), channel_id=1, source_target_pairs={{0,4},{2,6},{4,0},{6,2},{1,5},{3,7},{5,1},{7,3},{8,12},{10,14},{12... | collective-permute-start | bytes 196616 | tf_op jit(solution)/shard_map/ppermute | solution.py:436
  43.6 1.0 %inverse.1 = (f32[2,1024,128]{2,1,0:T(8,128)S(1)}, bf16[4096,256]{1,0:T(8,128)(2,1)S(1)}) custom-call(s32[1]{0:T(128)S(6)} %copy.5.count_ref, f32[4,128,128]{2,1,0:T(8,128)S(1)} %bitcast.4), custom_call_target="tpu_custom_call" | custom-call | flops 10000000 | bytes 3000000 | tf_op jit(solution)/shard_map/inverse/pallas_call | solution.py:364
  44.6 0.0 collective-permute-done.1.one_ref
  44.6 0.0 collective-permute-done.2.two_ref
  44.6 2.3 %collective-permute-done.3.three_ref = f32[128,128]{1,0:T(8,128)S(1)} collective-permute-done((f32[128,128]{1,0:T(8,128)S(1)}, f32[128,128]{1,0:T(8,128)S(1)}, u32[]{:S(2)}, u32[]{:S(2)}) %collective-permute-start.3) | collective-permute-done | bytes 65568 | tf_op jit(solution)/shard_map/ppermute | solution.py:436
  46.9 15.4 %all_to_all.11 = f32[32,4,128]{2,1,0:T(4,128)S(1)} all-to-all(f32[32,4,128]{2,1,0:T(4,128)S(1)} %bitcast.7), channel_id=1, replica_groups={{248,240,232,224,216,208,200,192,184,176,168,160,152,144,136,128,120,11..., dimensions={0} | all-to-all | bytes 131072 | tf_op jit(solution)/shard_map/all_to_all | solution.py:439
  62.3 1.2 %lags.1 = f32[4,1024]{1,0:T(4,128)} custom-call(f32[128,128]{1,0:T(8,128)S(1)} %bitcast.6, f32[2,1024,128]{2,1,0:T(8,128)S(1)} %get-tuple-element.13.after_ref.turn_ref, bf16[4096,256]{1,0:T(8,128)(2,1)S(1)} %get-tuple-element.14.table_ref), custom_call_target="tpu_custom_call" | custom-call | flops 134217728 | bytes 4000000 | tf_op jit(solution)/shard_map/lags/pallas_call | solution.py:418
  (3 shorter events, 0.1 us)
Async XLA Ops:
  0.0 1.4 %copy-start = (bf16[16,8,3072]{2,1,0:T(8,128)(2,1)S(1)}, bf16[16,8,3072]{2,1,0:T(8,128)(2,1)}, u32[]{:S(2)}) copy-start(bf16[16,8,3072]{2,1,0:T(8,128)(2,1)} %param.4) | copy-start | bytes 2359300
  0.0 1.4 %copy-start.1 = (s32[1,32]{1,0:T(1,128)S(1)}, s32[1,32]{1,0:T(1,128)}, u32[]{:S(2)}) copy-start(s32[1,32]{1,0:T(1,128)} %source_ref.1) | copy-start | bytes 388
  0.0 1.4 %copy-start.2 = (s32[1,32]{1,0:T(1,128)S(1)}, s32[1,32]{1,0:T(1,128)}, u32[]{:S(2)}) copy-start(s32[1,32]{1,0:T(1,128)} %partner_ref.1) | copy-start | bytes 388
  36.1 1.6 %collective-permute-start = (f32[512,128]{1,0:T(8,128)S(1)}, f32[512,128]{1,0:T(8,128)S(1)}, u32[]{:S(2)}, u32[]{:S(2)}) collective-permute-start(f32[512,128]{1,0:T(8,128)S(1)} %cross.3), channel_id=1, source_target_pairs={{0,1},{1,0},{2,3},{3,2},{4,5},{5,4},{6,7},{7,6},{8,9},{9,8},{10,11... | collective-permute-start | bytes 786440 | tf_op jit(solution)/shard_map/ppermute | solution.py:434
  37.8 6.8 %collective-permute-start.1 = (f32[128,128]{1,0:T(8,128)S(1)}, f32[128,128]{1,0:T(8,128)S(1)}, u32[]{:S(2)}, u32[]{:S(2)}) collective-permute-start(f32[128,128]{1,0:T(8,128)S(1)} %get-tuple-element.17), channel_id=1, source_target_pairs={{0,2},{2,4},{4,6},{6,0},{1,3},{3,5},{5,7},{7,1},{8,10},{10,12},{12... | collective-permute-start | bytes 196616 | tf_op jit(solution)/shard_map/ppermute | solution.py:436
  39.4 5.2 %collective-permute-start.2 = (f32[128,128]{1,0:T(8,128)S(1)}, f32[128,128]{1,0:T(8,128)S(1)}, u32[]{:S(2)}, u32[]{:S(2)}) collective-permute-start(f32[128,128]{1,0:T(8,128)S(1)} %get-tuple-element.16), channel_id=1, source_target_pairs={{0,6},{2,0},{4,2},{6,4},{1,7},{3,1},{5,3},{7,5},{8,14},{10,8},{12,... | collective-permute-start | bytes 196616 | tf_op jit(solution)/shard_map/ppermute | solution.py:436
  41.1 5.8 %collective-permute-start.3 = (f32[128,128]{1,0:T(8,128)S(1)}, f32[128,128]{1,0:T(8,128)S(1)}, u32[]{:S(2)}, u32[]{:S(2)}) collective-permute-start(f32[128,128]{1,0:T(8,128)S(1)} %get-tuple-element.15), channel_id=1, source_target_pairs={{0,4},{2,6},{4,0},{6,2},{1,5},{3,7},{5,1},{7,3},{8,12},{10,14},{12... | collective-permute-start | bytes 196616 | tf_op jit(solution)/shard_map/ppermute | solution.py:436

commit v7 on v6

--- a/solution.py
+++ b/solution.py
@@ -1,4 +1,3 @@
-import functools
 import math
 
 import jax
@@ -20,7 +19,7 @@
 PAIRS = 32
 HALF_PAIRS = PAIRS // 2
 DATA = 6 * CHANS
-PIECE = DATA + 8
+PIECE = DATA + 2
 MB = 1024 * 1024
 
 
@@ -172,7 +171,8 @@
                 slabs = mixed
             at = CHANS * (2 * (t % 3) + part)
             for s in range(8):
-                out_ref[SLOT[8 * (t // 3) + s], at:at + CHANS, :] = slabs[s]
+                row = PIECE * SLOT[8 * (t // 3) + s] + at
+                out_ref[row:row + CHANS, :] = slabs[s]
 
     partner = partner_ref[...]
     list_ref[...] = jnp.zeros((8, 128), jnp.float32)
@@ -186,16 +186,17 @@
         at, to = 4 * quad, 16 * (quad % 2) + 4 * (quad // 2)
         moved = pltpu.roll(plain, (to - at) % 128, 1)
         lists = jnp.where((lane >= to) & (lane < to + 4), moved, lists)
-    lists = lists.astype(jnp.bfloat16)
+    sources = pltpu.roll(pltpu.roll(lists, 6, 0), 64, 1)
+    lists = jnp.where((iota((8, 128), 0) == 0) & (lane >= 64), sources, lists).astype(jnp.bfloat16)
     for c in range(BLOCKS):
-        out_ref[c, DATA:PIECE, :] = lists
+        out_ref[PIECE * c + DATA:PIECE * (c + 1), :] = lists[:2]
 
 
 def transform(x, source, partner, table):
     vmem = pl.BlockSpec(memory_space=pltpu.VMEM)
     return pl.pallas_call(
         transform_kernel,
-        out_shape=jax.ShapeDtypeStruct((BLOCKS, PIECE, 128), jnp.bfloat16),
+        out_shape=jax.ShapeDtypeStruct((BLOCKS * PIECE, 128), jnp.bfloat16),
         in_specs=[vmem] * 6,
         out_specs=vmem,
         scratch_shapes=[
@@ -212,18 +213,28 @@
     )(x, source, partner, *table)
 
 
-def cross_kernel(away, got_ref, out_ref, data_ref, near_ref, far_ref, list_ref):
+def away_kernel(got_ref, out_ref, data_ref, list_ref, near_ref, far_ref):
     for o in range(BLOCKS):
         for q in range(6):
             rows = slice(CHANS * o, CHANS * (o + 1))
-            data_ref[rows, 128 * q:128 * q + 128] = got_ref[SLOT[o], CHANS * q:CHANS * (q + 1), :]
-    lists = got_ref[:, DATA:PIECE, :].astype(jnp.float32)
+            row = PIECE * SLOT[o] + CHANS * q
+            data_ref[rows, 128 * q:128 * q + 128] = got_ref[row:row + CHANS, :]
     list_ref[...] = jnp.zeros((2, 128, 128), jnp.float32)
-    list_ref[0, 0:BLOCKS, :] = lists[:, 0, :] * CHANS + lists[:, 1, :]
-    list_ref[1, 0:BLOCKS, :] = lists[:, 2, :]
+    for k in range(BLOCKS):
+        lists = got_ref[PIECE * k + DATA:PIECE * (k + 1), :].astype(jnp.float32)
+        list_ref[0, k:k + 1, :] = lists[0:1] * CHANS + lists[1:2]
+        list_ref[1, k:k + 1, :] = pltpu.roll(lists[0:1], 64, 1)
     partner = jnp.transpose(list_ref[0])
     source = jnp.transpose(list_ref[1])
     list_ref[0], list_ref[1] = partner, source
+    cross_pairs(1, data_ref, list_ref, out_ref, near_ref, far_ref)
+
+
+def keep_kernel(data_ref, list_ref, out_ref, near_ref, far_ref):
+    cross_pairs(0, data_ref, list_ref, out_ref, near_ref, far_ref)
+
+
+def cross_pairs(away, data_ref, list_ref, out_ref, near_ref, far_ref):
     core = (lax.axis_index("core") + away) % 2
     pick = pl.ds(pl.multiple_of(HALF_PAIRS * core, HALF_PAIRS), HALF_PAIRS)
     partner, source = list_ref[0, pick, :], list_ref[1, pick, :]
@@ -269,24 +280,26 @@
                     out_ref[pl.ds(pl.multiple_of(to, 8), 8), :] = tile
 
 
-def cross(got, away):
+def cross(kernel, *arrays):
     vmem = pl.BlockSpec(memory_space=pltpu.VMEM)
     pairs = BLOCKS * HALF_PAIRS
-    return pl.pallas_call(
-        functools.partial(cross_kernel, away),
-        out_shape=jax.ShapeDtypeStruct((pairs, 128), jnp.float32),
-        in_specs=[vmem],
-        out_specs=vmem,
+    shapes = [jax.ShapeDtypeStruct((pairs, 128), jnp.float32)]
+    if len(arrays) == 1:
+        shapes.append(jax.ShapeDtypeStruct((BLOCKS * CHANS, 6 * 128), jnp.bfloat16))
+        shapes.append(jax.ShapeDtypeStruct((2, 128, 128), jnp.float32))
+    return pl.pallas_call(
+        kernel,
+        out_shape=shapes,
+        in_specs=[vmem] * len(arrays),
+        out_specs=[vmem] * len(shapes),
         scratch_shapes=[
-            pltpu.VMEM((BLOCKS * CHANS, 6 * 128), jnp.bfloat16),
             pltpu.VMEM((pairs, 256), jnp.bfloat16),
             pltpu.VMEM((pairs, BLOCKS * CHANS), jnp.bfloat16),
-            pltpu.VMEM((2, 128, 128), jnp.float32),
         ],
         compiler_params=pltpu.CompilerParams(vmem_limit_bytes=16 * MB),
         cost_estimate=pl.CostEstimate(flops=2 * pairs * 768 * 768, bytes_accessed=2 * 10**6, transcendentals=0),
         name="cross",
-    )(got)
+    )(*arrays)
 
 
 def bin_of(block, lane):
@@ -429,11 +442,13 @@
 
 def shards(records, pair_source, pair_partner, pair_count):
     sent = transform(records.reshape(ROWS, N), pair_source, pair_partner, tables())
-    got = lax.all_to_all(sent, "chan", 0, 0, axis_index_groups=[ORDER])
-    away = cross(got, 1)
+    rows = BLOCKS * PIECE
+    got = lax.all_to_all(sent.reshape(rows // 2, 2, 128), "chan", 0, 0, tiled=True, axis_index_groups=[ORDER])
+    got = got.reshape(rows, 128)
+    away, data, lists = cross(away_kernel, got)
     near = lax.ppermute(away, "core", [(0, 1), (1, 0)])
-    spectra = (cross(got, 0) + near).reshape(4, 4 * BLOCKS, 128)
-    parts = [lax.ppermute(spectra[k], "x", [(x, (x + k) % 4) for x in range(4)]) for k in (1, 3, 2)]
+    spectra = (cross(keep_kernel, data, lists)[0] + near).reshape(4, 4 * BLOCKS, 128)
+    parts = [lax.ppermute(spectra[k], "x", [(x, (x + k) % 4) for x in range(4)]) for k in (2, 3, 1)]
     turn, table = inverse(pair_count, spectra)
     total = add_parts(spectra[0], parts, turn)
     last = lax.all_to_all(total.reshape(BLOCKS, 4, 128), "chan", 0, 0, axis_index_groups=[ORDER])

time: 63.9 us -> 63.1 us (0.987)
  blocking collectives: 46.4 us -> 45.3 us
    all_to_all x1, blocking collectives: 30.9 us -> 29.9 us  [shards(): lax.all_to_all(sent.reshape(rows // 2, 2, 128), 'chan', 0, 0, tiled=True,...]
where the time goes in v7:
time: 63.1 us; the launch traced here: 62.6 us
  blocking collectives  45.3 us (72%)
  Pallas kernels  8.57 us (14%)
  starting transfers between devices  5.22 us (8%)
  waiting for transfers between devices  2.73 us (4%)
  between operations  0.76 us (1%)
    all_to_all x1, blocking collectives, shards(): lax.all_to_all(sent.reshape(rows // 2, 2, 128), 'chan', 0, 0, tiled=True,...  29.9 us
    all_to_all x1, blocking collectives, shards(): lax.all_to_all(total.reshape(BLOCKS, 4, 128), 'chan', 0, 0, axis_index_gr...  15.3 us
    ppermute x3, starting transfers between devices, shards(): lax.ppermute(spectra[k], 'x', [(x, (x + k) % 4) for x in range(4)])  5.13 us
    pallas_call x1, Pallas kernels, transform(): pl.pallas_call(transform_kernel, out_shape=jax.ShapeDtypeStruct((BLOCKS *...  2.55 us
    pallas_call x2, Pallas kernels, cross(): pl.pallas_call(kernel, out_shape=shapes, in_specs=[vmem] * len(arrays), o...  2.52 us
    ppermute x3, waiting for transfers between devices, shards(): lax.ppermute(spectra[k], 'x', [(x, (x + k) % 4) for x in range(4)])  2.3 us
    pallas_call x1, Pallas kernels, tables(): pl.pallas_call(tables_kernel, out_shape=(jax.ShapeDtypeStruct((2, QUARTER...  1.34 us
  transfers between devices with their start and end apart: 4, of which 2 were waited for; matrix products, arithmetic and copies ran while one was open for 0% of the time, Pallas kernels for 3%

profile of v7, /device:TPU:8, one launch (start us, length us, event | category | flops | bytes accessed | tf_op | source)
XLA Modules:
  0.0 62.6 jit_solution(4504530375664530990)
XLA Ops:
  0.0 0.0 copy-start.2
  0.0 0.0 copy-start.1
  0.0 0.0 copy-start
  0.0 1.3 %tables.1 = (bf16[2,768,768]{2,1,0:T(8,128)(2,1)S(1)}, f32[4,16,768]{2,1,0:T(8,128)S(1)}, f32[2,48,768]{2,1,0:T(8,128)S(1)}) custom-call(), custom_call_target="tpu_custom_call" | custom-call | flops 1000000000 | bytes 10000000 | tf_op jit(solution)/shard_map/tables/pallas_call | solution.py:71
  1.4 0.0 copy-done.2
  1.4 0.0 copy-done.1
  1.4 0.0 copy-done
  1.4 2.6 %transform.1 = bf16[3136,128]{1,0:T(8,128)(2,1)S(1)} custom-call(bf16[128,3072]{1,0:T(8,128)(2,1)S(1)} %bitcast.11, s32[1,32]{1,0:T(1,128)S(1)} %copy-done.1, s32[1,32]{1,0:T(1,128)S(1)} %copy-done.2, bf16[2,768,768]{2,1,0:T(8,128)(2,1)S(1)} %get-tuple-element.13.even_table_ref, f32[4,16,768]{2,1,0:T(8,128)S(1)} %get-tuple-element.14.base_ref, ...), custom_call_target="tpu_custom_call" | custom-call | flops 1207959552 | bytes 2000000 | tf_op jit(solution)/shard_map/transform/pallas_call | solution.py:197
  3.9 29.9 %all_to_all.10 = bf16[1568,2,128]{2,1,0:T(2,128)(2,1)S(1)} all-to-all(bf16[1568,2,128]{2,1,0:T(2,128)(2,1)S(1)} %bitcast.8), channel_id=1, replica_groups={{248,240,232,224,216,208,200,192,184,176,168,160,152,144,136,128,120,11..., dimensions={0} | all-to-all | bytes 1605632 | tf_op jit(solution)/shard_map/all_to_all | solution.py:446
  33.9 1.4 %cross.2 = (f32[512,128]{1,0:T(8,128)S(1)}, bf16[512,768]{1,0:T(8,128)(2,1)S(1)}, f32[2,128,128]{2,1,0:T(8,128)S(1)}) custom-call(bf16[3136,128]{1,0:T(8,128)(2,1)S(1)} %bitcast.7), custom_call_target="tpu_custom_call" | custom-call | flops 603979776 | bytes 2000000 | tf_op jit(solution)/shard_map/cross/pallas_call | solution.py:290
  35.3 0.1 collective-permute-start
  35.4 1.1 %cross.3 = f32[512,128]{1,0:T(8,128)S(1)} custom-call(bf16[512,768]{1,0:T(8,128)(2,1)S(1)} %get-tuple-element.16.data_ref, f32[2,128,128]{2,1,0:T(8,128)S(1)} %get-tuple-element.17.list_ref), custom_call_target="tpu_custom_call" | custom-call | flops 603979776 | bytes 2000000 | tf_op jit(solution)/shard_map/cross/pallas_call | solution.py:290
  36.5 0.4 collective-permute-done
  37.0 1.6 %collective-permute-start.3 = (f32[128,128]{1,0:T(8,128)S(1)}, f32[128,128]{1,0:T(8,128)S(1)}, u32[]{:S(2)}, u32[]{:S(2)}) collective-permute-start(f32[128,128]{1,0:T(8,128)S(1)} %get-tuple-element.21), channel_id=1, source_target_pairs={{0,2},{2,4},{4,6},{6,0},{1,3},{3,5},{5,7},{7,1},{8,10},{10,12},{12... | collective-permute-start | bytes 196616 | tf_op jit(solution)/shard_map/ppermute | solution.py:451
  38.6 1.8 %collective-permute-start.2 = (f32[128,128]{1,0:T(8,128)S(1)}, f32[128,128]{1,0:T(8,128)S(1)}, u32[]{:S(2)}, u32[]{:S(2)}) collective-permute-start(f32[128,128]{1,0:T(8,128)S(1)} %get-tuple-element.22), channel_id=1, source_target_pairs={{0,6},{2,0},{4,2},{6,4},{1,7},{3,1},{5,3},{7,5},{8,14},{10,8},{12,... | collective-permute-start | bytes 196616 | tf_op jit(solution)/shard_map/ppermute | solution.py:451
  40.3 1.8 %collective-permute-start.1 = (f32[128,128]{1,0:T(8,128)S(1)}, f32[128,128]{1,0:T(8,128)S(1)}, u32[]{:S(2)}, u32[]{:S(2)}) collective-permute-start(f32[128,128]{1,0:T(8,128)S(1)} %get-tuple-element.23), channel_id=1, source_target_pairs={{0,4},{2,6},{4,0},{6,2},{1,5},{3,7},{5,1},{7,3},{8,12},{10,14},{12... | collective-permute-start | bytes 196616 | tf_op jit(solution)/shard_map/ppermute | solution.py:451
  42.8 1.0 %inverse.1 = (f32[2,1024,128]{2,1,0:T(8,128)S(1)}, bf16[4096,256]{1,0:T(8,128)(2,1)S(1)}) custom-call(s32[1]{0:T(128)S(6)} %copy.5.count_ref, f32[4,128,128]{2,1,0:T(8,128)S(1)} %bitcast.6), custom_call_target="tpu_custom_call" | custom-call | flops 10000000 | bytes 3000000 | tf_op jit(solution)/shard_map/inverse/pallas_call | solution.py:377
  43.8 0.0 collective-permute-done.3.three_ref
  43.8 0.0 collective-permute-done.2.two_ref
  43.8 2.3 %collective-permute-done.1.one_ref = f32[128,128]{1,0:T(8,128)S(1)} collective-permute-done((f32[128,128]{1,0:T(8,128)S(1)}, f32[128,128]{1,0:T(8,128)S(1)}, u32[]{:S(2)}, u32[]{:S(2)}) %collective-permute-start.1) | collective-permute-done | bytes 65568 | tf_op jit(solution)/shard_map/ppermute | solution.py:451
  46.1 15.3 %all_to_all.11 = f32[32,4,128]{2,1,0:T(4,128)S(1)} all-to-all(f32[32,4,128]{2,1,0:T(4,128)S(1)} %bitcast.10), channel_id=1, replica_groups={{248,240,232,224,216,208,200,192,184,176,168,160,152,144,136,128,120,11..., dimensions={0} | all-to-all | bytes 131072 | tf_op jit(solution)/shard_map/all_to_all | solution.py:454
  61.5 1.2 %lags.1 = f32[4,1024]{1,0:T(4,128)} custom-call(f32[128,128]{1,0:T(8,128)S(1)} %bitcast.9, f32[2,1024,128]{2,1,0:T(8,128)S(1)} %get-tuple-element.19.after_ref.turn_ref, bf16[4096,256]{1,0:T(8,128)(2,1)S(1)} %get-tuple-element.20.table_ref), custom_call_target="tpu_custom_call" | custom-call | flops 134217728 | bytes 4000000 | tf_op jit(solution)/shard_map/lags/pallas_call | solution.py:431
  (3 shorter events, 0.1 us)
Async XLA Ops:
  0.0 1.4 %copy-start.2 = (s32[1,32]{1,0:T(1,128)S(1)}, s32[1,32]{1,0:T(1,128)}, u32[]{:S(2)}) copy-start(s32[1,32]{1,0:T(1,128)} %partner_ref.1) | copy-start | bytes 388
  0.0 1.4 %copy-start.1 = (s32[1,32]{1,0:T(1,128)S(1)}, s32[1,32]{1,0:T(1,128)}, u32[]{:S(2)}) copy-start(s32[1,32]{1,0:T(1,128)} %source_ref.1) | copy-start | bytes 388
  0.0 1.4 %copy-start = (bf16[16,8,3072]{2,1,0:T(8,128)(2,1)S(1)}, bf16[16,8,3072]{2,1,0:T(8,128)(2,1)}, u32[]{:S(2)}) copy-start(bf16[16,8,3072]{2,1,0:T(8,128)(2,1)} %param.4) | copy-start | bytes 2359300
  35.3 1.6 %collective-permute-start = (f32[512,128]{1,0:T(8,128)S(1)}, f32[512,128]{1,0:T(8,128)S(1)}, u32[]{:S(2)}, u32[]{:S(2)}) collective-permute-start(f32[512,128]{1,0:T(8,128)S(1)} %get-tuple-element.18), channel_id=1, source_target_pairs={{0,1},{1,0},{2,3},{3,2},{4,5},{5,4},{6,7},{7,6},{8,9},{9,8},{10,11... | collective-permute-start | bytes 786440 | tf_op jit(solution)/shard_map/ppermute | solution.py:449
  37.0 6.8 %collective-permute-start.3 = (f32[128,128]{1,0:T(8,128)S(1)}, f32[128,128]{1,0:T(8,128)S(1)}, u32[]{:S(2)}, u32[]{:S(2)}) collective-permute-start(f32[128,128]{1,0:T(8,128)S(1)} %get-tuple-element.21), channel_id=1, source_target_pairs={{0,2},{2,4},{4,6},{6,0},{1,3},{3,5},{5,7},{7,1},{8,10},{10,12},{12... | collective-permute-start | bytes 196616 | tf_op jit(solution)/shard_map/ppermute | solution.py:451
  38.6 5.2 %collective-permute-start.2 = (f32[128,128]{1,0:T(8,128)S(1)}, f32[128,128]{1,0:T(8,128)S(1)}, u32[]{:S(2)}, u32[]{:S(2)}) collective-permute-start(f32[128,128]{1,0:T(8,128)S(1)} %get-tuple-element.22), channel_id=1, source_target_pairs={{0,6},{2,0},{4,2},{6,4},{1,7},{3,1},{5,3},{7,5},{8,14},{10,8},{12,... | collective-permute-start | bytes 196616 | tf_op jit(solution)/shard_map/ppermute | solution.py:451
  40.3 5.8 %collective-permute-start.1 = (f32[128,128]{1,0:T(8,128)S(1)}, f32[128,128]{1,0:T(8,128)S(1)}, u32[]{:S(2)}, u32[]{:S(2)}) collective-permute-start(f32[128,128]{1,0:T(8,128)S(1)} %get-tuple-element.23), channel_id=1, source_target_pairs={{0,4},{2,6},{4,0},{6,2},{1,5},{3,7},{5,1},{7,3},{8,12},{10,14},{12... | collective-permute-start | bytes 196616 | tf_op jit(solution)/shard_map/ppermute | solution.py:451

commit v8 on v7

--- a/solution.py
+++ b/solution.py
@@ -18,6 +18,7 @@
 BLOCKS = 32
 PAIRS = 32
 HALF_PAIRS = PAIRS // 2
+DENSE = 96
 DATA = 6 * CHANS
 PIECE = DATA + 2
 MB = 1024 * 1024
@@ -241,6 +242,7 @@
     channel = iota((HALF_PAIRS, BLOCKS * CHANS), 1).astype(jnp.float32)
     size = 256
     lane = iota((size, 128), 1)
+    held = {}
     for m in range(2):
         for o in range(16 * m, 16 * m + 16):
             at = SLOT[o]
@@ -276,14 +278,20 @@
                     (2 * pair, jnp.where(low, one, pltpu.roll(two, 4, 0))),
                     (2 * pair + 1, jnp.where(low, pltpu.roll(one, 4, 0), two)),
                 ):
-                    to = 4 * BLOCKS * ((x + 4 - lax.axis_index("x")) % 4) + 4 * min(slots)
+                    at = 4 * min(slots)
+                    if at >= DENSE:
+                        held[x, at - DENSE] = tile
+                        continue
+                    filler = pltpu.roll(held[x, at % 32], (48, 16, 32)[at // 32], 1)
+                    tile = jnp.where(iota((8, 128), 1) // 16 % 4 == 3, filler, tile)
+                    to = DENSE * ((x + 4 - lax.axis_index("x")) % 4) + at
                     out_ref[pl.ds(pl.multiple_of(to, 8), 8), :] = tile
 
 
 def cross(kernel, *arrays):
     vmem = pl.BlockSpec(memory_space=pltpu.VMEM)
     pairs = BLOCKS * HALF_PAIRS
-    shapes = [jax.ShapeDtypeStruct((pairs, 128), jnp.float32)]
+    shapes = [jax.ShapeDtypeStruct((4 * DENSE, 128), jnp.float32)]
     if len(arrays) == 1:
         shapes.append(jax.ShapeDtypeStruct((BLOCKS * CHANS, 6 * 128), jnp.bfloat16))
         shapes.append(jax.ShapeDtypeStruct((2, 128, 128), jnp.float32))
@@ -390,14 +398,19 @@
 
 
 def total_kernel(own_ref, one_ref, two_ref, three_ref, after_ref, out_ref):
-    out_ref[...] = own_ref[...] + one_ref[...] + two_ref[...] + three_ref[...]
+    total = own_ref[...] + one_ref[...] + two_ref[...] + three_ref[...]
+    out_ref[0:DENSE, :] = total
+    group = iota((32, 128), 1) // 16 % 4
+    first, second, third = (pltpu.roll(total[32 * t:32 * t + 32], 128 - (48, 16, 32)[t], 1) for t in range(3))
+    rest = jnp.where(group == 0, first, jnp.where(group == 2, second, third))
+    out_ref[DENSE:, :] = jnp.where(group == 3, 0.0, rest)
 
 
 def add_parts(own, parts, after):
     vmem = pl.BlockSpec(memory_space=pltpu.VMEM)
     return pl.pallas_call(
         total_kernel,
-        out_shape=jax.ShapeDtypeStruct(own.shape, jnp.float32),
+        out_shape=jax.ShapeDtypeStruct((4 * BLOCKS, 128), jnp.float32),
         in_specs=[vmem] * 4 + [pl.BlockSpec(memory_space=pl.ANY)],
         out_specs=vmem,
         compiler_params=pltpu.CompilerParams(vmem_limit_bytes=4 * MB),
@@ -447,7 +460,7 @@
     got = got.reshape(rows, 128)
     away, data, lists = cross(away_kernel, got)
     near = lax.ppermute(away, "core", [(0, 1), (1, 0)])
-    spectra = (cross(keep_kernel, data, lists)[0] + near).reshape(4, 4 * BLOCKS, 128)
+    spectra = (cross(keep_kernel, data, lists)[0] + near).reshape(4, DENSE, 128)
     parts = [lax.ppermute(spectra[k], "x", [(x, (x + k) % 4) for x in range(4)]) for k in (2, 3, 1)]
     turn, table = inverse(pair_count, spectra)
     total = add_parts(spectra[0], parts, turn)

time: 63.1 us -> 63.5 us (level)
  transfers between devices with their start and end apart: 4 -> 4, of which waited for: 2 -> 3; matrix products, arithmetic and copies ran while one was open for 0% -> 0% of each run, Pallas kernels for 3% -> 3%
where the time goes in v8:
time: 63.5 us; the launch traced here: 63.1 us
  blocking collectives  45.3 us (71%)
  Pallas kernels  8.7 us (14%)
  starting transfers between devices  5.23 us (8%)
  waiting for transfers between devices  3.08 us (5%)
  between operations  0.75 us (1%)
    all_to_all x1, blocking collectives, shards(): lax.all_to_all(sent.reshape(rows // 2, 2, 128), 'chan', 0, 0, tiled=True,...  29.9 us
    all_to_all x1, blocking collectives, shards(): lax.all_to_all(total.reshape(BLOCKS, 4, 128), 'chan', 0, 0, axis_index_gr...  15.3 us
    ppermute x3, starting transfers between devices, shards(): lax.ppermute(spectra[k], 'x', [(x, (x + k) % 4) for x in range(4)])  5.14 us
    ppermute x3, waiting for transfers between devices, shards(): lax.ppermute(spectra[k], 'x', [(x, (x + k) % 4) for x in range(4)])  2.76 us
    pallas_call x2, Pallas kernels, cross(): pl.pallas_call(kernel, out_shape=shapes, in_specs=[vmem] * len(arrays), o...  2.59 us
    pallas_call x1, Pallas kernels, transform(): pl.pallas_call(transform_kernel, out_shape=jax.ShapeDtypeStruct((BLOCKS *...  2.55 us
    pallas_call x1, Pallas kernels, tables(): pl.pallas_call(tables_kernel, out_shape=(jax.ShapeDtypeStruct((2, QUARTER...  1.34 us
  transfers between devices with their start and end apart: 4, of which 3 were waited for; matrix products, arithmetic and copies ran while one was open for 0% of the time, Pallas kernels for 3%

profile of v8, /device:TPU:8, one launch (start us, length us, event | category | flops | bytes accessed | tf_op | source)
XLA Modules:
  0.0 63.1 jit_solution(14119093602300604934)
XLA Ops:
  0.0 0.0 copy-start
  0.0 0.0 copy-start.1
  0.0 0.0 copy-start.2
  0.0 1.3 %tables.1 = (bf16[2,768,768]{2,1,0:T(8,128)(2,1)S(1)}, f32[4,16,768]{2,1,0:T(8,128)S(1)}, f32[2,48,768]{2,1,0:T(8,128)S(1)}) custom-call(), custom_call_target="tpu_custom_call" | custom-call | flops 1000000000 | bytes 10000000 | tf_op jit(solution)/shard_map/tables/pallas_call | solution.py:72
  1.4 0.0 copy-done
  1.4 0.0 copy-done.1
  1.4 0.0 copy-done.2
  1.4 2.6 %transform.1 = bf16[3136,128]{1,0:T(8,128)(2,1)S(1)} custom-call(bf16[128,3072]{1,0:T(8,128)(2,1)S(1)} %bitcast.11, s32[1,32]{1,0:T(1,128)S(1)} %copy-done.1, s32[1,32]{1,0:T(1,128)S(1)} %copy-done.2, bf16[2,768,768]{2,1,0:T(8,128)(2,1)S(1)} %get-tuple-element.13.even_table_ref, f32[4,16,768]{2,1,0:T(8,128)S(1)} %get-tuple-element.14.base_ref, ...), custom_call_target="tpu_custom_call" | custom-call | flops 1207959552 | bytes 2000000 | tf_op jit(solution)/shard_map/transform/pallas_call | solution.py:198
  3.9 29.9 %all_to_all.10 = bf16[1568,2,128]{2,1,0:T(2,128)(2,1)S(1)} all-to-all(bf16[1568,2,128]{2,1,0:T(2,128)(2,1)S(1)} %bitcast.8), channel_id=1, replica_groups={{248,240,232,224,216,208,200,192,184,176,168,160,152,144,136,128,120,11..., dimensions={0} | all-to-all | bytes 1605632 | tf_op jit(solution)/shard_map/all_to_all | solution.py:459
  33.9 1.5 %cross.2 = (f32[384,128]{1,0:T(8,128)S(1)}, bf16[512,768]{1,0:T(8,128)(2,1)S(1)}, f32[2,128,128]{2,1,0:T(8,128)S(1)}) custom-call(bf16[3136,128]{1,0:T(8,128)(2,1)S(1)} %bitcast.7), custom_call_target="tpu_custom_call" | custom-call | flops 603979776 | bytes 2000000 | tf_op jit(solution)/shard_map/cross/pallas_call | solution.py:298
  35.4 0.1 collective-permute-start
  35.5 1.1 %cross.3 = f32[384,128]{1,0:T(8,128)S(1)} custom-call(bf16[512,768]{1,0:T(8,128)(2,1)S(1)} %get-tuple-element.16.data_ref, f32[2,128,128]{2,1,0:T(8,128)S(1)} %get-tuple-element.17.list_ref), custom_call_target="tpu_custom_call" | custom-call | flops 603979776 | bytes 2000000 | tf_op jit(solution)/shard_map/cross/pallas_call | solution.py:298
  36.6 0.3 collective-permute-done
  37.0 3.1 %collective-permute-start.1 = (f32[96,128]{1,0:T(8,128)S(1)}, f32[96,128]{1,0:T(8,128)S(1)}, u32[]{:S(2)}, u32[]{:S(2)}) collective-permute-start(f32[96,128]{1,0:T(8,128)S(1)} %get-tuple-element.23), channel_id=1, source_target_pairs={{0,4},{2,6},{4,0},{6,2},{1,5},{3,7},{5,1},{7,3},{8,12},{10,14},{12... | collective-permute-start | bytes 147464 | tf_op jit(solution)/shard_map/ppermute | solution.py:464
  40.1 1.1 %collective-permute-start.2 = (f32[96,128]{1,0:T(8,128)S(1)}, f32[96,128]{1,0:T(8,128)S(1)}, u32[]{:S(2)}, u32[]{:S(2)}) collective-permute-start(f32[96,128]{1,0:T(8,128)S(1)} %get-tuple-element.22), channel_id=1, source_target_pairs={{0,6},{2,0},{4,2},{6,4},{1,7},{3,1},{5,3},{7,5},{8,14},{10,8},{12,... | collective-permute-start | bytes 147464 | tf_op jit(solution)/shard_map/ppermute | solution.py:464
  41.2 0.9 %collective-permute-start.3 = (f32[96,128]{1,0:T(8,128)S(1)}, f32[96,128]{1,0:T(8,128)S(1)}, u32[]{:S(2)}, u32[]{:S(2)}) collective-permute-start(f32[96,128]{1,0:T(8,128)S(1)} %get-tuple-element.21), channel_id=1, source_target_pairs={{0,2},{2,4},{4,6},{6,0},{1,3},{3,5},{5,7},{7,1},{8,10},{10,12},{12... | collective-permute-start | bytes 147464 | tf_op jit(solution)/shard_map/ppermute | solution.py:464
  42.8 1.0 %inverse.1 = (f32[2,1024,128]{2,1,0:T(8,128)S(1)}, bf16[4096,256]{1,0:T(8,128)(2,1)S(1)}) custom-call(s32[1]{0:T(128)S(6)} %copy.5.count_ref, f32[4,96,128]{2,1,0:T(8,128)S(1)} %bitcast.6), custom_call_target="tpu_custom_call" | custom-call | flops 10000000 | bytes 3000000 | tf_op jit(solution)/shard_map/inverse/pallas_call | solution.py:385
  43.7 0.0 collective-permute-done.1.one_ref
  43.8 0.4 collective-permute-done.2.two_ref
  44.2 2.3 %collective-permute-done.3.three_ref = f32[96,128]{1,0:T(8,128)S(1)} collective-permute-done((f32[96,128]{1,0:T(8,128)S(1)}, f32[96,128]{1,0:T(8,128)S(1)}, u32[]{:S(2)}, u32[]{:S(2)}) %collective-permute-start.3) | collective-permute-done | bytes 49184 | tf_op jit(solution)/shard_map/ppermute | solution.py:464
  46.5 0.1 total.1
  46.6 15.3 %all_to_all.11 = f32[32,4,128]{2,1,0:T(4,128)S(1)} all-to-all(f32[32,4,128]{2,1,0:T(4,128)S(1)} %bitcast.9), channel_id=1, replica_groups={{248,240,232,224,216,208,200,192,184,176,168,160,152,144,136,128,120,11..., dimensions={0} | all-to-all | bytes 131072 | tf_op jit(solution)/shard_map/all_to_all | solution.py:467
  61.9 1.2 %lags.1 = f32[4,1024]{1,0:T(4,128)} custom-call(f32[128,128]{1,0:T(8,128)S(1)} %bitcast.10, f32[2,1024,128]{2,1,0:T(8,128)S(1)} %get-tuple-element.19.after_ref.turn_ref, bf16[4096,256]{1,0:T(8,128)(2,1)S(1)} %get-tuple-element.20.table_ref), custom_call_target="tpu_custom_call" | custom-call | flops 134217728 | bytes 4000000 | tf_op jit(solution)/shard_map/lags/pallas_call | solution.py:444
  (2 shorter events, 0.0 us)
Async XLA Ops:
  0.0 1.4 %copy-start = (bf16[16,8,3072]{2,1,0:T(8,128)(2,1)S(1)}, bf16[16,8,3072]{2,1,0:T(8,128)(2,1)}, u32[]{:S(2)}) copy-start(bf16[16,8,3072]{2,1,0:T(8,128)(2,1)} %param.4) | copy-start | bytes 2359300
  0.0 1.4 %copy-start.1 = (s32[1,32]{1,0:T(1,128)S(1)}, s32[1,32]{1,0:T(1,128)}, u32[]{:S(2)}) copy-start(s32[1,32]{1,0:T(1,128)} %source_ref.1) | copy-start | bytes 388
  0.0 1.4 %copy-start.2 = (s32[1,32]{1,0:T(1,128)S(1)}, s32[1,32]{1,0:T(1,128)}, u32[]{:S(2)}) copy-start(s32[1,32]{1,0:T(1,128)} %partner_ref.1) | copy-start | bytes 388
  35.4 1.5 %collective-permute-start = (f32[384,128]{1,0:T(8,128)S(1)}, f32[384,128]{1,0:T(8,128)S(1)}, u32[]{:S(2)}, u32[]{:S(2)}) collective-permute-start(f32[384,128]{1,0:T(8,128)S(1)} %get-tuple-element.18), channel_id=1, source_target_pairs={{0,1},{1,0},{2,3},{3,2},{4,5},{5,4},{6,7},{7,6},{8,9},{9,8},{10,11... | collective-permute-start | bytes 589832 | tf_op jit(solution)/shard_map/ppermute | solution.py:462
  37.0 6.8 %collective-permute-start.1 = (f32[96,128]{1,0:T(8,128)S(1)}, f32[96,128]{1,0:T(8,128)S(1)}, u32[]{:S(2)}, u32[]{:S(2)}) collective-permute-start(f32[96,128]{1,0:T(8,128)S(1)} %get-tuple-element.23), channel_id=1, source_target_pairs={{0,4},{2,6},{4,0},{6,2},{1,5},{3,7},{5,1},{7,3},{8,12},{10,14},{12... | collective-permute-start | bytes 147464 | tf_op jit(solution)/shard_map/ppermute | solution.py:464
  40.1 4.1 %collective-permute-start.2 = (f32[96,128]{1,0:T(8,128)S(1)}, f32[96,128]{1,0:T(8,128)S(1)}, u32[]{:S(2)}, u32[]{:S(2)}) collective-permute-start(f32[96,128]{1,0:T(8,128)S(1)} %get-tuple-element.22), channel_id=1, source_target_pairs={{0,6},{2,0},{4,2},{6,4},{1,7},{3,1},{5,3},{7,5},{8,14},{10,8},{12,... | collective-permute-start | bytes 147464 | tf_op jit(solution)/shard_map/ppermute | solution.py:464
  41.2 5.3 %collective-permute-start.3 = (f32[96,128]{1,0:T(8,128)S(1)}, f32[96,128]{1,0:T(8,128)S(1)}, u32[]{:S(2)}, u32[]{:S(2)}) collective-permute-start(f32[96,128]{1,0:T(8,128)S(1)} %get-tuple-element.21), channel_id=1, source_target_pairs={{0,2},{2,4},{4,6},{6,0},{1,3},{3,5},{5,7},{7,1},{8,10},{10,12},{12... | collective-permute-start | bytes 147464 | tf_op jit(solution)/shard_map/ppermute | solution.py:464

commit v9 on v8

--- a/solution.py
+++ b/solution.py
@@ -461,7 +461,7 @@
     away, data, lists = cross(away_kernel, got)
     near = lax.ppermute(away, "core", [(0, 1), (1, 0)])
     spectra = (cross(keep_kernel, data, lists)[0] + near).reshape(4, DENSE, 128)
-    parts = [lax.ppermute(spectra[k], "x", [(x, (x + k) % 4) for x in range(4)]) for k in (2, 3, 1)]
+    parts = [lax.ppermute(spectra[k], "x", [(x, (x + k) % 4) for x in range(4)]) for k in (1, 3, 2)]
     turn, table = inverse(pair_count, spectra)
     total = add_parts(spectra[0], parts, turn)
     last = lax.all_to_all(total.reshape(BLOCKS, 4, 128), "chan", 0, 0, axis_index_groups=[ORDER])

time: 63.5 us -> 62.9 us (level)
  waiting for transfers between devices: 3.08 us -> 2.44 us
    ppermute x3, waiting for transfers between devices: 2.76 us -> 2.12 us  [shards(): lax.ppermute(spectra[k], 'x', [(x, (x + k) % 4) for x in range(4)])]
  transfers between devices with their start and end apart: 4 -> 4, of which waited for: 3 -> 2; matrix products, arithmetic and copies ran while one was open for 0% -> 0% of each run, Pallas kernels for 3% -> 3%
where the time goes in v9:
time: 62.9 us; the launch traced here: 62.4 us
  blocking collectives  45.3 us (72%)
  Pallas kernels  8.7 us (14%)
  starting transfers between devices  5.22 us (8%)
  waiting for transfers between devices  2.44 us (4%)
  between operations  0.75 us (1%)
    all_to_all x1, blocking collectives, shards(): lax.all_to_all(sent.reshape(rows // 2, 2, 128), 'chan', 0, 0, tiled=True,...  29.9 us
    all_to_all x1, blocking collectives, shards(): lax.all_to_all(total.reshape(BLOCKS, 4, 128), 'chan', 0, 0, axis_index_gr...  15.3 us
    ppermute x3, starting transfers between devices, shards(): lax.ppermute(spectra[k], 'x', [(x, (x + k) % 4) for x in range(4)])  5.13 us
    pallas_call x2, Pallas kernels, cross(): pl.pallas_call(kernel, out_shape=shapes, in_specs=[vmem] * len(arrays), o...  2.59 us
    pallas_call x1, Pallas kernels, transform(): pl.pallas_call(transform_kernel, out_shape=jax.ShapeDtypeStruct((BLOCKS *...  2.55 us
    ppermute x3, waiting for transfers between devices, shards(): lax.ppermute(spectra[k], 'x', [(x, (x + k) % 4) for x in range(4)])  2.12 us
    pallas_call x1, Pallas kernels, tables(): pl.pallas_call(tables_kernel, out_shape=(jax.ShapeDtypeStruct((2, QUARTER...  1.34 us
  transfers between devices with their start and end apart: 4, of which 2 were waited for; matrix products, arithmetic and copies ran while one was open for 0% of the time, Pallas kernels for 3%

profile of v9, /device:TPU:8, one launch (start us, length us, event | category | flops | bytes accessed | tf_op | source)
XLA Modules:
  0.0 62.4 jit_solution(1237284120919645431)
XLA Ops:
  0.0 0.0 copy-start
  0.0 0.0 copy-start.1
  0.0 0.0 copy-start.2
  0.0 1.3 %tables.1 = (bf16[2,768,768]{2,1,0:T(8,128)(2,1)S(1)}, f32[4,16,768]{2,1,0:T(8,128)S(1)}, f32[2,48,768]{2,1,0:T(8,128)S(1)}) custom-call(), custom_call_target="tpu_custom_call" | custom-call | flops 1000000000 | bytes 10000000 | tf_op jit(solution)/shard_map/tables/pallas_call | solution.py:72
  1.4 0.0 copy-done
  1.4 0.0 copy-done.1
  1.4 0.0 copy-done.2
  1.4 2.6 %transform.1 = bf16[3136,128]{1,0:T(8,128)(2,1)S(1)} custom-call(bf16[128,3072]{1,0:T(8,128)(2,1)S(1)} %bitcast.11, s32[1,32]{1,0:T(1,128)S(1)} %copy-done.1, s32[1,32]{1,0:T(1,128)S(1)} %copy-done.2, bf16[2,768,768]{2,1,0:T(8,128)(2,1)S(1)} %get-tuple-element.13.even_table_ref, f32[4,16,768]{2,1,0:T(8,128)S(1)} %get-tuple-element.14.base_ref, ...), custom_call_target="tpu_custom_call" | custom-call | flops 1207959552 | bytes 2000000 | tf_op jit(solution)/shard_map/transform/pallas_call | solution.py:198
  3.9 29.9 %all_to_all.10 = bf16[1568,2,128]{2,1,0:T(2,128)(2,1)S(1)} all-to-all(bf16[1568,2,128]{2,1,0:T(2,128)(2,1)S(1)} %bitcast.8), channel_id=1, replica_groups={{248,240,232,224,216,208,200,192,184,176,168,160,152,144,136,128,120,11..., dimensions={0} | all-to-all | bytes 1605632 | tf_op jit(solution)/shard_map/all_to_all | solution.py:459
  33.9 1.5 %cross.2 = (f32[384,128]{1,0:T(8,128)S(1)}, bf16[512,768]{1,0:T(8,128)(2,1)S(1)}, f32[2,128,128]{2,1,0:T(8,128)S(1)}) custom-call(bf16[3136,128]{1,0:T(8,128)(2,1)S(1)} %bitcast.7), custom_call_target="tpu_custom_call" | custom-call | flops 603979776 | bytes 2000000 | tf_op jit(solution)/shard_map/cross/pallas_call | solution.py:298
  35.4 0.1 collective-permute-start
  35.5 1.1 %cross.3 = f32[384,128]{1,0:T(8,128)S(1)} custom-call(bf16[512,768]{1,0:T(8,128)(2,1)S(1)} %get-tuple-element.16.data_ref, f32[2,128,128]{2,1,0:T(8,128)S(1)} %get-tuple-element.17.list_ref), custom_call_target="tpu_custom_call" | custom-call | flops 603979776 | bytes 2000000 | tf_op jit(solution)/shard_map/cross/pallas_call | solution.py:298
  36.6 0.3 collective-permute-done
  37.0 1.6 %collective-permute-start.1 = (f32[96,128]{1,0:T(8,128)S(1)}, f32[96,128]{1,0:T(8,128)S(1)}, u32[]{:S(2)}, u32[]{:S(2)}) collective-permute-start(f32[96,128]{1,0:T(8,128)S(1)} %get-tuple-element.23), channel_id=1, source_target_pairs={{0,2},{2,4},{4,6},{6,0},{1,3},{3,5},{5,7},{7,1},{8,10},{10,12},{12... | collective-permute-start | bytes 147464 | tf_op jit(solution)/shard_map/ppermute | solution.py:464
  38.5 1.8 %collective-permute-start.2 = (f32[96,128]{1,0:T(8,128)S(1)}, f32[96,128]{1,0:T(8,128)S(1)}, u32[]{:S(2)}, u32[]{:S(2)}) collective-permute-start(f32[96,128]{1,0:T(8,128)S(1)} %get-tuple-element.22), channel_id=1, source_target_pairs={{0,6},{2,0},{4,2},{6,4},{1,7},{3,1},{5,3},{7,5},{8,14},{10,8},{12,... | collective-permute-start | bytes 147464 | tf_op jit(solution)/shard_map/ppermute | solution.py:464
  40.3 1.8 %collective-permute-start.3 = (f32[96,128]{1,0:T(8,128)S(1)}, f32[96,128]{1,0:T(8,128)S(1)}, u32[]{:S(2)}, u32[]{:S(2)}) collective-permute-start(f32[96,128]{1,0:T(8,128)S(1)} %get-tuple-element.21), channel_id=1, source_target_pairs={{0,4},{2,6},{4,0},{6,2},{1,5},{3,7},{5,1},{7,3},{8,12},{10,14},{12... | collective-permute-start | bytes 147464 | tf_op jit(solution)/shard_map/ppermute | solution.py:464
  42.7 1.0 %inverse.1 = (f32[2,1024,128]{2,1,0:T(8,128)S(1)}, bf16[4096,256]{1,0:T(8,128)(2,1)S(1)}) custom-call(s32[1]{0:T(128)S(6)} %copy.5.count_ref, f32[4,96,128]{2,1,0:T(8,128)S(1)} %bitcast.6), custom_call_target="tpu_custom_call" | custom-call | flops 10000000 | bytes 3000000 | tf_op jit(solution)/shard_map/inverse/pallas_call | solution.py:385
  43.7 0.0 collective-permute-done.1.one_ref
  43.7 0.0 collective-permute-done.2.two_ref
  43.8 2.1 %collective-permute-done.3.three_ref = f32[96,128]{1,0:T(8,128)S(1)} collective-permute-done((f32[96,128]{1,0:T(8,128)S(1)}, f32[96,128]{1,0:T(8,128)S(1)}, u32[]{:S(2)}, u32[]{:S(2)}) %collective-permute-start.3) | collective-permute-done | bytes 49184 | tf_op jit(solution)/shard_map/ppermute | solution.py:464
  45.9 0.1 total.1
  46.0 15.3 %all_to_all.11 = f32[32,4,128]{2,1,0:T(4,128)S(1)} all-to-all(f32[32,4,128]{2,1,0:T(4,128)S(1)} %bitcast.9), channel_id=1, replica_groups={{248,240,232,224,216,208,200,192,184,176,168,160,152,144,136,128,120,11..., dimensions={0} | all-to-all | bytes 131072 | tf_op jit(solution)/shard_map/all_to_all | solution.py:467
  61.3 1.2 %lags.1 = f32[4,1024]{1,0:T(4,128)} custom-call(f32[128,128]{1,0:T(8,128)S(1)} %bitcast.10, f32[2,1024,128]{2,1,0:T(8,128)S(1)} %get-tuple-element.19.after_ref.turn_ref, bf16[4096,256]{1,0:T(8,128)(2,1)S(1)} %get-tuple-element.20.table_ref), custom_call_target="tpu_custom_call" | custom-call | flops 134217728 | bytes 4000000 | tf_op jit(solution)/shard_map/lags/pallas_call | solution.py:444
  (2 shorter events, 0.0 us)
Async XLA Ops:
  0.0 1.4 %copy-start = (bf16[16,8,3072]{2,1,0:T(8,128)(2,1)S(1)}, bf16[16,8,3072]{2,1,0:T(8,128)(2,1)}, u32[]{:S(2)}) copy-start(bf16[16,8,3072]{2,1,0:T(8,128)(2,1)} %param.4) | copy-start | bytes 2359300
  0.0 1.4 %copy-start.1 = (s32[1,32]{1,0:T(1,128)S(1)}, s32[1,32]{1,0:T(1,128)}, u32[]{:S(2)}) copy-start(s32[1,32]{1,0:T(1,128)} %source_ref.1) | copy-start | bytes 388
  0.0 1.4 %copy-start.2 = (s32[1,32]{1,0:T(1,128)S(1)}, s32[1,32]{1,0:T(1,128)}, u32[]{:S(2)}) copy-start(s32[1,32]{1,0:T(1,128)} %partner_ref.1) | copy-start | bytes 388
  35.4 1.5 %collective-permute-start = (f32[384,128]{1,0:T(8,128)S(1)}, f32[384,128]{1,0:T(8,128)S(1)}, u32[]{:S(2)}, u32[]{:S(2)}) collective-permute-start(f32[384,128]{1,0:T(8,128)S(1)} %get-tuple-element.18), channel_id=1, source_target_pairs={{0,1},{1,0},{2,3},{3,2},{4,5},{5,4},{6,7},{7,6},{8,9},{9,8},{10,11... | collective-permute-start | bytes 589832 | tf_op jit(solution)/shard_map/ppermute | solution.py:462
  37.0 6.8 %collective-permute-start.1 = (f32[96,128]{1,0:T(8,128)S(1)}, f32[96,128]{1,0:T(8,128)S(1)}, u32[]{:S(2)}, u32[]{:S(2)}) collective-permute-start(f32[96,128]{1,0:T(8,128)S(1)} %get-tuple-element.23), channel_id=1, source_target_pairs={{0,2},{2,4},{4,6},{6,0},{1,3},{3,5},{5,7},{7,1},{8,10},{10,12},{12... | collective-permute-start | bytes 147464 | tf_op jit(solution)/shard_map/ppermute | solution.py:464
  38.5 5.2 %collective-permute-start.2 = (f32[96,128]{1,0:T(8,128)S(1)}, f32[96,128]{1,0:T(8,128)S(1)}, u32[]{:S(2)}, u32[]{:S(2)}) collective-permute-start(f32[96,128]{1,0:T(8,128)S(1)} %get-tuple-element.22), channel_id=1, source_target_pairs={{0,6},{2,0},{4,2},{6,4},{1,7},{3,1},{5,3},{7,5},{8,14},{10,8},{12,... | collective-permute-start | bytes 147464 | tf_op jit(solution)/shard_map/ppermute | solution.py:464
  40.3 5.6 %collective-permute-start.3 = (f32[96,128]{1,0:T(8,128)S(1)}, f32[96,128]{1,0:T(8,128)S(1)}, u32[]{:S(2)}, u32[]{:S(2)}) collective-permute-start(f32[96,128]{1,0:T(8,128)S(1)} %get-tuple-element.21), channel_id=1, source_target_pairs={{0,4},{2,6},{4,0},{6,2},{1,5},{3,7},{5,1},{7,3},{8,12},{10,14},{12... | collective-permute-start | bytes 147464 | tf_op jit(solution)/shard_map/ppermute | solution.py:464
